TPU v7x, 128 devices: a whole 4x4x4 slice. The times are simulated.
128 devices in a mesh: row: 8 (over y_hi, z), col: 16 (over x, y_lo, core).
Axes of the slice: x: 4, y: 4 (y_hi: 2, y_lo: 2; y = y_hi * 2 + y_lo), z: 4, core: 2. Of those that a mesh axis runs over, the one named last changes fastest.
Arguments:
- strain: bfloat16 [2048, 33280], P(('row', 'col')), may hold values from -6 to 6
- file_channels: int32 [2048], P(('row', 'col')), may hold values from 0 to 511, as said below
- file_counts: int32 [128], P(('row', 'col')), may hold values from 0 to 16, as said below
- window_start: int32 [128], P(('row', 'col')), may hold values from 0 to 512
Outputs:
- correlations: bfloat16 [512, 512, 1024], P('row', 'col')
Inputs may be any that keep to these rules, and one draw needn't show every extreme that they name: `file_channels`: the first file_counts[d] slots of file d are live. The live slots of the 8 files with one col index hold, each exactly once, the channels g whose owner ((g // 4) // 16, (g // 4) % 16) has that col index; dead slots hold arbitrary channel numbers. One file holds at most 2 channels of one owner, and exactly 2 for some file and owner in every group of files with one col index. `file_counts`: in every group of files with one col index some file has all 16 slots live.
All inputs are finite; a program needn't handle non-finite values.
Results may differ from a plain program's by a relative error of at most 0.0076.
Values may be sent and summed in bfloat16 or wider, within the bound.
No kernel may reach another device: no remote copies, remote signals or barrier semaphores. Data moves between devices by JAX's collectives and lax.ppermute only.
A program may use at most 128 MiB of HBM per device.

v0:
```python
import math

import jax
import jax.numpy as jnp
from jax import lax
from jax.sharding import PartitionSpec as P

NF = 2048
NT = 4096
LAGS = 1024
SEGS = 8
CH_DEV = 4
SMOOTH = 32
EDGE = 128


def dft_block(first_freq, freq_count, length):
    sample_index = jnp.arange(length, dtype=jnp.int32)[:, None]
    freq_index = first_freq + jnp.arange(freq_count, dtype=jnp.int32)[None, :]
    phases = jnp.mod(sample_index * freq_index, length).astype(jnp.float32) * (
        2.0 * math.pi / length
    )
    return jnp.concatenate([jnp.cos(phases), -jnp.sin(phases)], axis=1).astype(jnp.bfloat16)


def lag_table():
    freq_index = jnp.arange(NF, dtype=jnp.int32)[:, None]
    lag_index = jnp.arange(LAGS, dtype=jnp.int32)[None, :] - LAGS // 2
    phases = jnp.mod(freq_index * lag_index, NT).astype(jnp.float32) * (2.0 * math.pi / NT)
    return jnp.concatenate([jnp.cos(phases), -jnp.sin(phases)], axis=0).astype(jnp.bfloat16)


def band_taper(freq_count):
    freq_index = jnp.arange(freq_count, dtype=jnp.float32)
    distance = jnp.minimum(freq_index + 0.5, freq_count - freq_index - 0.5)
    rising = jnp.minimum(distance / EDGE, 1.0)
    return jnp.sin(0.5 * math.pi * rising) ** 2


def whiten(real_part, imag_part):
    powers = real_part * real_part + imag_part * imag_part
    padded = jnp.pad(powers, ((0, 0), (SMOOTH + 1, SMOOTH)))
    running = jnp.cumsum(padded, axis=1)
    window_sum = running[:, 2 * SMOOTH + 1 :] - running[:, : powers.shape[1]]
    scaling = band_taper(powers.shape[1])[None, :] / jnp.sqrt(window_sum / (2 * SMOOTH + 1) + 1e-06)
    return (real_part * scaling, imag_part * scaling)


def spectra_of(traces):
    channels = traces.shape[0]
    segment_rows = traces.reshape(channels * SEGS, NT)
    block_width = min(256, NF)
    block_count = NF // block_width

    def spectra_one_block(block_index):
        table = dft_block(block_index * block_width, block_width, NT)
        return jnp.dot(segment_rows, table, preferred_element_type=jnp.float32)

    pieces = lax.map(spectra_one_block, jnp.arange(block_count, dtype=jnp.int32))
    pieces = pieces.reshape(block_count, channels * SEGS, 2, block_width)
    real_part = jnp.transpose(pieces[:, :, 0], (1, 0, 2)).reshape(channels * SEGS, NF)
    imag_part = jnp.transpose(pieces[:, :, 1], (1, 0, 2)).reshape(channels * SEGS, NF)
    real_part, imag_part = whiten(real_part, imag_part)
    stacked = jnp.stack(
        [real_part.reshape(channels, SEGS, NF), imag_part.reshape(channels, SEGS, NF)], axis=1
    )
    return stacked.astype(jnp.bfloat16)


def correlate(row_spectra, row_ids, col_spectra, col_ids, inverse):
    flipped = jnp.concatenate([-col_spectra[:, 1:2], col_spectra[:, 0:1]], axis=1)
    row_total = row_spectra.shape[0]
    col_total = col_spectra.shape[0]
    block_cols = 8
    norm_scale = 1.0 / math.sqrt(SEGS * NF)

    def correlate_one_block(block_index):
        first_col = block_index * block_cols
        own_cols = lax.dynamic_slice_in_dim(col_spectra, first_col, block_cols, 0)
        turned = lax.dynamic_slice_in_dim(flipped, first_col, block_cols, 0)
        real_cross = jnp.einsum(
            "icsf,jcsf->ijf", row_spectra, own_cols, preferred_element_type=jnp.float32
        )
        imag_cross = jnp.einsum(
            "icsf,jcsf->ijf", row_spectra, turned, preferred_element_type=jnp.float32
        )
        cross = jnp.concatenate([real_cross, imag_cross], axis=2).astype(jnp.bfloat16)
        lagged = jnp.dot(
            cross.reshape(row_total * block_cols, 2 * NF),
            inverse,
            preferred_element_type=jnp.float32,
        )
        block_ids = lax.dynamic_slice_in_dim(col_ids, first_col, block_cols, 0)
        keep_pair = (row_ids[:, None] != block_ids[None, :]).astype(jnp.float32)
        lagged = lagged.reshape(row_total, block_cols, LAGS)
        return (lagged * (keep_pair[:, :, None] * norm_scale)).astype(jnp.bfloat16)

    results = lax.map(correlate_one_block, jnp.arange(col_total // block_cols, dtype=jnp.int32))
    return jnp.transpose(results, (1, 0, 2, 3)).reshape(row_total, col_total, LAGS)


def local(strain, file_channels, file_counts, window_start):
    col_count = lax.axis_size("col")
    my_row = lax.axis_index("row")
    my_col = lax.axis_index("col")
    slot_total = strain.shape[0]
    window = lax.dynamic_slice_in_dim(strain, window_start[0], SEGS * NT, 1)
    slot_index = jnp.arange(slot_total, dtype=jnp.int32)
    live_slot = slot_index < file_counts[0]
    owner_row = file_channels // CH_DEV // col_count
    local_slot = file_channels % CH_DEV
    labels = jnp.where(live_slot, owner_row * CH_DEV + local_slot, -1).astype(jnp.bfloat16)
    arrived, arrived_labels = (
        lax.all_gather(window, "row", axis=0, tiled=True),
        lax.all_gather(labels, "row", axis=0, tiled=True),
    )
    wanted = (my_row * CH_DEV + jnp.arange(CH_DEV, dtype=jnp.int32)).astype(jnp.float32)
    picking = (arrived_labels.astype(jnp.float32)[None, :] == wanted[:, None]).astype(jnp.bfloat16)
    traces = jnp.dot(picking, arrived, preferred_element_type=jnp.float32).astype(jnp.bfloat16)
    own_spectra = spectra_of(traces)
    col_spectra = lax.all_gather(own_spectra, "row", axis=0, tiled=True)
    col_local = jnp.arange(col_spectra.shape[0], dtype=jnp.int32)
    col_ids = (col_local // CH_DEV * col_count + my_col) * CH_DEV + col_local % CH_DEV
    row_base = my_row * col_count * CH_DEV
    inverse = lag_table()
    row_spectra = lax.all_gather(own_spectra, "col", axis=0, tiled=True)
    row_ids = row_base + jnp.arange(row_spectra.shape[0], dtype=jnp.int32)
    return correlate(row_spectra, row_ids, col_spectra, col_ids, inverse)


def solution(mesh):
    placed = (P(("row", "col"), None), P(("row", "col")), P(("row", "col")), P(("row", "col")))
    return jax.shard_map(
        local, mesh=mesh, in_specs=placed, out_specs=P("row", "col", None), check_vma=False
    )
```

profile of v0, /device:TPU:1, one launch (start us, length us, event | category | flops | bytes accessed | tf_op | source)
XLA Modules:
  0.0 758.2 jit_solution(4038430030077687703)
XLA Ops:
  7.8 1.3 constant_dynamic-slice_fusion.2
  9.8 1.3 dynamic-slice
  12.7 23.0 %all-reduce.2 = bf16[128]{0:T(256)(128)(2,1)S(1)} all-reduce(bf16[128]{0:T(256)(128)(2,1)S(1)} %dynamic-update-slice), channel_id=1, replica_groups=mesh['row'=8,'col'=16] {'row'}, use_global_device_ids=true, to_apply=%add.2 | all-reduce | flops 128 | bytes 512
  35.8 84.3 %all-gather.4.cloned.1.call-done = bf16[128,32768]{1,0:T(8,128)(2,1)} async-done(((bf16[16,32768]{1,0:T(8,128)(2,1)}), bf16[128,32768]{1,0:T(8,128)(2,1)}) %all-gather.4.cloned.1.call-update) | async-done | bytes 8388624 | tf_op jit(solution)/shard_map/all_gather | solution.py:114
  120.0 4.6 convolution_convert_fusion
  124.9 152.4 %while.23 = (s32[]{:T(128)}, f32[8,32,512]{2,1,0:T(8,128)S(1)}, s32[8]{0:T(128)S(1)}, bf16[32,4096]{1,0:T(8,128)(2,1)S(1)}, s32[]{:T(128)}, /*index=5*/s32[1]{0:T(128)}) while((s32[]{:T(128)}, f32[8,32,512]{2,1,0:T(8,128)S(1)}, s32[8]{0:T(128)S(1)}, bf16[32,4096]{1,0:T(8,128)(2,1)S(1)}, s32[]{:T(128)}, /*index=5*/s32[1]{0:T(128)}) %tuple.53), condition=%wide.region_1.2_spmd, body=%wide.region_0.1_spmd.sunk | while | flops 160432384 | bytes 8718437 | solution.py:59
  126.1 17.0 %cosine_convert_fusion.3 = (bf16[4096,256]{1,0:T(8,128)(2,1)S(1)}, bf16[4096,256]{1,0:T(8,128)(2,1)S(1)}) fusion(s32[256]{0:T(256)S(1)} %iota_add_fusion.6), kind=kLoop, calls=%fused_computation.12.clone.1 | loop fusion | flops 17825792 | bytes 4195328 | tf_op jit(solution)/shard_map/convert.4
  143.1 0.8 fusion.81
  145.2 17.0 %cosine_convert_fusion.3 = (bf16[4096,256]{1,0:T(8,128)(2,1)S(1)}, bf16[4096,256]{1,0:T(8,128)(2,1)S(1)}) fusion(s32[256]{0:T(256)S(1)} %iota_add_fusion.6), kind=kLoop, calls=%fused_computation.12.clone.1 | loop fusion | flops 17825792 | bytes 4195328 | tf_op jit(solution)/shard_map/convert.4
  162.2 0.8 fusion.81
  164.2 17.0 %cosine_convert_fusion.3 = (bf16[4096,256]{1,0:T(8,128)(2,1)S(1)}, bf16[4096,256]{1,0:T(8,128)(2,1)S(1)}) fusion(s32[256]{0:T(256)S(1)} %iota_add_fusion.6), kind=kLoop, calls=%fused_computation.12.clone.1 | loop fusion | flops 17825792 | bytes 4195328 | tf_op jit(solution)/shard_map/convert.4
  181.2 0.8 fusion.81
  183.3 17.0 %cosine_convert_fusion.3 = (bf16[4096,256]{1,0:T(8,128)(2,1)S(1)}, bf16[4096,256]{1,0:T(8,128)(2,1)S(1)}) fusion(s32[256]{0:T(256)S(1)} %iota_add_fusion.6), kind=kLoop, calls=%fused_computation.12.clone.1 | loop fusion | flops 17825792 | bytes 4195328 | tf_op jit(solution)/shard_map/convert.4
  200.3 0.8 fusion.81
  202.4 17.0 %cosine_convert_fusion.3 = (bf16[4096,256]{1,0:T(8,128)(2,1)S(1)}, bf16[4096,256]{1,0:T(8,128)(2,1)S(1)}) fusion(s32[256]{0:T(256)S(1)} %iota_add_fusion.6), kind=kLoop, calls=%fused_computation.12.clone.1 | loop fusion | flops 17825792 | bytes 4195328 | tf_op jit(solution)/shard_map/convert.4
  219.3 0.8 fusion.81
  221.4 17.0 %cosine_convert_fusion.3 = (bf16[4096,256]{1,0:T(8,128)(2,1)S(1)}, bf16[4096,256]{1,0:T(8,128)(2,1)S(1)}) fusion(s32[256]{0:T(256)S(1)} %iota_add_fusion.6), kind=kLoop, calls=%fused_computation.12.clone.1 | loop fusion | flops 17825792 | bytes 4195328 | tf_op jit(solution)/shard_map/convert.4
  238.4 0.8 fusion.81
  240.5 17.0 %cosine_convert_fusion.3 = (bf16[4096,256]{1,0:T(8,128)(2,1)S(1)}, bf16[4096,256]{1,0:T(8,128)(2,1)S(1)}) fusion(s32[256]{0:T(256)S(1)} %iota_add_fusion.6), kind=kLoop, calls=%fused_computation.12.clone.1 | loop fusion | flops 17825792 | bytes 4195328 | tf_op jit(solution)/shard_map/convert.4
  257.4 0.8 fusion.81
  259.5 17.0 %cosine_convert_fusion.3 = (bf16[4096,256]{1,0:T(8,128)(2,1)S(1)}, bf16[4096,256]{1,0:T(8,128)(2,1)S(1)}) fusion(s32[256]{0:T(256)S(1)} %iota_add_fusion.6), kind=kLoop, calls=%fused_computation.12.clone.1 | loop fusion | flops 17825792 | bytes 4195328 | tf_op jit(solution)/shard_map/convert.4
  276.5 0.8 fusion.81
  278.9 9.2 %reduce-window.6 = f32[32,17,128]{2,1,0:T(8,128)S(1)} reduce-window(f32[32,17,128]{2,1,0:T(8,128)S(1)} %reshape.99, f32[]{:T(128)} %constant.160.clone.1), window={size=1x1x128 pad=0_0x0_0x127_0}, to_apply=%region_2.3 | reduce-window | flops 8843264 | bytes 557060 | tf_op jit(solution)/shard_map/reduce-window
  289.1 0.8 pad_maximum_fusion.3
  290.7 35.0 %cosine_convert_fusion.1 = (bf16[2048,1024]{1,0:T(8,128)(2,1)}, bf16[2048,1024]{1,0:T(8,128)(2,1)}) fusion(s32[1024]{0:T(1024)S(1)} %iota_add_fusion.3), kind=kLoop, calls=%fused_computation.43 | loop fusion | flops 35651584 | bytes 8392704 | tf_op jit(solution)/shard_map/convert.6
  325.7 7.7 %pad_maximum_fusion.1 = bf16[4096,1024]{1,0:T(8,128)(2,1)} fusion(bf16[2048,1024]{1,0:T(8,128)(2,1)} %get-tuple-element.175, bf16[2048,1024]{1,0:T(8,128)(2,1)} %get-tuple-element.174), kind=kLoop, calls=%fused_computation.41 | loop fusion | flops 16777216 | bytes 16777216 | tf_op jit(solution)/shard_map/concatenate | solution.py:30
  333.4 8.6 %all-gather.6.cloned.1.call-done = bf16[32,2,8,2048]{3,2,1,0:T(8,128)(2,1)} async-done(((bf16[4,2,8,2048]{3,2,1,0:T(8,128)(2,1)}), bf16[32,2,8,2048]{3,2,1,0:T(8,128)(2,1)}) %all-gather.6.cloned.1.call-update) | async-done | bytes 2097168 | tf_op jit(solution)/shard_map/all_gather | solution.py:121
  341.9 1.7 slice_negate_fusion
  343.8 35.7 %all-gather.8.cloned.1.call-done = bf16[64,2,8,2048]{3,2,1,0:T(8,128)(2,1)} async-done(((bf16[4,2,8,2048]{3,2,1,0:T(8,128)(2,1)}), bf16[64,2,8,2048]{3,2,1,0:T(8,128)(2,1)}) %all-gather.8.cloned.1.call-update) | async-done | bytes 4194320 | tf_op jit(solution)/shard_map/all_gather | solution.py:126
  379.5 14.3 %copy.23 = bf16[64,2,8,2048]{0,2,1,3:T(8,128)(2,1)} copy(bf16[64,2,8,2048]{3,2,1,0:T(8,128)(2,1)} %all-gather.8.cloned.1.call-done) | data formatting | bytes 8388608
  393.9 352.8 %while.24 = (s32[]{:T(128)}, bf16[4,64,8,1024]{3,2,1,0:T(8,128)(2,1)}, s32[4]{0:T(128)S(1)}, bf16[32,2,8,2048]{3,2,1,0:T(8,128)(2,1)}, bf16[64,2,8,2048]{0,2,1,3...) while((s32[]{:T(128)}, ...), condition=%wide.region_5.6_spmd.clone, body=%wide.region_4.5_spmd.clone.sunk | while | flops 4367320064 | bytes 56628544 | solution.py:98
  395.1 1.1 constant_dynamic-slice_fusion.4
  396.3 8.5 %copy.42 = bf16[8,2,8,2048]{2,0,1,3:T(8,128)(2,1)} copy(bf16[8,2,8,2048]{3,2,1,0:T(8,128)(2,1)S(1)} %get-tuple-element.262) | data formatting | bytes 1048576 | tf_op jit(solution)/shard_map/while/body/eval_jaxpr/dynamic_slice | solution.py:80
  404.7 8.6 %fusion.88 = bf16[64,8,2048]{0,1,2:T(8,128)(2,1)} fusion(bf16[8,2,8,2048]{2,0,1,3:T(8,128)(2,1)} %copy.42, bf16[64,2,8,2048]{0,2,1,3:T(8,128)(2,1)} %get-tuple-element.312), kind=kOutput, calls=%fused_computation.26.clone.1 | convolution fusion | flops 34603008 | bytes 6815744 | tf_op jit(solution)/shard_map/while/body/eval_jaxpr/icsf,jcsf->ijf/dot_general | solution.py:84
  413.3 8.5 %copy.43 = bf16[8,2,8,2048]{2,0,1,3:T(8,128)(2,1)} copy(bf16[8,2,8,2048]{3,2,1,0:T(8,128)(2,1)S(1)} %get-tuple-element.263) | data formatting | bytes 1048576 | tf_op jit(solution)/shard_map/while/body/eval_jaxpr/dynamic_slice | solution.py:79
  421.8 7.4 fusion.89
  429.3 30.5 %pad_maximum_fusion.5 = bf16[64,8,4096]{0,1,2:T(8,128)(2,1)} fusion(bf16[64,8,2048]{0,1,2:T(8,128)(2,1)S(1)} %copy-done.2, bf16[64,8,2048]{0,1,2:T(8,128)(2,1)S(1)} %fusion.89), kind=kLoop, calls=%fused_computation.20.clone.1 | loop fusion | flops 2097152 | bytes 8388608 | tf_op jit(solution)/shard_map/while/body/eval_jaxpr/concatenate | solution.py:87
  459.8 12.0 %copy.44 = bf16[64,8,4096]{2,1,0:T(8,128)(2,1)} copy(bf16[64,8,4096]{0,1,2:T(8,128)(2,1)} %pad_maximum_fusion.5) | data formatting | bytes 8388608 | tf_op jit(solution)/shard_map/while/body/eval_jaxpr/concatenate | solution.py:87
  471.9 10.2 %fusion.90 = bf16[4,64,8,1024]{3,2,1,0:T(8,128)(2,1)} fusion(bf16[4,64,8,1024]{3,2,1,0:T(8,128)(2,1)} %get-tuple-element.296, s32[]{:T(128)} %get-tuple-element.295, bf16[64,8,4096]{2,1,0:T(8,128)(2,1)} %copy.44, bf16[4096,1024]{1,0:T(8,128)(2,1)} %get-tuple-element.314, f32[64,8]{1,0:T(8,128)S(1)} %compare_select_fusion.9), kind=kOutput, calls=%fused_computation.29.clone.1 | convolution fusion | flops 4296015872 | bytes 13634048 | tf_op jit(solution)/shard_map/while/body/eval_jaxpr/dot_general | solution.py:88
  483.4 1.1 constant_dynamic-slice_fusion.4
  484.5 8.5 %copy.42 = bf16[8,2,8,2048]{2,0,1,3:T(8,128)(2,1)} copy(bf16[8,2,8,2048]{3,2,1,0:T(8,128)(2,1)S(1)} %get-tuple-element.262) | data formatting | bytes 1048576 | tf_op jit(solution)/shard_map/while/body/eval_jaxpr/dynamic_slice | solution.py:80
  493.0 8.6 %fusion.88 = bf16[64,8,2048]{0,1,2:T(8,128)(2,1)} fusion(bf16[8,2,8,2048]{2,0,1,3:T(8,128)(2,1)} %copy.42, bf16[64,2,8,2048]{0,2,1,3:T(8,128)(2,1)} %get-tuple-element.312), kind=kOutput, calls=%fused_computation.26.clone.1 | convolution fusion | flops 34603008 | bytes 6815744 | tf_op jit(solution)/shard_map/while/body/eval_jaxpr/icsf,jcsf->ijf/dot_general | solution.py:84
  501.6 8.5 %copy.43 = bf16[8,2,8,2048]{2,0,1,3:T(8,128)(2,1)} copy(bf16[8,2,8,2048]{3,2,1,0:T(8,128)(2,1)S(1)} %get-tuple-element.263) | data formatting | bytes 1048576 | tf_op jit(solution)/shard_map/while/body/eval_jaxpr/dynamic_slice | solution.py:79
  510.1 7.4 fusion.89
  517.5 30.5 %pad_maximum_fusion.5 = bf16[64,8,4096]{0,1,2:T(8,128)(2,1)} fusion(bf16[64,8,2048]{0,1,2:T(8,128)(2,1)S(1)} %copy-done.2, bf16[64,8,2048]{0,1,2:T(8,128)(2,1)S(1)} %fusion.89), kind=kLoop, calls=%fused_computation.20.clone.1 | loop fusion | flops 2097152 | bytes 8388608 | tf_op jit(solution)/shard_map/while/body/eval_jaxpr/concatenate | solution.py:87
  548.1 12.0 %copy.44 = bf16[64,8,4096]{2,1,0:T(8,128)(2,1)} copy(bf16[64,8,4096]{0,1,2:T(8,128)(2,1)} %pad_maximum_fusion.5) | data formatting | bytes 8388608 | tf_op jit(solution)/shard_map/while/body/eval_jaxpr/concatenate | solution.py:87
  560.2 10.1 %fusion.90 = bf16[4,64,8,1024]{3,2,1,0:T(8,128)(2,1)} fusion(bf16[4,64,8,1024]{3,2,1,0:T(8,128)(2,1)} %get-tuple-element.296, s32[]{:T(128)} %get-tuple-element.295, bf16[64,8,4096]{2,1,0:T(8,128)(2,1)} %copy.44, bf16[4096,1024]{1,0:T(8,128)(2,1)} %get-tuple-element.314, f32[64,8]{1,0:T(8,128)S(1)} %compare_select_fusion.9), kind=kOutput, calls=%fused_computation.29.clone.1 | convolution fusion | flops 4296015872 | bytes 13634048 | tf_op jit(solution)/shard_map/while/body/eval_jaxpr/dot_general | solution.py:88
  571.6 1.1 constant_dynamic-slice_fusion.4
  572.7 8.5 %copy.42 = bf16[8,2,8,2048]{2,0,1,3:T(8,128)(2,1)} copy(bf16[8,2,8,2048]{3,2,1,0:T(8,128)(2,1)S(1)} %get-tuple-element.262) | data formatting | bytes 1048576 | tf_op jit(solution)/shard_map/while/body/eval_jaxpr/dynamic_slice | solution.py:80
  581.2 8.6 %fusion.88 = bf16[64,8,2048]{0,1,2:T(8,128)(2,1)} fusion(bf16[8,2,8,2048]{2,0,1,3:T(8,128)(2,1)} %copy.42, bf16[64,2,8,2048]{0,2,1,3:T(8,128)(2,1)} %get-tuple-element.312), kind=kOutput, calls=%fused_computation.26.clone.1 | convolution fusion | flops 34603008 | bytes 6815744 | tf_op jit(solution)/shard_map/while/body/eval_jaxpr/icsf,jcsf->ijf/dot_general | solution.py:84
  589.8 8.5 %copy.43 = bf16[8,2,8,2048]{2,0,1,3:T(8,128)(2,1)} copy(bf16[8,2,8,2048]{3,2,1,0:T(8,128)(2,1)S(1)} %get-tuple-element.263) | data formatting | bytes 1048576 | tf_op jit(solution)/shard_map/while/body/eval_jaxpr/dynamic_slice | solution.py:79
  598.3 7.4 fusion.89
  605.7 30.5 %pad_maximum_fusion.5 = bf16[64,8,4096]{0,1,2:T(8,128)(2,1)} fusion(bf16[64,8,2048]{0,1,2:T(8,128)(2,1)S(1)} %copy-done.2, bf16[64,8,2048]{0,1,2:T(8,128)(2,1)S(1)} %fusion.89), kind=kLoop, calls=%fused_computation.20.clone.1 | loop fusion | flops 2097152 | bytes 8388608 | tf_op jit(solution)/shard_map/while/body/eval_jaxpr/concatenate | solution.py:87
  636.2 12.0 %copy.44 = bf16[64,8,4096]{2,1,0:T(8,128)(2,1)} copy(bf16[64,8,4096]{0,1,2:T(8,128)(2,1)} %pad_maximum_fusion.5) | data formatting | bytes 8388608 | tf_op jit(solution)/shard_map/while/body/eval_jaxpr/concatenate | solution.py:87
  648.4 10.1 %fusion.90 = bf16[4,64,8,1024]{3,2,1,0:T(8,128)(2,1)} fusion(bf16[4,64,8,1024]{3,2,1,0:T(8,128)(2,1)} %get-tuple-element.296, s32[]{:T(128)} %get-tuple-element.295, bf16[64,8,4096]{2,1,0:T(8,128)(2,1)} %copy.44, bf16[4096,1024]{1,0:T(8,128)(2,1)} %get-tuple-element.314, f32[64,8]{1,0:T(8,128)S(1)} %compare_select_fusion.9), kind=kOutput, calls=%fused_computation.29.clone.1 | convolution fusion | flops 4296015872 | bytes 13634048 | tf_op jit(solution)/shard_map/while/body/eval_jaxpr/dot_general | solution.py:88
  659.7 1.1 constant_dynamic-slice_fusion.4
  660.9 8.5 %copy.42 = bf16[8,2,8,2048]{2,0,1,3:T(8,128)(2,1)} copy(bf16[8,2,8,2048]{3,2,1,0:T(8,128)(2,1)S(1)} %get-tuple-element.262) | data formatting | bytes 1048576 | tf_op jit(solution)/shard_map/while/body/eval_jaxpr/dynamic_slice | solution.py:80
  669.4 8.6 %fusion.88 = bf16[64,8,2048]{0,1,2:T(8,128)(2,1)} fusion(bf16[8,2,8,2048]{2,0,1,3:T(8,128)(2,1)} %copy.42, bf16[64,2,8,2048]{0,2,1,3:T(8,128)(2,1)} %get-tuple-element.312), kind=kOutput, calls=%fused_computation.26.clone.1 | convolution fusion | flops 34603008 | bytes 6815744 | tf_op jit(solution)/shard_map/while/body/eval_jaxpr/icsf,jcsf->ijf/dot_general | solution.py:84
  678.0 8.5 %copy.43 = bf16[8,2,8,2048]{2,0,1,3:T(8,128)(2,1)} copy(bf16[8,2,8,2048]{3,2,1,0:T(8,128)(2,1)S(1)} %get-tuple-element.263) | data formatting | bytes 1048576 | tf_op jit(solution)/shard_map/while/body/eval_jaxpr/dynamic_slice | solution.py:79
  686.4 7.4 fusion.89
  693.9 30.5 %pad_maximum_fusion.5 = bf16[64,8,4096]{0,1,2:T(8,128)(2,1)} fusion(bf16[64,8,2048]{0,1,2:T(8,128)(2,1)S(1)} %copy-done.2, bf16[64,8,2048]{0,1,2:T(8,128)(2,1)S(1)} %fusion.89), kind=kLoop, calls=%fused_computation.20.clone.1 | loop fusion | flops 2097152 | bytes 8388608 | tf_op jit(solution)/shard_map/while/body/eval_jaxpr/concatenate | solution.py:87
  724.4 12.0 %copy.44 = bf16[64,8,4096]{2,1,0:T(8,128)(2,1)} copy(bf16[64,8,4096]{0,1,2:T(8,128)(2,1)} %pad_maximum_fusion.5) | data formatting | bytes 8388608 | tf_op jit(solution)/shard_map/while/body/eval_jaxpr/concatenate | solution.py:87
  736.6 10.2 %fusion.90 = bf16[4,64,8,1024]{3,2,1,0:T(8,128)(2,1)} fusion(bf16[4,64,8,1024]{3,2,1,0:T(8,128)(2,1)} %get-tuple-element.296, s32[]{:T(128)} %get-tuple-element.295, bf16[64,8,4096]{2,1,0:T(8,128)(2,1)} %copy.44, bf16[4096,1024]{1,0:T(8,128)(2,1)} %get-tuple-element.314, f32[64,8]{1,0:T(8,128)S(1)} %compare_select_fusion.9), kind=kOutput, calls=%fused_computation.29.clone.1 | convolution fusion | flops 4296015872 | bytes 13634048 | tf_op jit(solution)/shard_map/while/body/eval_jaxpr/dot_general | solution.py:88
  746.7 4.9 copy_bitcast_fusion
  (79 shorter events, 13.0 us)
Async XLA Ops:
  6.5 1.2 copy-start
  6.5 113.5 %all-gather.4.cloned.1.call-start = ((), (), s32[]{:S(2)}) async-start(), calls=%async_computation | async-start | bytes 9437184 | tf_op jit(solution)/shard_map/all_gather | solution.py:114
  9.1 332.8 %all-gather.6.cloned.1.call-start = ((), (), s32[]{:S(2)}) async-start(), calls=%async_computation.1 | async-start | bytes 2359296 | tf_op jit(solution)/shard_map/all_gather | solution.py:121
  289.9 89.6 %all-gather.8.cloned.1.call-start = ((), (), s32[]{:S(2)}) async-start(), calls=%async_computation.2 | async-start | bytes 4456448 | tf_op jit(solution)/shard_map/all_gather | solution.py:126
  421.8 7.4 copy-start.2
  510.1 7.4 copy-start.2
  598.3 7.4 copy-start.2
  686.4 7.4 copy-start.2
  746.7 4.9 copy-start.1
Sparse Core Ops, SparseCore 0:
  9.7 110.2 all-gather.3
  290.0 51.8 all-gather.5
  343.6 35.8 all-gather.7
where the time goes:
time: 760 us; the launch traced here: 758 us
  other arithmetic  314 us (41%)
  local copies, waits for them, and re-layouts  153 us (20%)
  waiting for transfers between devices  129 us (17%)
  matrix products  116 us (15%)
  blocking collectives  23 us (3%)
  between operations  15.3 us (2%)
  loops' own time  8.1 us (1%)
    another operation x12, other arithmetic  180 us
    concatenate x4, other arithmetic, correlate_one_block(): jnp.concatenate([real_cross, imag_cross], axis=2).astype(jnp.bfloat16)  122 us
    all_gather x1, waiting for transfers between devices, local(): lax.all_gather(window, 'row', axis=0, tiled=True)  84.3 us
    concatenate x4, local copies, waits for them, and re-layouts, correlate_one_block(): jnp.concatenate([real_cross, imag_cross], axis=2).astype(jnp.bfloat16)  47.9 us
    dot_general x4, matrix products, correlate_one_block(): jnp.dot(cross.reshape(row_total * block_cols, 2 * NF), inverse, preferred...  40.6 us
    dynamic_slice x8, local copies, waits for them, and re-layouts, correlate_one_block(): turned = lax.dynamic_slice_in_dim(flipped, first_col, block_cols, 0)  38.5 us
    all_gather x1, waiting for transfers between devices, local(): row_spectra = lax.all_gather(own_spectra, 'col', axis=0, tiled=True)  35.7 us
    dot_general x4, matrix products, correlate_one_block(): jnp.einsum('icsf,jcsf->ijf', row_spectra, turned, preferred_element_type=...  34.4 us
  transfers between devices with their start and end apart: 3, of which 3 were waited for; matrix products, arithmetic and copies ran while one was open for 6% of the time, Pallas kernels for 0%

commit v1 on v0

v1 whole, which is shorter than its diff:
```python
import functools
import math

import jax
import jax.numpy as jnp
import numpy as np
from jax import lax
from jax.experimental import pallas as pl
from jax.experimental.pallas import tpu as pltpu
from jax.sharding import PartitionSpec as P

NF = 2048
NT = 4096
LAGS = 1024
SEGS = 8
CH = 4
SLOTS = 16
SMOOTH = 32
EDGE = 128
WIN = SEGS * NT
HALF = NF // 2
GRP = 16
NGRP = HALF // GRP
BF = jnp.bfloat16
F32 = jnp.float32


def frequency_order():
    p = np.arange(HALF).reshape(NGRP, 1, GRP)
    mirror = np.where(p == 0, HALF, NF - p)
    return np.concatenate([p, mirror], axis=1).reshape(NF)


def trig(product, size):
    angle = (product % size).astype(np.float32) * np.float32(2.0 * math.pi / size)
    return np.cos(angle.astype(np.float64)), -np.sin(angle.astype(np.float64))


@functools.cache
def dft_table():
    order = frequency_order().astype(np.int64)
    cos, sin = trig(np.arange(NT, dtype=np.int64)[:, None] * order[None, :], NT)
    both = np.stack([cos.reshape(NT, 8, 256), sin.reshape(NT, 8, 256)], axis=2)
    return both.transpose(1, 0, 2, 3).reshape(8, NT, 512).astype(jnp.bfloat16)


@functools.cache
def smooth_table():
    order = frequency_order()
    near = np.abs(order[:, None] - order[None, :]) <= SMOOTH
    tiles = NF // 128
    out = np.zeros((tiles, 3, 128, 128), np.float32)
    for t in range(tiles):
        for k in range(3):
            s = (t + k - 1) % tiles
            out[t, k] = near[s * 128 : s * 128 + 128, t * 128 : t * 128 + 128]
    assert out.sum() == near.sum()
    return out.reshape(tiles, 384, 128).astype(jnp.bfloat16)


@functools.cache
def taper_row():
    f = frequency_order().astype(np.float64)
    rising = np.minimum(np.minimum(f + 0.5, NF - f - 0.5) / EDGE, 1.0)
    return (np.sin(0.5 * math.pi * rising) ** 2).astype(np.float32).reshape(1, NF)


@functools.cache
def spread_table():
    lane = np.arange(128)
    out = np.zeros((128, 8, 128), np.float32)
    for u in range(8):
        out[:, u] = (lane[:, None] // 16 == u) & (lane[:, None] % 16 == lane[None, :] % 16)
    return out.reshape(128, 1024).astype(jnp.bfloat16)


@functools.cache
def lag_tables():
    p = np.arange(HALF, dtype=np.int64)
    out = np.zeros((4, LAGS // 2, HALF), np.float32)
    for odd in range(2):
        m = np.arange(odd, LAGS, 2, dtype=np.int64) - LAGS // 2
        cos, sin = trig(m[:, None] * p[None, :], NT)
        mid_cos, mid_sin = trig(m * HALF, NT)
        out[2 * odd], out[2 * odd + 1] = cos, sin
        out[2 * odd + 1, :, 0] = np.rint(mid_sin if odd else mid_cos)
    return out.astype(jnp.bfloat16)


def spectra_kernel(pick_ref, got_ref, smooth_ref, taper_ref, spread_ref, table_ref, out_ref, x_ref, re_ref, im_ref):
    step = pl.program_id(0)

    @pl.when(step == 0)
    def _():
        for s in range(SEGS):
            seg = got_ref[:, s * NT : (s + 1) * NT]
            x = jnp.dot(pick_ref[...], seg, preferred_element_type=F32)
            x_ref[s * 8 : s * 8 + 8, :] = x

    prod = jnp.dot(x_ref[...].astype(BF), table_ref[0], preferred_element_type=F32)
    cols = pl.ds(pl.multiple_of(step * 256, 256), 256)
    re_ref[:, cols] = prod[:, :256]
    im_ref[:, cols] = prod[:, 256:]

    @pl.when(step == pl.num_programs(0) - 1)
    def _():
        tiles = NF // 128

        def power(t):
            lanes = slice(t % tiles * 128, t % tiles * 128 + 128)
            re, im = re_ref[:, lanes], im_ref[:, lanes]
            p = re * re + im * im
            hi = p.astype(BF)
            return jnp.concatenate([hi, (p - hi.astype(F32)).astype(BF)], axis=0)

        powers = [power(t) for t in range(tiles)]
        row = lax.broadcasted_iota(jnp.int32, (64, 128), 0)
        is_re = (row // CH) % 2 == 0
        lane_seg = lax.broadcasted_iota(jnp.int32, (8, 128), 1) // 16
        for t in range(tiles):
            lanes = slice(t * 128, t * 128 + 128)
            near = jnp.concatenate([powers[t - 1], powers[t], powers[(t + 1) % tiles]], axis=1)
            both = jnp.dot(near, smooth_ref[t], preferred_element_type=F32)
            smooth = (both[:64] + both[64:]) * (1.0 / (2 * SMOOTH + 1))
            scale = taper_ref[:, lanes] * lax.rsqrt(smooth + 1e-06)
            spec = (jnp.where(is_re, re_ref[:, lanes], im_ref[:, lanes]) * scale).astype(BF)
            spread = jnp.dot(spec, spread_ref[...], preferred_element_type=F32)
            groups = []
            for u in range(8):
                chunk = spread[:, u * 128 : u * 128 + 128]
                acc = chunk[0:8]
                for s in range(1, SEGS):
                    acc = jnp.where(lane_seg == s, chunk[s * 8 : s * 8 + 8], acc)
                groups.append(acc)
            out_ref[t * 64 : t * 64 + 64, :] = jnp.concatenate(groups, axis=0).astype(BF)


def spectra_of(pick, got):
    whole = lambda shape: pl.BlockSpec(shape, lambda i: (0,) * len(shape))
    return pl.pallas_call(
        spectra_kernel,
        grid=(8,),
        out_shape=jax.ShapeDtypeStruct((1024, 128), BF),
        in_specs=[
            whole((8, SLOTS)),
            whole((SLOTS, WIN)),
            whole((16, 384, 128)),
            whole((1, NF)),
            whole((128, 1024)),
            pl.BlockSpec((1, NT, 512), lambda i: (i, 0, 0)),
        ],
        out_specs=whole((1024, 128)),
        scratch_shapes=[
            pltpu.VMEM((64, NT), F32),
            pltpu.VMEM((64, NF), F32),
            pltpu.VMEM((64, NF), F32),
        ],
        compiler_params=pltpu.CompilerParams(vmem_limit_bytes=40 * 2**20),
        cost_estimate=pl.CostEstimate(flops=2 * 64 * NT * NT, bytes_accessed=NT * NT * 2, transcendentals=0),
        name="spectra",
    )(pick, got, smooth_table(), taper_row(), spread_table(), dft_table())


def pair_kernel(pos_ref, a_ref, b_ref, lag_ref, out_ref, x_ref, y_ref, f_ref):
    nrow, ncol = b_ref.shape[0], a_ref.shape[0]
    sub = lax.broadcasted_iota(jnp.int32, (16, 128), 0)
    lane = lax.broadcasted_iota(jnp.int32, (16, 128), 1)
    diagonal = (lane % GRP == sub).astype(F32)
    first = (lane // CH) % 2 == 0
    swap_sign = jnp.where(lax.broadcasted_iota(jnp.int32, (16, 128), 0) % 8 < 4, 1.0, -1.0)

    def group(g, special):
        rows = pl.ds(pl.multiple_of(g * 16, 16), 16)
        tiles = [a_ref[d, rows, :] for d in range(ncol)]
        turned = []
        for d in range(ncol):
            v = tiles[d].astype(F32)
            v = jnp.concatenate([pltpu.roll(v[0:8], 4, 0), pltpu.roll(v[8:16], 4, 0)], axis=0)
            turned.append(v * swap_sign)
        own = [b_ref[d, rows, :].astype(F32) for d in range(nrow)]
        prods = []
        for h in range(2):
            left = jnp.concatenate([t.astype(F32)[h * 8 : h * 8 + 8] for t in tiles], axis=0)
            right = jnp.concatenate([t[h * 8 : h * 8 + 8] for t in turned], axis=0)
            w = jnp.concatenate([left, right], axis=1).astype(BF)
            blocks = []
            for d in range(nrow):
                for c in range(CH):
                    r = h * 8 + c
                    re = own[d][r : r + 1, :] * diagonal
                    im = own[d][r + CH : r + CH + 1, :] * diagonal
                    blocks.append(jnp.concatenate([re, im], axis=1).astype(BF))
            lhs = jnp.concatenate(blocks, axis=0)
            prods.append(
                lax.dot_general(lhs, w, (((1,), (1,)), ((), ())), preferred_element_type=F32)
            )
        pairs = nrow * CH // 2
        for jp in range(pairs):
            parts = []
            for h in range(2):
                t0 = prods[h][jp * 16 : jp * 16 + 16]
                t1 = prods[h][(jp + pairs) * 16 : (jp + pairs) * 16 + 16]
                re = jnp.where(first, t0, pltpu.roll(t1, 4, 1))
                im = jnp.where(first, pltpu.roll(t0, 124, 1), t1)
                parts += [re, im]
            re0, im0, re1, im1 = parts
            sums = [re0 + re1, im0 - im1, re0 - re1, im0 + im1]
            if special:
                top = sub == 0
                sums = [
                    jnp.where(top, re0, sums[0]),
                    jnp.where(top, re1, sums[1]),
                    jnp.where(top, re0, sums[2]),
                    jnp.where(top, im1, sums[3]),
                ]
            for k in range(4):
                x_ref[k, rows, jp * 128 : jp * 128 + 128] = sums[k].astype(BF)

    group(0, True)

    @pl.loop(1, NGRP)
    def _(g):
        group(g, False)

    @pl.loop(0, 8)
    def _(n):
        cols = pl.ds(pl.multiple_of(n * 256, 256), 256)
        for odd in range(2):
            y = jnp.dot(lag_ref[2 * odd], x_ref[2 * odd, :, cols], preferred_element_type=F32)
            y += jnp.dot(lag_ref[2 * odd + 1], x_ref[2 * odd + 1, :, cols], preferred_element_type=F32)
            y_ref[0, pl.ds(odd, LAGS // 2, stride=2), :] = y[:, :128]
            y_ref[1, pl.ds(odd, LAGS // 2, stride=2), :] = y[:, 128:]
        for k in range(2):
            at = pl.ds(pl.multiple_of((n * 2 + k) * 128, 128), 128)
            for t in range(LAGS // 128):
                f_ref[t, at, :] = jnp.transpose(y_ref[k, t * 128 : t * 128 + 128, :])

    my_row, my_col = pos_ref[0], pos_ref[1]
    line = lax.broadcasted_iota(jnp.int32, (16, 128), 0)

    @pl.loop(0, ncol)
    def _(d):
        for c in range(CH):
            own = jnp.where(d == my_col, my_row * CH + c, -1)
            for e in range(2):
                drop = line + e * 16 == own
                for t in range(LAGS // 128):
                    v = f_ref[t, pl.ds(d * 8 + e * 4 + c, 16, stride=128), :]
                    v = jnp.where(drop, 0.0, v * (1.0 / math.sqrt(SEGS * NF)))
                    out_ref[d * CH + c, e * 16 : e * 16 + 16, t * 128 : t * 128 + 128] = v.astype(BF)


def pairs_of(pos, a, b):
    nrow, ncol = b.shape[0], a.shape[0]
    assert nrow * CH == 32 and ncol * CH == 64
    vmem = pl.BlockSpec(memory_space=pltpu.VMEM)
    return pl.pallas_call(
        pair_kernel,
        out_shape=jax.ShapeDtypeStruct((ncol * CH, nrow * CH, LAGS), BF),
        in_specs=[pl.BlockSpec(memory_space=pltpu.SMEM), vmem, vmem, vmem],
        out_specs=vmem,
        scratch_shapes=[
            pltpu.VMEM((4, HALF, 2048), BF),
            pltpu.VMEM((2, LAGS, 128), F32),
            pltpu.VMEM((LAGS // 128, 2048, 128), F32),
        ],
        compiler_params=pltpu.CompilerParams(vmem_limit_bytes=52 * 2**20),
        cost_estimate=pl.CostEstimate(flops=2**34, bytes_accessed=16 * 2**20, transcendentals=0),
        name="pairs",
    )(pos, a, b, lag_tables())


def local(strain, file_channels, file_counts, window_start):
    nrow, ncol = lax.axis_size("row"), lax.axis_size("col")
    my_row, my_col = lax.axis_index("row"), lax.axis_index("col")
    window = lax.dynamic_slice_in_dim(strain, window_start[0], WIN, 1)
    slot = jnp.arange(SLOTS, dtype=jnp.int32)
    live = slot < file_counts[0]
    owner = jnp.where(live, file_channels // CH // ncol, -1)
    place = file_channels % CH
    before = (owner[None, :] == owner[:, None]) & (slot[None, :] < slot[:, None])
    rank = jnp.sum(before.astype(jnp.int32), axis=1)
    lines = jnp.arange(2 * nrow, dtype=jnp.int32)
    choose = (owner[None, :] == lines[:, None] // 2) & (rank[None, :] == lines[:, None] % 2)
    labels = jnp.sum(jnp.where(choose, place[None, :] + 1, 0), axis=1) - 1
    bundle = jnp.dot(choose.astype(BF), window, preferred_element_type=F32).astype(BF)
    tags = jnp.broadcast_to(labels.astype(BF)[:, None], (2 * nrow, 128))
    sent = jnp.concatenate([bundle, tags], axis=1).reshape(nrow, 2, WIN + 128)
    got = lax.all_to_all(sent, "row", 0, 0).reshape(2 * nrow, WIN + 128)
    wanted = (jnp.arange(8, dtype=jnp.int32) % CH).astype(F32)
    pick = (got[:, WIN].astype(F32)[None, :] == wanted[:, None]).astype(BF)
    own = spectra_of(pick, got[:, :WIN])
    b = lax.all_gather(own, "row", axis=0)
    a = lax.all_gather(own, "col", axis=0)
    pos = jnp.stack([my_row, my_col]).astype(jnp.int32)
    return pairs_of(pos, a, b)


def solution(mesh):
    placed = (P(("row", "col"), None), P(("row", "col")), P(("row", "col")), P(("row", "col")))
    return jax.shard_map(
        local, mesh=mesh, in_specs=placed, out_specs=P("row", "col", None), check_vma=False
    )
```

time: 760 us -> 204 us (0.27)
  other arithmetic: 314 us -> 1.39 us
  local copies, waits for them, and re-layouts: 153 us -> 2.94 us
  matrix products: 116 us -> 0.5 us
  Pallas kernels: 0 us -> 69.1 us
  blocking collectives: 23 us -> 0 us
  waiting for transfers between devices: 129 us -> 106 us
  starting transfers between devices: 0.27 us -> 8.58 us
  loops' own time: 8.1 us -> 0 us
    another operation x14 -> x1, other arithmetic: 181 us -> 0.08 us  [local(): pos = jnp.stack([my_row, my_col]).astype(jnp.int32)]
    concatenate x6 -> x1, other arithmetic: 130 us -> 0.07 us  [local(): sent = jnp.concatenate([bundle, tags], axis=1).reshape(nrow, 2, WIN + 128)]
    dot_general x21 -> x1, matrix products: 116 us -> 0.5 us  [local(): jnp.dot(choose.astype(BF), window, preferred_element_type=F32).astype(BF)]
    dynamic_slice x29 -> x0, local copies, waits for them, and re-layouts: 81.1 us -> none  [the longest x8 38.5 us: correlate_one_block(): turned = lax.dynamic_slice_in_dim(flipped, first_col, block_cols, 0)]
    pallas_call x0 -> x2, Pallas kernels: none -> 69.1 us  [the longest x1 50.6 us: pairs_of(): pl.pallas_call(pair_kernel, out_shape=jax.ShapeDtypeStruct((ncol * CH, nr...]
    concatenate x4 -> x0, local copies, waits for them, and re-layouts: 47.9 us -> none  [correlate_one_block(): jnp.concatenate([real_cross, imag_cross], axis=2).astype(jnp.bfloat16)]
    all_gather x3 -> x2, waiting for transfers between devices: 129 us -> 91.1 us  [the longest x1 53.6 us: local(): b = lax.all_gather(own, 'row', axis=0)]
    unnamed x1 -> x0, blocking collectives: 23 us -> none
  transfers between devices with their start and end apart: 3 -> 3, of which waited for: 3 -> 3; matrix products, arithmetic and copies ran while one was open for 6% -> 0% of each run, Pallas kernels for 0% -> 0%
where the time goes in v1:
time: 204 us; the launch traced here: 203 us
  waiting for transfers between devices  106 us (52%)
  Pallas kernels  69.1 us (34%)
  between operations  14.9 us (7%)
  starting transfers between devices  8.58 us (4%)
  local copies, waits for them, and re-layouts  2.94 us (1%)
    all_gather x1, waiting for transfers between devices, local(): b = lax.all_gather(own, 'row', axis=0)  53.6 us
    pallas_call x1, Pallas kernels, pairs_of(): pl.pallas_call(pair_kernel, out_shape=jax.ShapeDtypeStruct((ncol * CH, nr...  50.6 us
    all_gather x1, waiting for transfers between devices, local(): a = lax.all_gather(own, 'col', axis=0)  37.6 us
    pallas_call x1, Pallas kernels, spectra_of(): pl.pallas_call(spectra_kernel, grid=(8,), out_shape=jax.ShapeDtypeStruct(...  18.5 us
    all_to_all x1, waiting for transfers between devices, local(): got = lax.all_to_all(sent, 'row', 0, 0).reshape(2 * nrow, WIN + 128)  14.2 us
    all_to_all x1, starting transfers between devices, local(): got = lax.all_to_all(sent, 'row', 0, 0).reshape(2 * nrow, WIN + 128)  8.5 us
  transfers between devices with their start and end apart: 3, of which 3 were waited for; matrix products, arithmetic and copies ran while one was open for 0% of the time, Pallas kernels for 0%

profile of v1, /device:TPU:1, one launch (start us, length us, event | category | flops | bytes accessed | tf_op | source)
XLA Modules:
  0.0 203.4 jit_solution(13733869819936144115)
XLA Ops:
  6.5 0.0 copy-start
  7.9 0.7 compare_select_fusion
  8.6 0.2 convert_reduce_fusion.1
  8.8 0.2 select_reduce_fusion
  9.0 0.0 copy-done
  9.0 0.5 convolution_convert_fusion
  9.5 0.1 broadcast_in_dim.14
  9.6 0.1 pad_maximum_fusion
  9.7 1.2 reshape.84
  10.9 8.5 %all-to-all-start = ((bf16[8,2,32896]{2,1,0:T(2,128)(2,1)}), bf16[8,2,32896]{2,1,0:T(2,128)(2,1)S(1)}, u32[]{:S(2)}, u32[]{:S(2)}) async-start(bf16[8,2,32896]{2,1,0:T(2,128)(2,1)} %reshape.84), calls=%async_computation | async-start | bytes 2105344 | tf_op jit(solution)/shard_map/all_to_all | solution.py:289
  19.4 0.0 all-gather.7.cloned.1.call-start
  19.4 14.2 %all-to-all-done = bf16[8,2,32896]{2,1,0:T(2,128)(2,1)S(1)} async-done(((bf16[8,2,32896]{2,1,0:T(2,128)(2,1)}), bf16[8,2,32896]{2,1,0:T(2,128)(2,1)S(1)}, u32[]{:S(2)}, u32[]{:S(2)}) %all-to-all-start) | async-done | bytes 1052704 | tf_op jit(solution)/shard_map/all_to_all | solution.py:289
  33.6 0.4 reshape.85
  34.0 0.0 copy-start.1
  34.1 0.0 copy-start.2
  34.1 0.0 copy-start.3
  34.1 0.1 convert_reduce_fusion
  34.2 0.1 slice.9.got_ref
  34.3 0.1 compare_convert_fusion.pick_ref
  34.3 1.1 copy-done.1
  35.5 0.0 copy-done.2
  35.5 0.0 copy-done.3
  35.5 18.5 %spectra.1 = bf16[1024,128]{1,0:T(8,128)(2,1)} custom-call(bf16[8,16]{1,0:T(8,128)(2,1)S(1)} %compare_convert_fusion.pick_ref, bf16[16,32768]{1,0:T(8,128)(2,1)S(1)} %slice.9.got_ref, bf16[16,384,128]{2,1,0:T(8,128)(2,1)S(1)} %copy-done.1, f32[1,2048]{1,0:T(1,128)S(1)} %copy-done.3, bf16[128,1024]{1,0:T(8,128)(2,1)S(1)} %copy-done.2, ...), custom_call_target="tpu_custom_call" | custom-call | flops 2147483648 | bytes 33554432 | tf_op jit(solution)/shard_map/spectra/pallas_call | solution.py:140
  54.0 0.0 all-gather.7.cloned.1.call-update
  54.0 0.0 all-gather.5.cloned.1.call-start
  54.0 0.7 all-gather.5.cloned.1.call-update
  54.8 0.1 pad_add_fusion.pos_ref
  54.8 53.6 %all-gather.7.cloned.1.call-done = bf16[8192,128]{1,0:T(8,128)(2,1)} async-done(((bf16[1024,128]{1,0:T(8,128)(2,1)}), bf16[8192,128]{1,0:T(8,128)(2,1)}) %all-gather.7.cloned.1.call-update) | async-done | bytes 2097168 | tf_op jit(solution)/shard_map/all_gather | solution.py:293
  108.4 37.6 %all-gather.5.cloned.1.call-done = bf16[16384,128]{1,0:T(8,128)(2,1)} async-done(((bf16[1024,128]{1,0:T(8,128)(2,1)}), bf16[16384,128]{1,0:T(8,128)(2,1)}) %all-gather.5.cloned.1.call-update) | async-done | bytes 4194320 | tf_op jit(solution)/shard_map/all_gather | solution.py:294
  146.0 50.6 %pairs.1 = bf16[64,32,1024]{2,1,0:T(8,128)(2,1)} custom-call(s32[2]{0:T(128)S(1)} %pad_add_fusion.pos_ref, bf16[16,1024,128]{2,1,0:T(8,128)(2,1)} %bitcast.10, bf16[8,1024,128]{2,1,0:T(8,128)(2,1)} %bitcast.11, bf16[4,512,1024]{2,1,0:T(8,128)(2,1)} %constant.102.clone.lag_ref), custom_call_target="tpu_custom_call" | custom-call | flops 17179869184 | bytes 16777216 | tf_op jit(solution)/shard_map/pairs/pallas_call | solution.py:257
  (3 shorter events, 0.0 us)
Async XLA Ops:
  6.5 2.5 %copy-start = (bf16[16,33280]{1,0:T(8,128)(2,1)S(1)}, bf16[16,33280]{1,0:T(8,128)(2,1)}, u32[]{:S(2)}) copy-start(bf16[16,33280]{1,0:T(8,128)(2,1)} %param.9) | copy-start | bytes 3194884
  10.9 22.7 %all-to-all-start = ((bf16[8,2,32896]{2,1,0:T(2,128)(2,1)}), bf16[8,2,32896]{2,1,0:T(2,128)(2,1)S(1)}, u32[]{:S(2)}, u32[]{:S(2)}) async-start(bf16[8,2,32896]{2,1,0:T(2,128)(2,1)} %reshape.84), calls=%async_computation | async-start | bytes 2105344 | tf_op jit(solution)/shard_map/all_to_all | solution.py:289
  19.4 89.0 %all-gather.7.cloned.1.call-start = ((), (), s32[]{:S(2)}) async-start(), calls=%async_computation.2 | async-start | bytes 2359296 | tf_op jit(solution)/shard_map/all_gather | solution.py:293
  34.0 1.4 copy-start.1
  34.1 1.4 copy-start.2
  34.1 1.4 copy-start.3
  54.0 92.0 %all-gather.5.cloned.1.call-start = ((), (), s32[]{:S(2)}) async-start(), calls=%async_computation.1 | async-start | bytes 4456448 | tf_op jit(solution)/shard_map/all_gather | solution.py:294
Sparse Core Ops, SparseCore 0:
  54.1 54.2 all-gather.6
  110.1 35.8 all-gather.4

commit v2 on v1

--- a/solution.py
+++ b/solution.py
@@ -161,13 +161,35 @@
     )(pick, got, smooth_table(), taper_row(), spread_table(), dft_table())
 
 
-def pair_kernel(pos_ref, a_ref, b_ref, lag_ref, out_ref, x_ref, y_ref, f_ref):
-    nrow, ncol = b_ref.shape[0], a_ref.shape[0]
+CHUNKS = 4
+
+
+def pair_kernel(pos_ref, a_hbm, *refs):
+    nrow, ncol = 8, 16
+    b_hbm = refs[:nrow]
+    lag_hbm, out_hbm, a_ref, b_ref, lag_ref, x_ref, y_ref, f_ref, o_ref, in_sem, lag_sem, out_sem = refs[nrow:]
+    size = 1024 // CHUNKS
+
+    def arrive(k):
+        rows = pl.ds(k * size, size)
+        copies = [pltpu.make_async_copy(a_hbm.at[:, rows, :], a_ref.at[:, rows, :], in_sem.at[k, nrow])]
+        for r in range(nrow):
+            copies.append(
+                pltpu.make_async_copy(
+                    b_hbm[r].at[rows, :], b_ref.at[pos_ref[2 + r], rows, :], in_sem.at[k, r]))
+        return copies
+
+    for k in range(CHUNKS):
+        for copy in arrive(k):
+            copy.start()
+    lag_copy = pltpu.make_async_copy(lag_hbm, lag_ref, lag_sem)
+    lag_copy.start()
+
     sub = lax.broadcasted_iota(jnp.int32, (16, 128), 0)
     lane = lax.broadcasted_iota(jnp.int32, (16, 128), 1)
-    diagonal = (lane % GRP == sub).astype(F32)
+    diagonal = (lane % GRP == sub).astype(F32).astype(BF)
     first = (lane // CH) % 2 == 0
-    swap_sign = jnp.where(lax.broadcasted_iota(jnp.int32, (16, 128), 0) % 8 < 4, 1.0, -1.0)
+    swap_sign = jnp.where(sub % 8 < 4, 1.0, -1.0)
 
     def group(g, special):
         rows = pl.ds(pl.multiple_of(g * 16, 16), 16)
@@ -187,9 +209,9 @@
             for d in range(nrow):
                 for c in range(CH):
                     r = h * 8 + c
-                    re = own[d][r : r + 1, :] * diagonal
-                    im = own[d][r + CH : r + CH + 1, :] * diagonal
-                    blocks.append(jnp.concatenate([re, im], axis=1).astype(BF))
+                    re = jnp.broadcast_to(own[d][r : r + 1, :], (16, 128)).astype(BF)
+                    im = jnp.broadcast_to(own[d][r + CH : r + CH + 1, :], (16, 128)).astype(BF)
+                    blocks.append(jnp.concatenate([re * diagonal, im * diagonal], axis=1))
             lhs = jnp.concatenate(blocks, axis=0)
             prods.append(
                 lax.dot_general(lhs, w, (((1,), (1,)), ((), ())), preferred_element_type=F32)
@@ -216,11 +238,18 @@
             for k in range(4):
                 x_ref[k, rows, jp * 128 : jp * 128 + 128] = sums[k].astype(BF)
 
+    @pl.loop(0, CHUNKS)
+    def _(k):
+        for copy in arrive(k):
+            copy.wait()
+
+        @pl.loop(0, NGRP // CHUNKS, step=4)
+        def _(g):
+            for u in range(4):
+                group(k * (NGRP // CHUNKS) + g + u, False)
+
     group(0, True)
-
-    @pl.loop(1, NGRP)
-    def _(g):
-        group(g, False)
+    lag_copy.wait()
 
     @pl.loop(0, 8)
     def _(n):
@@ -231,43 +260,81 @@
             y_ref[0, pl.ds(odd, LAGS // 2, stride=2), :] = y[:, :128]
             y_ref[1, pl.ds(odd, LAGS // 2, stride=2), :] = y[:, 128:]
         for k in range(2):
-            at = pl.ds(pl.multiple_of((n * 2 + k) * 128, 128), 128)
+            at = pl.ds((n * 2 + k) * 129, 128)
             for t in range(LAGS // 128):
                 f_ref[t, at, :] = jnp.transpose(y_ref[k, t * 128 : t * 128 + 128, :])
 
     my_row, my_col = pos_ref[0], pos_ref[1]
     line = lax.broadcasted_iota(jnp.int32, (16, 128), 0)
 
+    def leave(d):
+        return pltpu.make_async_copy(
+            o_ref.at[d % 2], out_hbm.at[pl.ds(d * CH, CH), :, :], out_sem.at[d % 2])
+
     @pl.loop(0, ncol)
     def _(d):
+        @pl.when(d >= 2)
+        def _():
+            leave(d - 2).wait()
+
         for c in range(CH):
             own = jnp.where(d == my_col, my_row * CH + c, -1)
             for e in range(2):
                 drop = line + e * 16 == own
                 for t in range(LAGS // 128):
-                    v = f_ref[t, pl.ds(d * 8 + e * 4 + c, 16, stride=128), :]
+                    v = f_ref[t, pl.ds(d * 8 + e * 4 + c, 16, stride=129), :]
                     v = jnp.where(drop, 0.0, v * (1.0 / math.sqrt(SEGS * NF)))
-                    out_ref[d * CH + c, e * 16 : e * 16 + 16, t * 128 : t * 128 + 128] = v.astype(BF)
+                    o_ref[d % 2, c, e * 16 : e * 16 + 16, t * 128 : t * 128 + 128] = v.astype(BF)
+        leave(d).start()
+
+    leave(ncol - 2).wait()
+    leave(ncol - 1).wait()
 
 
 def pairs_of(pos, a, b):
-    nrow, ncol = b.shape[0], a.shape[0]
-    assert nrow * CH == 32 and ncol * CH == 64
-    vmem = pl.BlockSpec(memory_space=pltpu.VMEM)
+    nrow, ncol = len(b), a.shape[0]
+    assert nrow == 8 and ncol == 16
+    anywhere = pl.BlockSpec(memory_space=pl.ANY)
     return pl.pallas_call(
         pair_kernel,
         out_shape=jax.ShapeDtypeStruct((ncol * CH, nrow * CH, LAGS), BF),
-        in_specs=[pl.BlockSpec(memory_space=pltpu.SMEM), vmem, vmem, vmem],
-        out_specs=vmem,
+        in_specs=[pl.BlockSpec(memory_space=pltpu.SMEM)] + [anywhere] * (nrow + 2),
+        out_specs=anywhere,
         scratch_shapes=[
+            pltpu.VMEM((ncol, 1024, 128), BF),
+            pltpu.VMEM((nrow, 1024, 128), BF),
+            pltpu.VMEM((4, LAGS // 2, HALF), BF),
             pltpu.VMEM((4, HALF, 2048), BF),
             pltpu.VMEM((2, LAGS, 128), F32),
-            pltpu.VMEM((LAGS // 128, 2048, 128), F32),
+            pltpu.VMEM((LAGS // 128, 16 * 129 + 8, 128), F32),
+            pltpu.VMEM((2, CH, nrow * CH, LAGS), BF),
+            pltpu.SemaphoreType.DMA((CHUNKS, nrow + 1)),
+            pltpu.SemaphoreType.DMA,
+            pltpu.SemaphoreType.DMA((2,)),
         ],
         compiler_params=pltpu.CompilerParams(vmem_limit_bytes=52 * 2**20),
         cost_estimate=pl.CostEstimate(flops=2**34, bytes_accessed=16 * 2**20, transcendentals=0),
         name="pairs",
-    )(pos, a, b, lag_tables())
+    )(pos, a, *b, lag_tables())
+
+
+def over_row(own, my_row):
+    def move(block, step, across=0):
+        pairs = [(y * 4 + z, (y ^ across) * 4 + (z + step) % 4) for y in range(2) for z in range(4)]
+        return lax.ppermute(block, "row", pairs)
+
+    y, z = my_row // 4, my_row % 4
+    index = lambda step, across: (y ^ across) * 4 + (z + step) % 4
+    other = move(own, 0, 1)
+    left, right = move(own, 1), move(own, -1)
+    other_left, other_right = move(other, 1), move(other, -1)
+    far, other_far = move(left, 1), move(other_right, -1)
+    blocks = [own, other, left, right, other_left, other_right, far, other_far]
+    rows = [
+        index(0, 0), index(0, 1), index(-1, 0), index(1, 0),
+        index(-1, 1), index(1, 1), index(2, 0), index(2, 1),
+    ]
+    return blocks, rows
 
 
 def local(strain, file_channels, file_counts, window_start):
@@ -290,9 +357,9 @@
     wanted = (jnp.arange(8, dtype=jnp.int32) % CH).astype(F32)
     pick = (got[:, WIN].astype(F32)[None, :] == wanted[:, None]).astype(BF)
     own = spectra_of(pick, got[:, :WIN])
-    b = lax.all_gather(own, "row", axis=0)
     a = lax.all_gather(own, "col", axis=0)
-    pos = jnp.stack([my_row, my_col]).astype(jnp.int32)
+    b, rows = over_row(own, my_row)
+    pos = jnp.stack([my_row, my_col, *rows]).astype(jnp.int32)
     return pairs_of(pos, a, b)
 
 

time: 204 us -> 134 us (0.66)
  waiting for transfers between devices: 106 us -> 41.8 us
  Pallas kernels: 69.1 us -> 53.2 us
  starting transfers between devices: 8.58 us -> 19.2 us
    all_gather x1 -> x0, waiting for transfers between devices: 53.6 us -> none  [local(): b = lax.all_gather(own, 'row', axis=0)]
    all_gather x1, waiting for transfers between devices: 37.6 us -> 13 us  [local(): a = lax.all_gather(own, 'col', axis=0)]
    pallas_call x1, Pallas kernels: 50.6 us -> 34.8 us  [pairs_of(): pl.pallas_call(pair_kernel, out_shape=jax.ShapeDtypeStruct((ncol * CH, nr...]
    ppermute x0 -> x7, waiting for transfers between devices: none -> 14.6 us  [move(): return lax.ppermute(block, 'row', pairs)]
    ppermute x0 -> x7, starting transfers between devices: none -> 10.6 us  [move(): return lax.ppermute(block, 'row', pairs)]
  transfers between devices with their start and end apart: 3 -> 9, of which waited for: 3 -> 7; matrix products, arithmetic and copies ran while one was open for 0% -> 0% of each run, Pallas kernels for 0% -> 0%
where the time goes in v2:
time: 134 us
  Pallas kernels  53.2 us (40%)
  waiting for transfers between devices  41.8 us (31%)
  starting transfers between devices  19.2 us (14%)
  between operations  14.9 us (11%)
  local copies, waits for them, and re-layouts  3.03 us (2%)
    pallas_call x1, Pallas kernels, pairs_of(): pl.pallas_call(pair_kernel, out_shape=jax.ShapeDtypeStruct((ncol * CH, nr...  34.8 us
    pallas_call x1, Pallas kernels, spectra_of(): pl.pallas_call(spectra_kernel, grid=(8,), out_shape=jax.ShapeDtypeStruct(...  18.5 us
    ppermute x7, waiting for transfers between devices, move(): return lax.ppermute(block, 'row', pairs)  14.6 us
    all_to_all x1, waiting for transfers between devices, local(): got = lax.all_to_all(sent, 'row', 0, 0).reshape(2 * nrow, WIN + 128)  14.2 us
    all_gather x1, waiting for transfers between devices, local(): a = lax.all_gather(own, 'col', axis=0)  13 us
    ppermute x7, starting transfers between devices, move(): return lax.ppermute(block, 'row', pairs)  10.6 us
    all_to_all x1, starting transfers between devices, local(): got = lax.all_to_all(sent, 'row', 0, 0).reshape(2 * nrow, WIN + 128)  8.49 us
  transfers between devices with their start and end apart: 9, of which 7 were waited for; matrix products, arithmetic and copies ran while one was open for 0% of the time, Pallas kernels for 0%

profile of v2, /device:TPU:1, one launch (start us, length us, event | category | flops | bytes accessed | tf_op | source)
XLA Modules:
  0.0 134.0 jit_solution(9177892054772649485)
XLA Ops:
  6.5 0.0 copy-start
  7.9 0.7 compare_select_fusion
  8.6 0.2 convert_reduce_fusion.1
  8.8 0.2 select_reduce_fusion
  9.0 0.0 copy-done
  9.0 0.5 convolution_convert_fusion
  9.5 0.1 broadcast_in_dim.14
  9.6 0.1 pad_maximum_fusion
  9.7 1.2 reshape.84
  10.9 8.5 %all-to-all-start = ((bf16[8,2,32896]{2,1,0:T(2,128)(2,1)}), bf16[8,2,32896]{2,1,0:T(2,128)(2,1)S(1)}, u32[]{:S(2)}, u32[]{:S(2)}) async-start(bf16[8,2,32896]{2,1,0:T(2,128)(2,1)} %reshape.84), calls=%async_computation | async-start | bytes 2105344 | tf_op jit(solution)/shard_map/all_to_all | solution.py:356
  19.4 0.0 all-gather.3.cloned.1.call-start
  19.4 14.2 %all-to-all-done = bf16[8,2,32896]{2,1,0:T(2,128)(2,1)S(1)} async-done(((bf16[8,2,32896]{2,1,0:T(2,128)(2,1)}), bf16[8,2,32896]{2,1,0:T(2,128)(2,1)S(1)}, u32[]{:S(2)}, u32[]{:S(2)}) %all-to-all-start) | async-done | bytes 1052704 | tf_op jit(solution)/shard_map/all_to_all | solution.py:356
  33.6 0.4 reshape.85
  34.0 0.0 copy-start.1
  34.0 0.0 copy-start.2
  34.1 0.0 copy-start.3
  34.1 0.1 convert_reduce_fusion
  34.2 0.1 slice.9.got_ref
  34.3 0.1 compare_convert_fusion.pick_ref
  34.3 1.1 copy-done.1
  35.4 0.0 copy-done.2
  35.5 0.0 copy-done.3
  35.5 18.5 %spectra.1.refs_0_ = bf16[1024,128]{1,0:T(8,128)(2,1)} custom-call(bf16[8,16]{1,0:T(8,128)(2,1)S(1)} %compare_convert_fusion.pick_ref, bf16[16,32768]{1,0:T(8,128)(2,1)S(1)} %slice.9.got_ref, bf16[16,384,128]{2,1,0:T(8,128)(2,1)S(1)} %copy-done.1, f32[1,2048]{1,0:T(1,128)S(1)} %copy-done.3, bf16[128,1024]{1,0:T(8,128)(2,1)S(1)} %copy-done.2, ...), custom_call_target="tpu_custom_call" | custom-call | flops 2147483648 | bytes 33554432 | tf_op jit(solution)/shard_map/spectra/pallas_call | solution.py:140
  54.0 0.0 all-gather.3.cloned.1.call-update
  54.0 3.5 %collective-permute-start = (bf16[1024,128]{1,0:T(8,128)(2,1)}, bf16[1024,128]{1,0:T(8,128)(2,1)S(1)}, u32[]{:S(2)}, u32[]{:S(2)}) collective-permute-start(bf16[1024,128]{1,0:T(8,128)(2,1)} %spectra.1.refs_0_), channel_id=1, source_target_pairs={{0,64},{16,80},{32,96},{48,112},{64,0},{80,16},{96,32},{112,48},{1... | collective-permute-start | bytes 786440 | tf_op jit(solution)/shard_map/ppermute | solution.py:324
  57.5 0.9 collective-permute-start.1
  58.4 4.2 %collective-permute-done.refs_1_ = bf16[1024,128]{1,0:T(8,128)(2,1)S(1)} collective-permute-done((bf16[1024,128]{1,0:T(8,128)(2,1)}, bf16[1024,128]{1,0:T(8,128)(2,1)S(1)}, u32[]{:S(2)}, u32[]{:S(2)}) %collective-permute-start) | collective-permute-done | bytes 262176 | tf_op jit(solution)/shard_map/ppermute | solution.py:324
  62.6 1.9 %collective-permute-start.4 = (bf16[1024,128]{1,0:T(8,128)(2,1)S(1)}, bf16[1024,128]{1,0:T(8,128)(2,1)S(1)}, u32[]{:S(2)}, u32[]{:S(2)}) collective-permute-start(bf16[1024,128]{1,0:T(8,128)(2,1)S(1)} %collective-permute-done.refs_1_), channel_id=1, source_target_pairs={{0,48},{16,0},{32,16},{48,32},{64,112},{80,64},{96,80},{112,96},{1... | collective-permute-start | bytes 786440 | tf_op jit(solution)/shard_map/ppermute | solution.py:324
  64.5 0.2 collective-permute-start.2
  64.7 1.3 collective-permute-start.3
  66.0 0.0 collective-permute-done.1.refs_2_
  66.0 0.0 collective-permute-start.5
  66.0 2.2 %collective-permute-done.4.refs_5_ = bf16[1024,128]{1,0:T(8,128)(2,1)S(1)} collective-permute-done((bf16[1024,128]{1,0:T(8,128)(2,1)S(1)}, bf16[1024,128]{1,0:T(8,128)(2,1)S(1)}, u32[]{:S(2)}, u32[]{:S(2)}) %collective-permute-start.4) | collective-permute-done | bytes 262176 | tf_op jit(solution)/shard_map/ppermute | solution.py:324
  68.2 2.8 %collective-permute-start.6 = (bf16[1024,128]{1,0:T(8,128)(2,1)S(1)}, bf16[1024,128]{1,0:T(8,128)(2,1)S(1)}, u32[]{:S(2)}, u32[]{:S(2)}) collective-permute-start(bf16[1024,128]{1,0:T(8,128)(2,1)S(1)} %collective-permute-done.4.refs_5_), channel_id=1, source_target_pairs={{0,48},{16,0},{32,16},{48,32},{64,112},{80,64},{96,80},{112,96},{1... | collective-permute-start | bytes 786440 | tf_op jit(solution)/shard_map/ppermute | solution.py:324
  71.0 0.1 stack.43.pos_ref
  71.0 2.6 %collective-permute-done.2.refs_3_ = bf16[1024,128]{1,0:T(8,128)(2,1)S(1)} collective-permute-done((bf16[1024,128]{1,0:T(8,128)(2,1)}, bf16[1024,128]{1,0:T(8,128)(2,1)S(1)}, u32[]{:S(2)}, u32[]{:S(2)}) %collective-permute-start.2) | collective-permute-done | bytes 262176 | tf_op jit(solution)/shard_map/ppermute | solution.py:324
  73.6 2.4 %collective-permute-done.5.refs_6_ = bf16[1024,128]{1,0:T(8,128)(2,1)S(1)} collective-permute-done((bf16[1024,128]{1,0:T(8,128)(2,1)S(1)}, bf16[1024,128]{1,0:T(8,128)(2,1)S(1)}, u32[]{:S(2)}, u32[]{:S(2)}) %collective-permute-start.5) | collective-permute-done | bytes 262176 | tf_op jit(solution)/shard_map/ppermute | solution.py:324
  76.0 0.0 collective-permute-done.3.refs_4_
  76.0 3.4 %collective-permute-done.6.refs_7_ = bf16[1024,128]{1,0:T(8,128)(2,1)S(1)} collective-permute-done((bf16[1024,128]{1,0:T(8,128)(2,1)S(1)}, bf16[1024,128]{1,0:T(8,128)(2,1)S(1)}, u32[]{:S(2)}, u32[]{:S(2)}) %collective-permute-start.6) | collective-permute-done | bytes 262176 | tf_op jit(solution)/shard_map/ppermute | solution.py:324
  79.3 0.0 copy-start.4
  79.3 13.0 %all-gather.3.cloned.1.call-done = bf16[16384,128]{1,0:T(8,128)(2,1)} async-done(((bf16[1024,128]{1,0:T(8,128)(2,1)}), bf16[16384,128]{1,0:T(8,128)(2,1)}) %all-gather.3.cloned.1.call-update) | async-done | bytes 4194320 | tf_op jit(solution)/shard_map/all_gather | solution.py:360
  92.3 0.0 copy-done.4
  92.3 34.8 %pairs.1 = bf16[64,32,1024]{2,1,0:T(8,128)(2,1)} custom-call(s32[10]{0:T(128)S(1)} %stack.43.pos_ref, bf16[16,1024,128]{2,1,0:T(8,128)(2,1)} %bitcast.17, bf16[1024,128]{1,0:T(8,128)(2,1)} %spectra.1.refs_0_, bf16[1024,128]{1,0:T(8,128)(2,1)S(1)} %collective-permute-done.refs_1_, bf16[1024,128]{1,0:T(8,128)(2,1)S(1)} %collective-permute-done.1.refs_2_, ...), custom_call_target="tpu_custom_call" | custom-call | flops 17179869184 | bytes 16777216 | tf_op jit(solution)/shard_map/pairs/pallas_call | solution.py:298
  (3 shorter events, 0.0 us)
Async XLA Ops:
  6.5 2.5 %copy-start = (bf16[16,33280]{1,0:T(8,128)(2,1)S(1)}, bf16[16,33280]{1,0:T(8,128)(2,1)}, u32[]{:S(2)}) copy-start(bf16[16,33280]{1,0:T(8,128)(2,1)} %param.9) | copy-start | bytes 3194884
  10.9 22.7 %all-to-all-start = ((bf16[8,2,32896]{2,1,0:T(2,128)(2,1)}), bf16[8,2,32896]{2,1,0:T(2,128)(2,1)S(1)}, u32[]{:S(2)}, u32[]{:S(2)}) async-start(bf16[8,2,32896]{2,1,0:T(2,128)(2,1)} %reshape.84), calls=%async_computation | async-start | bytes 2105344 | tf_op jit(solution)/shard_map/all_to_all | solution.py:356
  19.4 73.0 %all-gather.3.cloned.1.call-start = ((), (), s32[]{:S(2)}) async-start(), calls=%async_computation.1 | async-start | bytes 4456448 | tf_op jit(solution)/shard_map/all_gather | solution.py:360
  34.0 1.4 %copy-start.1 = (bf16[16,384,128]{2,1,0:T(8,128)(2,1)S(1)}, bf16[16,384,128]{2,1,0:T(8,128)(2,1)}, u32[]{:S(2)}) copy-start(bf16[16,384,128]{2,1,0:T(8,128)(2,1)} %constant.138.clone.smooth_ref) | copy-start | bytes 4718596
  34.0 1.4 %copy-start.2 = (bf16[128,1024]{1,0:T(8,128)(2,1)S(1)}, bf16[128,1024]{1,0:T(8,128)(2,1)}, u32[]{:S(2)}) copy-start(bf16[128,1024]{1,0:T(8,128)(2,1)} %constant.140.clone.spread_ref) | copy-start | bytes 786436
  34.1 1.4 %copy-start.3 = (f32[1,2048]{1,0:T(1,128)S(1)}, f32[1,2048]{1,0:T(1,128)}, u32[]{:S(2)}) copy-start(f32[1,2048]{1,0:T(1,128)} %constant.139.clone.taper_ref) | copy-start | bytes 24580
  54.0 8.6 %collective-permute-start = (bf16[1024,128]{1,0:T(8,128)(2,1)}, bf16[1024,128]{1,0:T(8,128)(2,1)S(1)}, u32[]{:S(2)}, u32[]{:S(2)}) collective-permute-start(bf16[1024,128]{1,0:T(8,128)(2,1)} %spectra.1.refs_0_), channel_id=1, source_target_pairs={{0,64},{16,80},{32,96},{48,112},{64,0},{80,16},{96,32},{112,48},{1... | collective-permute-start | bytes 786440 | tf_op jit(solution)/shard_map/ppermute | solution.py:324
  57.5 8.5 %collective-permute-start.1 = (bf16[1024,128]{1,0:T(8,128)(2,1)}, bf16[1024,128]{1,0:T(8,128)(2,1)S(1)}, u32[]{:S(2)}, u32[]{:S(2)}) collective-permute-start(bf16[1024,128]{1,0:T(8,128)(2,1)} %spectra.1.refs_0_), channel_id=1, source_target_pairs={{0,16},{16,32},{32,48},{48,0},{64,80},{80,96},{96,112},{112,64},{1... | collective-permute-start | bytes 786440 | tf_op jit(solution)/shard_map/ppermute | solution.py:324
  62.6 5.6 %collective-permute-start.4 = (bf16[1024,128]{1,0:T(8,128)(2,1)S(1)}, bf16[1024,128]{1,0:T(8,128)(2,1)S(1)}, u32[]{:S(2)}, u32[]{:S(2)}) collective-permute-start(bf16[1024,128]{1,0:T(8,128)(2,1)S(1)} %collective-permute-done.refs_1_), channel_id=1, source_target_pairs={{0,48},{16,0},{32,16},{48,32},{64,112},{80,64},{96,80},{112,96},{1... | collective-permute-start | bytes 786440 | tf_op jit(solution)/shard_map/ppermute | solution.py:324
  64.5 9.1 %collective-permute-start.2 = (bf16[1024,128]{1,0:T(8,128)(2,1)}, bf16[1024,128]{1,0:T(8,128)(2,1)S(1)}, u32[]{:S(2)}, u32[]{:S(2)}) collective-permute-start(bf16[1024,128]{1,0:T(8,128)(2,1)} %spectra.1.refs_0_), channel_id=1, source_target_pairs={{0,48},{16,0},{32,16},{48,32},{64,112},{80,64},{96,80},{112,96},{1... | collective-permute-start | bytes 786440 | tf_op jit(solution)/shard_map/ppermute | solution.py:324
  64.7 11.3 %collective-permute-start.3 = (bf16[1024,128]{1,0:T(8,128)(2,1)S(1)}, bf16[1024,128]{1,0:T(8,128)(2,1)S(1)}, u32[]{:S(2)}, u32[]{:S(2)}) collective-permute-start(bf16[1024,128]{1,0:T(8,128)(2,1)S(1)} %collective-permute-done.refs_1_), channel_id=1, source_target_pairs={{0,16},{16,32},{32,48},{48,0},{64,80},{80,96},{96,112},{112,64},{1... | collective-permute-start | bytes 786440 | tf_op jit(solution)/shard_map/ppermute | solution.py:324
  66.0 10.0 %collective-permute-start.5 = (bf16[1024,128]{1,0:T(8,128)(2,1)S(1)}, bf16[1024,128]{1,0:T(8,128)(2,1)S(1)}, u32[]{:S(2)}, u32[]{:S(2)}) collective-permute-start(bf16[1024,128]{1,0:T(8,128)(2,1)S(1)} %collective-permute-done.1.refs_2_), channel_id=1, source_target_pairs={{0,16},{16,32},{32,48},{48,0},{64,80},{80,96},{96,112},{112,64},{1... | collective-permute-start | bytes 786440 | tf_op jit(solution)/shard_map/ppermute | solution.py:324
  68.2 11.1 %collective-permute-start.6 = (bf16[1024,128]{1,0:T(8,128)(2,1)S(1)}, bf16[1024,128]{1,0:T(8,128)(2,1)S(1)}, u32[]{:S(2)}, u32[]{:S(2)}) collective-permute-start(bf16[1024,128]{1,0:T(8,128)(2,1)S(1)} %collective-permute-done.4.refs_5_), channel_id=1, source_target_pairs={{0,48},{16,0},{32,16},{48,32},{64,112},{80,64},{96,80},{112,96},{1... | collective-permute-start | bytes 786440 | tf_op jit(solution)/shard_map/ppermute | solution.py:324
  79.3 13.0 %copy-start.4 = (bf16[1024,128]{1,0:T(8,128)(2,1)}, bf16[1024,128]{1,0:T(8,128)(2,1)S(1)}, u32[]{:S(2)}) copy-start(bf16[1024,128]{1,0:T(8,128)(2,1)S(1)} %collective-permute-done.6.refs_7_) | copy-start | bytes 786436
Sparse Core Ops, SparseCore 0:
  54.1 38.1 all-gather.2

commit v3 on v2

--- a/solution.py
+++ b/solution.py
@@ -25,12 +25,6 @@
 F32 = jnp.float32
 
 
-def frequency_order():
-    p = np.arange(HALF).reshape(NGRP, 1, GRP)
-    mirror = np.where(p == 0, HALF, NF - p)
-    return np.concatenate([p, mirror], axis=1).reshape(NF)
-
-
 def trig(product, size):
     angle = (product % size).astype(np.float32) * np.float32(2.0 * math.pi / size)
     return np.cos(angle.astype(np.float64)), -np.sin(angle.astype(np.float64))
@@ -38,31 +32,52 @@
 
 @functools.cache
 def dft_table():
-    order = frequency_order().astype(np.int64)
-    cos, sin = trig(np.arange(NT, dtype=np.int64)[:, None] * order[None, :], NT)
-    both = np.stack([cos.reshape(NT, 8, 256), sin.reshape(NT, 8, 256)], axis=2)
-    return both.transpose(1, 0, 2, 3).reshape(8, NT, 512).astype(jnp.bfloat16)
-
-
-@functools.cache
-def smooth_table():
-    order = frequency_order()
-    near = np.abs(order[:, None] - order[None, :]) <= SMOOTH
-    tiles = NF // 128
-    out = np.zeros((tiles, 3, 128, 128), np.float32)
-    for t in range(tiles):
-        for k in range(3):
-            s = (t + k - 1) % tiles
-            out[t, k] = near[s * 128 : s * 128 + 128, t * 128 : t * 128 + 128]
-    assert out.sum() == near.sum()
-    return out.reshape(tiles, 384, 128).astype(jnp.bfloat16)
-
-
-@functools.cache
-def taper_row():
-    f = frequency_order().astype(np.float64)
+    p = np.arange(HALF, dtype=np.int64)
+    parts = []
+    for odd in range(2):
+        n = np.arange(odd, NT, 2, dtype=np.int64)
+        cos, sin = trig(n[:, None] * p[None, :], NT)
+        mid_cos, mid_sin = trig(n * HALF, NT)
+        sin[:, 0] = np.rint(mid_sin if odd else mid_cos)
+        both = np.stack([cos.reshape(NT // 2, 8, 128), sin.reshape(NT // 2, 8, 128)], axis=2)
+        parts.append(both.transpose(1, 0, 2, 3).reshape(8, NT // 2, 256))
+    return np.stack(parts, axis=1).astype(jnp.bfloat16)
+
+
+@functools.cache
+def parting_table():
+    lane = np.arange(256)
+    return (lane[:, None] == (lane % 128 * 2 + lane // 128)[None, :]).astype(jnp.bfloat16)
+
+
+@functools.cache
+def smooth_tables():
+    p = np.arange(HALF)
+    order = np.concatenate([p, np.where(p == 0, HALF, NF - p)]).reshape(16, 128)
+    tables, use, count = [], [], 0
+    for t in range(16):
+        near = [np.abs(order[s][:, None] - order[t][None, :]) <= SMOOTH for s in range(16)]
+        tiles = [s for s in range(16) if near[s].any()]
+        table = np.zeros((4, 128, 128), np.float32)
+        for k, s in enumerate(tiles):
+            table[k] = near[s]
+        count += table.sum()
+        tiles += [t] * (4 - len(tiles))
+        same = [k for k, other in enumerate(tables) if (other == table).all()]
+        if not same:
+            tables.append(table)
+        use.append((tiles, same[0] if same else len(tables) - 1))
+    f = np.arange(NF)
+    assert count == (np.minimum(f + SMOOTH, NF - 1) - np.maximum(f - SMOOTH, 0) + 1).sum()
+    return np.stack(tables).reshape(len(tables), 512, 128).astype(jnp.bfloat16), tuple(use)
+
+
+@functools.cache
+def taper_rows():
+    p = np.arange(HALF)
+    f = np.stack([p, np.where(p == 0, HALF, NF - p)]).astype(np.float64)
     rising = np.minimum(np.minimum(f + 0.5, NF - f - 0.5) / EDGE, 1.0)
-    return (np.sin(0.5 * math.pi * rising) ** 2).astype(np.float32).reshape(1, NF)
+    return (np.sin(0.5 * math.pi * rising) ** 2).astype(np.float32)
 
 
 @functools.cache
@@ -87,78 +102,90 @@
     return out.astype(jnp.bfloat16)
 
 
-def spectra_kernel(pick_ref, got_ref, smooth_ref, taper_ref, spread_ref, table_ref, out_ref, x_ref, re_ref, im_ref):
-    step = pl.program_id(0)
-
-    @pl.when(step == 0)
-    def _():
-        for s in range(SEGS):
-            seg = got_ref[:, s * NT : (s + 1) * NT]
-            x = jnp.dot(pick_ref[...], seg, preferred_element_type=F32)
-            x_ref[s * 8 : s * 8 + 8, :] = x
-
-    prod = jnp.dot(x_ref[...].astype(BF), table_ref[0], preferred_element_type=F32)
-    cols = pl.ds(pl.multiple_of(step * 256, 256), 256)
-    re_ref[:, cols] = prod[:, :256]
-    im_ref[:, cols] = prod[:, 256:]
-
-    @pl.when(step == pl.num_programs(0) - 1)
-    def _():
-        tiles = NF // 128
-
-        def power(t):
-            lanes = slice(t % tiles * 128, t % tiles * 128 + 128)
-            re, im = re_ref[:, lanes], im_ref[:, lanes]
-            p = re * re + im * im
-            hi = p.astype(BF)
-            return jnp.concatenate([hi, (p - hi.astype(F32)).astype(BF)], axis=0)
-
-        powers = [power(t) for t in range(tiles)]
-        row = lax.broadcasted_iota(jnp.int32, (64, 128), 0)
-        is_re = (row // CH) % 2 == 0
-        lane_seg = lax.broadcasted_iota(jnp.int32, (8, 128), 1) // 16
-        for t in range(tiles):
-            lanes = slice(t * 128, t * 128 + 128)
-            near = jnp.concatenate([powers[t - 1], powers[t], powers[(t + 1) % tiles]], axis=1)
-            both = jnp.dot(near, smooth_ref[t], preferred_element_type=F32)
+def spectra_kernel(got_ref, part_ref, smooth_ref, taper_ref, spread_ref, table_hbm, out_ref,
+                   table_ref, x_ref, half_ref, re_ref, im_ref, power_ref, sem):
+    def arrive(k):
+        return pltpu.make_async_copy(table_hbm.at[k], table_ref.at[k], sem.at[k])
+
+    for k in range(8):
+        arrive(k).start()
+    tags = jnp.transpose(got_ref[:, WIN : WIN + 128].astype(F32))[0:8]
+    wanted = lax.broadcasted_iota(jnp.int32, (8, SLOTS), 0) % CH
+    pick = (tags == wanted.astype(F32)).astype(F32).astype(BF)
+    for s in range(SEGS):
+        seg = got_ref[:, s * NT : (s + 1) * NT]
+        x_ref[s * 8 : s * 8 + 8, :] = jnp.dot(pick, seg, preferred_element_type=F32)
+    for t in range(NT // 256):
+        x = x_ref[:, t * 256 : t * 256 + 256].astype(BF)
+        parted = jnp.dot(x, part_ref[...], preferred_element_type=F32).astype(BF)
+        half_ref[0, :, t * 128 : t * 128 + 128] = parted[:, :128]
+        half_ref[1, :, t * 128 : t * 128 + 128] = parted[:, 128:]
+
+    lane0 = lax.broadcasted_iota(jnp.int32, (64, 128), 1) == 0
+
+    @pl.loop(0, 8)
+    def _(k):
+        arrive(k).wait()
+        even = jnp.dot(half_ref[0], table_ref[k, 0], preferred_element_type=F32)
+        odd = jnp.dot(half_ref[1], table_ref[k, 1], preferred_element_type=F32)
+        ec, es, oc, os = even[:, :128], even[:, 128:], odd[:, :128], odd[:, 128:]
+        middle = lane0 & (k == 0)
+        re = [ec + oc, jnp.where(middle, es, ec - oc)]
+        im = [jnp.where(middle, 0.0, es + os), jnp.where(middle, os, os - es)]
+        for h in range(2):
+            re_ref[h, k] = re[h]
+            im_ref[h, k] = im[h]
+            power = re[h] * re[h] + im[h] * im[h]
+            hi = power.astype(BF)
+            power_ref[h, k, 0:64, :] = hi
+            power_ref[h, k, 64:128, :] = (power - hi.astype(F32)).astype(BF)
+
+    use = smooth_tables()[1]
+    is_re = (lax.broadcasted_iota(jnp.int32, (64, 128), 0) // CH) % 2 == 0
+    lane_seg = lax.broadcasted_iota(jnp.int32, (8, 128), 1) // 16
+    for t in range(8):
+        halves = []
+        for h in range(2):
+            tiles, number = use[h * 8 + t]
+            near = jnp.concatenate([power_ref[k // 8, k % 8] for k in tiles], axis=1)
+            both = jnp.dot(near, smooth_ref[number], preferred_element_type=F32)
             smooth = (both[:64] + both[64:]) * (1.0 / (2 * SMOOTH + 1))
-            scale = taper_ref[:, lanes] * lax.rsqrt(smooth + 1e-06)
-            spec = (jnp.where(is_re, re_ref[:, lanes], im_ref[:, lanes]) * scale).astype(BF)
+            scale = taper_ref[h : h + 1, t * 128 : t * 128 + 128] * lax.rsqrt(smooth + 1e-06)
+            spec = (jnp.where(is_re, re_ref[h, t], im_ref[h, t]) * scale).astype(BF)
             spread = jnp.dot(spec, spread_ref[...], preferred_element_type=F32)
-            groups = []
+            chunks = []
             for u in range(8):
                 chunk = spread[:, u * 128 : u * 128 + 128]
                 acc = chunk[0:8]
                 for s in range(1, SEGS):
                     acc = jnp.where(lane_seg == s, chunk[s * 8 : s * 8 + 8], acc)
-                groups.append(acc)
-            out_ref[t * 64 : t * 64 + 64, :] = jnp.concatenate(groups, axis=0).astype(BF)
-
-
-def spectra_of(pick, got):
-    whole = lambda shape: pl.BlockSpec(shape, lambda i: (0,) * len(shape))
+                chunks.append(acc)
+            halves.append(chunks)
+        for u in range(8):
+            rows = jnp.concatenate([halves[0][u], halves[1][u]], axis=0).astype(BF)
+            out_ref[(t * 8 + u) * 16 : (t * 8 + u) * 16 + 16, :] = rows
+
+
+def spectra_of(got):
+    vmem = pl.BlockSpec(memory_space=pltpu.VMEM)
     return pl.pallas_call(
         spectra_kernel,
-        grid=(8,),
         out_shape=jax.ShapeDtypeStruct((1024, 128), BF),
-        in_specs=[
-            whole((8, SLOTS)),
-            whole((SLOTS, WIN)),
-            whole((16, 384, 128)),
-            whole((1, NF)),
-            whole((128, 1024)),
-            pl.BlockSpec((1, NT, 512), lambda i: (i, 0, 0)),
-        ],
-        out_specs=whole((1024, 128)),
+        in_specs=[vmem] * 5 + [pl.BlockSpec(memory_space=pl.ANY)],
+        out_specs=vmem,
         scratch_shapes=[
+            pltpu.VMEM((8, 2, NT // 2, 256), BF),
             pltpu.VMEM((64, NT), F32),
-            pltpu.VMEM((64, NF), F32),
-            pltpu.VMEM((64, NF), F32),
+            pltpu.VMEM((2, 64, NT // 2), BF),
+            pltpu.VMEM((2, 8, 64, 128), F32),
+            pltpu.VMEM((2, 8, 64, 128), F32),
+            pltpu.VMEM((2, 8, 128, 128), BF),
+            pltpu.SemaphoreType.DMA((8,)),
         ],
         compiler_params=pltpu.CompilerParams(vmem_limit_bytes=40 * 2**20),
-        cost_estimate=pl.CostEstimate(flops=2 * 64 * NT * NT, bytes_accessed=NT * NT * 2, transcendentals=0),
+        cost_estimate=pl.CostEstimate(flops=2**31, bytes_accessed=NT * NT, transcendentals=0),
         name="spectra",
-    )(pick, got, smooth_table(), taper_row(), spread_table(), dft_table())
+    )(got, parting_table(), smooth_tables()[0], taper_rows(), spread_table(), dft_table())
 
 
 CHUNKS = 4
@@ -354,9 +381,7 @@
     tags = jnp.broadcast_to(labels.astype(BF)[:, None], (2 * nrow, 128))
     sent = jnp.concatenate([bundle, tags], axis=1).reshape(nrow, 2, WIN + 128)
     got = lax.all_to_all(sent, "row", 0, 0).reshape(2 * nrow, WIN + 128)
-    wanted = (jnp.arange(8, dtype=jnp.int32) % CH).astype(F32)
-    pick = (got[:, WIN].astype(F32)[None, :] == wanted[:, None]).astype(BF)
-    own = spectra_of(pick, got[:, :WIN])
+    own = spectra_of(got)
     a = lax.all_gather(own, "col", axis=0)
     b, rows = over_row(own, my_row)
     pos = jnp.stack([my_row, my_col, *rows]).astype(jnp.int32)

time: 134 us -> 126 us (0.940)
  blocking collectives: 0 us -> 24.7 us
  starting transfers between devices: 19.2 us -> 5.78 us
  waiting for transfers between devices: 41.8 us -> 30.6 us
  Pallas kernels: 53.2 us -> 46 us
    all_to_all x0 -> x1, blocking collectives: none -> 24.7 us  [local(): got = lax.all_to_all(sent, 'row', 0, 0).reshape(2 * nrow, WIN + 128)]
    all_to_all x1 -> x0, waiting for transfers between devices: 14.2 us -> none  [local(): got = lax.all_to_all(sent, 'row', 0, 0).reshape(2 * nrow, WIN + 128)]
    all_to_all x1 -> x0, starting transfers between devices: 8.49 us -> none  [local(): got = lax.all_to_all(sent, 'row', 0, 0).reshape(2 * nrow, WIN + 128)]
    pallas_call x1, Pallas kernels: 18.5 us -> 11.2 us  [spectra_of(): pl.pallas_call(spectra_kernel, out_shape=jax.ShapeDtypeStruct((1024, 128)...]
    ppermute x7, starting transfers between devices: 10.6 us -> 5.78 us  [move(): return lax.ppermute(block, 'row', pairs)]
    ppermute x7, waiting for transfers between devices: 14.6 us -> 17.9 us  [move(): return lax.ppermute(block, 'row', pairs)]
  transfers between devices with their start and end apart: 9 -> 8, of which waited for: 7 -> 6; matrix products, arithmetic and copies ran while one was open for 0% -> 0% of each run, Pallas kernels for 0% -> 0%
where the time goes in v3:
time: 126 us
  Pallas kernels  46 us (37%)
  waiting for transfers between devices  30.6 us (24%)
  blocking collectives  24.7 us (20%)
  between operations  14.9 us (12%)
  starting transfers between devices  5.78 us (5%)
  local copies, waits for them, and re-layouts  2.19 us (2%)
    pallas_call x1, Pallas kernels, pairs_of(): pl.pallas_call(pair_kernel, out_shape=jax.ShapeDtypeStruct((ncol * CH, nr...  34.8 us
    all_to_all x1, blocking collectives, local(): got = lax.all_to_all(sent, 'row', 0, 0).reshape(2 * nrow, WIN + 128)  24.7 us
    ppermute x7, waiting for transfers between devices, move(): return lax.ppermute(block, 'row', pairs)  17.9 us
    all_gather x1, waiting for transfers between devices, local(): a = lax.all_gather(own, 'col', axis=0)  12.7 us
    pallas_call x1, Pallas kernels, spectra_of(): pl.pallas_call(spectra_kernel, out_shape=jax.ShapeDtypeStruct((1024, 128)...  11.2 us
    ppermute x7, starting transfers between devices, move(): return lax.ppermute(block, 'row', pairs)  5.78 us
  transfers between devices with their start and end apart: 8, of which 6 were waited for; matrix products, arithmetic and copies ran while one was open for 0% of the time, Pallas kernels for 0%

profile of v3, /device:TPU:1, one launch (start us, length us, event | category | flops | bytes accessed | tf_op | source)
XLA Modules:
  0.0 125.7 jit_solution(12289385472932394321)
XLA Ops:
  6.5 0.0 copy-start
  6.5 0.0 all-gather.3.cloned.1.call-start
  7.9 0.7 compare_select_fusion
  8.6 0.2 convert_reduce_fusion
  8.8 0.2 select_reduce_fusion
  9.0 0.0 copy-done
  9.0 0.5 convolution_convert_fusion
  9.5 0.1 broadcast_in_dim.14
  9.6 0.1 pad_maximum_fusion
  9.7 0.4 reshape.67
  10.1 24.7 %all_to_all.5 = bf16[8,2,32896]{2,1,0:T(2,128)(2,1)} all-to-all(bf16[8,2,32896]{2,1,0:T(2,128)(2,1)S(1)} %reshape.67), channel_id=1, replica_groups=mesh['row'=8,'col'=16] {'row'}, dimensions={0} | all-to-all | bytes 2105344 | tf_op jit(solution)/shard_map/all_to_all | solution.py:383
  34.8 0.0 copy-start.1
  34.8 0.0 copy-start.2
  34.8 0.0 copy-start.3
  34.8 0.0 copy-start.4
  34.8 1.6 %reshape.68.got_ref = bf16[16,32896]{1,0:T(8,128)(2,1)S(1)} reshape(bf16[8,2,32896]{2,1,0:T(2,128)(2,1)} %all_to_all.5) | data formatting | bytes 2105344 | tf_op jit(solution)/shard_map/reshape | solution.py:383
  36.4 0.0 copy-done.1
  36.4 0.0 copy-done.2
  36.4 0.0 copy-done.3
  36.4 0.0 copy-done.4
  36.4 11.2 %spectra.1.refs_0_ = bf16[1024,128]{1,0:T(8,128)(2,1)} custom-call(bf16[16,32896]{1,0:T(8,128)(2,1)S(1)} %reshape.68.got_ref, bf16[256,256]{1,0:T(8,128)(2,1)S(1)} %copy-done.3, bf16[5,512,128]{2,1,0:T(8,128)(2,1)S(1)} %copy-done.1, f32[2,1024]{1,0:T(2,128)S(1)} %copy-done.4, bf16[128,1024]{1,0:T(8,128)(2,1)S(1)} %copy-done.2, ...), custom_call_target="tpu_custom_call" | custom-call | flops 2147483648 | bytes 16777216 | tf_op jit(solution)/shard_map/spectra/pallas_call | solution.py:171
  47.6 0.0 all-gather.3.cloned.1.call-update
  47.7 0.6 collective-permute-start
  48.3 0.4 collective-permute-start.1
  48.7 6.6 %collective-permute-done.refs_1_ = bf16[1024,128]{1,0:T(8,128)(2,1)S(1)} collective-permute-done((bf16[1024,128]{1,0:T(8,128)(2,1)}, bf16[1024,128]{1,0:T(8,128)(2,1)S(1)}, u32[]{:S(2)}, u32[]{:S(2)}) %collective-permute-start) | collective-permute-done | bytes 262176 | tf_op jit(solution)/shard_map/ppermute | solution.py:351
  55.3 0.9 collective-permute-start.4
  56.1 0.7 collective-permute-start.2
  56.8 0.8 collective-permute-start.3
  57.6 0.0 collective-permute-done.1.refs_2_
  57.6 0.6 collective-permute-start.5
  58.2 2.5 %collective-permute-done.4.refs_5_ = bf16[1024,128]{1,0:T(8,128)(2,1)S(1)} collective-permute-done((bf16[1024,128]{1,0:T(8,128)(2,1)S(1)}, bf16[1024,128]{1,0:T(8,128)(2,1)S(1)}, u32[]{:S(2)}, u32[]{:S(2)}) %collective-permute-start.4) | collective-permute-done | bytes 262176 | tf_op jit(solution)/shard_map/ppermute | solution.py:351
  60.7 1.8 %collective-permute-start.6 = (bf16[1024,128]{1,0:T(8,128)(2,1)S(1)}, bf16[1024,128]{1,0:T(8,128)(2,1)S(1)}, u32[]{:S(2)}, u32[]{:S(2)}) collective-permute-start(bf16[1024,128]{1,0:T(8,128)(2,1)S(1)} %collective-permute-done.4.refs_5_), channel_id=1, source_target_pairs={{0,48},{16,0},{32,16},{48,32},{64,112},{80,64},{96,80},{112,96},{1... | collective-permute-start | bytes 786440 | tf_op jit(solution)/shard_map/ppermute | solution.py:351
  62.6 0.1 stack.43.pos_ref
  62.7 3.2 %collective-permute-done.2.refs_3_ = bf16[1024,128]{1,0:T(8,128)(2,1)S(1)} collective-permute-done((bf16[1024,128]{1,0:T(8,128)(2,1)}, bf16[1024,128]{1,0:T(8,128)(2,1)S(1)}, u32[]{:S(2)}, u32[]{:S(2)}) %collective-permute-start.2) | collective-permute-done | bytes 262176 | tf_op jit(solution)/shard_map/ppermute | solution.py:351
  65.8 2.3 %collective-permute-done.5.refs_6_ = bf16[1024,128]{1,0:T(8,128)(2,1)S(1)} collective-permute-done((bf16[1024,128]{1,0:T(8,128)(2,1)S(1)}, bf16[1024,128]{1,0:T(8,128)(2,1)S(1)}, u32[]{:S(2)}, u32[]{:S(2)}) %collective-permute-start.5) | collective-permute-done | bytes 262176 | tf_op jit(solution)/shard_map/ppermute | solution.py:351
  68.1 0.0 collective-permute-done.3.refs_4_
  68.1 3.3 %collective-permute-done.6.refs_7_ = bf16[1024,128]{1,0:T(8,128)(2,1)S(1)} collective-permute-done((bf16[1024,128]{1,0:T(8,128)(2,1)S(1)}, bf16[1024,128]{1,0:T(8,128)(2,1)S(1)}, u32[]{:S(2)}, u32[]{:S(2)}) %collective-permute-start.6) | collective-permute-done | bytes 262176 | tf_op jit(solution)/shard_map/ppermute | solution.py:351
  71.5 0.0 copy-start.5
  71.5 12.7 %all-gather.3.cloned.1.call-done = bf16[16384,128]{1,0:T(8,128)(2,1)} async-done(((bf16[1024,128]{1,0:T(8,128)(2,1)}), bf16[16384,128]{1,0:T(8,128)(2,1)}) %all-gather.3.cloned.1.call-update) | async-done | bytes 4194320 | tf_op jit(solution)/shard_map/all_gather | solution.py:385
  84.1 0.0 copy-done.5
  84.1 34.8 %pairs.1 = bf16[64,32,1024]{2,1,0:T(8,128)(2,1)} custom-call(s32[10]{0:T(128)S(1)} %stack.43.pos_ref, bf16[16,1024,128]{2,1,0:T(8,128)(2,1)} %bitcast.17, bf16[1024,128]{1,0:T(8,128)(2,1)} %spectra.1.refs_0_, bf16[1024,128]{1,0:T(8,128)(2,1)S(1)} %collective-permute-done.refs_1_, bf16[1024,128]{1,0:T(8,128)(2,1)S(1)} %collective-permute-done.1.refs_2_, ...), custom_call_target="tpu_custom_call" | custom-call | flops 17179869184 | bytes 16777216 | tf_op jit(solution)/shard_map/pairs/pallas_call | solution.py:325
  (2 shorter events, 0.0 us)
Async XLA Ops:
  6.5 2.5 %copy-start = (bf16[16,33280]{1,0:T(8,128)(2,1)S(1)}, bf16[16,33280]{1,0:T(8,128)(2,1)}, u32[]{:S(2)}) copy-start(bf16[16,33280]{1,0:T(8,128)(2,1)} %param.10) | copy-start | bytes 3194884
  6.5 77.6 %all-gather.3.cloned.1.call-start = ((), (), s32[]{:S(2)}) async-start(), calls=%async_computation.1 | async-start | bytes 4456448 | tf_op jit(solution)/shard_map/all_gather | solution.py:385
  34.8 1.6 %copy-start.1 = (bf16[5,512,128]{2,1,0:T(8,128)(2,1)S(1)}, bf16[5,512,128]{2,1,0:T(8,128)(2,1)}, u32[]{:S(2)}) copy-start(bf16[5,512,128]{2,1,0:T(8,128)(2,1)} %constant.132.clone.smooth_ref) | copy-start | bytes 1966084
  34.8 1.6 %copy-start.2 = (bf16[128,1024]{1,0:T(8,128)(2,1)S(1)}, bf16[128,1024]{1,0:T(8,128)(2,1)}, u32[]{:S(2)}) copy-start(bf16[128,1024]{1,0:T(8,128)(2,1)} %constant.134.clone.spread_ref) | copy-start | bytes 786436
  34.8 1.6 %copy-start.3 = (bf16[256,256]{1,0:T(8,128)(2,1)S(1)}, bf16[256,256]{1,0:T(8,128)(2,1)}, u32[]{:S(2)}) copy-start(bf16[256,256]{1,0:T(8,128)(2,1)} %constant.131.clone.part_ref) | copy-start | bytes 393220
  34.8 1.6 %copy-start.4 = (f32[2,1024]{1,0:T(2,128)S(1)}, f32[2,1024]{1,0:T(2,128)}, u32[]{:S(2)}) copy-start(f32[2,1024]{1,0:T(2,128)} %constant.133.clone.taper_ref) | copy-start | bytes 24580
  47.7 7.6 %collective-permute-start = (bf16[1024,128]{1,0:T(8,128)(2,1)}, bf16[1024,128]{1,0:T(8,128)(2,1)S(1)}, u32[]{:S(2)}, u32[]{:S(2)}) collective-permute-start(bf16[1024,128]{1,0:T(8,128)(2,1)} %spectra.1.refs_0_), channel_id=1, source_target_pairs={{0,64},{16,80},{32,96},{48,112},{64,0},{80,16},{96,32},{112,48},{1... | collective-permute-start | bytes 786440 | tf_op jit(solution)/shard_map/ppermute | solution.py:351
  48.3 9.3 %collective-permute-start.1 = (bf16[1024,128]{1,0:T(8,128)(2,1)}, bf16[1024,128]{1,0:T(8,128)(2,1)S(1)}, u32[]{:S(2)}, u32[]{:S(2)}) collective-permute-start(bf16[1024,128]{1,0:T(8,128)(2,1)} %spectra.1.refs_0_), channel_id=1, source_target_pairs={{0,16},{16,32},{32,48},{48,0},{64,80},{80,96},{96,112},{112,64},{1... | collective-permute-start | bytes 786440 | tf_op jit(solution)/shard_map/ppermute | solution.py:351
  55.3 5.5 %collective-permute-start.4 = (bf16[1024,128]{1,0:T(8,128)(2,1)S(1)}, bf16[1024,128]{1,0:T(8,128)(2,1)S(1)}, u32[]{:S(2)}, u32[]{:S(2)}) collective-permute-start(bf16[1024,128]{1,0:T(8,128)(2,1)S(1)} %collective-permute-done.refs_1_), channel_id=1, source_target_pairs={{0,48},{16,0},{32,16},{48,32},{64,112},{80,64},{96,80},{112,96},{1... | collective-permute-start | bytes 786440 | tf_op jit(solution)/shard_map/ppermute | solution.py:351
  56.1 9.7 %collective-permute-start.2 = (bf16[1024,128]{1,0:T(8,128)(2,1)}, bf16[1024,128]{1,0:T(8,128)(2,1)S(1)}, u32[]{:S(2)}, u32[]{:S(2)}) collective-permute-start(bf16[1024,128]{1,0:T(8,128)(2,1)} %spectra.1.refs_0_), channel_id=1, source_target_pairs={{0,48},{16,0},{32,16},{48,32},{64,112},{80,64},{96,80},{112,96},{1... | collective-permute-start | bytes 786440 | tf_op jit(solution)/shard_map/ppermute | solution.py:351
  56.8 11.3 %collective-permute-start.3 = (bf16[1024,128]{1,0:T(8,128)(2,1)S(1)}, bf16[1024,128]{1,0:T(8,128)(2,1)S(1)}, u32[]{:S(2)}, u32[]{:S(2)}) collective-permute-start(bf16[1024,128]{1,0:T(8,128)(2,1)S(1)} %collective-permute-done.refs_1_), channel_id=1, source_target_pairs={{0,16},{16,32},{32,48},{48,0},{64,80},{80,96},{96,112},{112,64},{1... | collective-permute-start | bytes 786440 | tf_op jit(solution)/shard_map/ppermute | solution.py:351
  57.6 10.5 %collective-permute-start.5 = (bf16[1024,128]{1,0:T(8,128)(2,1)S(1)}, bf16[1024,128]{1,0:T(8,128)(2,1)S(1)}, u32[]{:S(2)}, u32[]{:S(2)}) collective-permute-start(bf16[1024,128]{1,0:T(8,128)(2,1)S(1)} %collective-permute-done.1.refs_2_), channel_id=1, source_target_pairs={{0,16},{16,32},{32,48},{48,0},{64,80},{80,96},{96,112},{112,64},{1... | collective-permute-start | bytes 786440 | tf_op jit(solution)/shard_map/ppermute | solution.py:351
  60.7 10.7 %collective-permute-start.6 = (bf16[1024,128]{1,0:T(8,128)(2,1)S(1)}, bf16[1024,128]{1,0:T(8,128)(2,1)S(1)}, u32[]{:S(2)}, u32[]{:S(2)}) collective-permute-start(bf16[1024,128]{1,0:T(8,128)(2,1)S(1)} %collective-permute-done.4.refs_5_), channel_id=1, source_target_pairs={{0,48},{16,0},{32,16},{48,32},{64,112},{80,64},{96,80},{112,96},{1... | collective-permute-start | bytes 786440 | tf_op jit(solution)/shard_map/ppermute | solution.py:351
  71.5 12.7 %copy-start.5 = (bf16[1024,128]{1,0:T(8,128)(2,1)}, bf16[1024,128]{1,0:T(8,128)(2,1)S(1)}, u32[]{:S(2)}) copy-start(bf16[1024,128]{1,0:T(8,128)(2,1)S(1)} %collective-permute-done.6.refs_7_) | copy-start | bytes 786436
Sparse Core Ops, SparseCore 0:
  47.8 36.2 all-gather.2

commit v4 on v3

--- a/solution.py
+++ b/solution.py
@@ -89,17 +89,26 @@
     return out.reshape(128, 1024).astype(jnp.bfloat16)
 
 
+LAG_ROWS = 272
+
+
 @functools.cache
 def lag_tables():
     p = np.arange(HALF, dtype=np.int64)
-    out = np.zeros((4, LAGS // 2, HALF), np.float32)
+    out = np.zeros((4, LAG_ROWS, HALF), np.float32)
     for odd in range(2):
-        m = np.arange(odd, LAGS, 2, dtype=np.int64) - LAGS // 2
+        m = np.arange(odd, LAGS // 2 + 1, 2, dtype=np.int64)
         cos, sin = trig(m[:, None] * p[None, :], NT)
-        mid_cos, mid_sin = trig(m * HALF, NT)
-        out[2 * odd], out[2 * odd + 1] = cos, sin
-        out[2 * odd + 1, :, 0] = np.rint(mid_sin if odd else mid_cos)
+        out[2 * odd, : len(m)], out[2 * odd + 1, : len(m)] = cos, sin
+        if odd:
+            out[3, : len(m), 0] = np.rint(trig(m * HALF, NT)[1])
     return out.astype(jnp.bfloat16)
+
+
+@functools.cache
+def turning_tables():
+    r = np.arange(256)
+    return np.stack([(r[:, None] + r[None, :] == n) for n in (256, 255)]).astype(jnp.bfloat16)
 
 
 def spectra_kernel(got_ref, part_ref, smooth_ref, taper_ref, spread_ref, table_hbm, out_ref,
@@ -194,7 +203,7 @@
 def pair_kernel(pos_ref, a_hbm, *refs):
     nrow, ncol = 8, 16
     b_hbm = refs[:nrow]
-    lag_hbm, out_hbm, a_ref, b_ref, lag_ref, x_ref, y_ref, f_ref, o_ref, in_sem, lag_sem, out_sem = refs[nrow:]
+    lag_hbm, turn_ref, out_hbm, a_ref, b_ref, lag_ref, x_ref, y_ref, f_ref, o_ref, in_sem, lag_sem, out_sem = refs[nrow:]
     size = 1024 // CHUNKS
 
     def arrive(k):
@@ -247,8 +256,9 @@
         for jp in range(pairs):
             parts = []
             for h in range(2):
-                t0 = prods[h][jp * 16 : jp * 16 + 16]
-                t1 = prods[h][(jp + pairs) * 16 : (jp + pairs) * 16 + 16]
+                j = jp // 8 * 16 + jp % 8
+                t0 = prods[h][j * 16 : j * 16 + 16]
+                t1 = prods[h][(j + 8) * 16 : (j + 8) * 16 + 16]
                 re = jnp.where(first, t0, pltpu.roll(t1, 4, 1))
                 im = jnp.where(first, pltpu.roll(t0, 124, 1), t1)
                 parts += [re, im]
@@ -270,52 +280,62 @@
         for copy in arrive(k):
             copy.wait()
 
-        @pl.loop(0, NGRP // CHUNKS, step=4)
-        def _(g):
-            for u in range(4):
-                group(k * (NGRP // CHUNKS) + g + u, False)
+        for u in range(NGRP // CHUNKS):
+            group(k * (NGRP // CHUNKS) + u, False)
 
     group(0, True)
     lag_copy.wait()
 
-    @pl.loop(0, 8)
-    def _(n):
-        cols = pl.ds(pl.multiple_of(n * 256, 256), 256)
-        for odd in range(2):
-            y = jnp.dot(lag_ref[2 * odd], x_ref[2 * odd, :, cols], preferred_element_type=F32)
-            y += jnp.dot(lag_ref[2 * odd + 1], x_ref[2 * odd + 1, :, cols], preferred_element_type=F32)
-            y_ref[0, pl.ds(odd, LAGS // 2, stride=2), :] = y[:, :128]
-            y_ref[1, pl.ds(odd, LAGS // 2, stride=2), :] = y[:, 128:]
-        for k in range(2):
-            at = pl.ds((n * 2 + k) * 129, 128)
-            for t in range(LAGS // 128):
-                f_ref[t, at, :] = jnp.transpose(y_ref[k, t * 128 : t * 128 + 128, :])
-
     my_row, my_col = pos_ref[0], pos_ref[1]
     line = lax.broadcasted_iota(jnp.int32, (16, 128), 0)
-
-    def leave(d):
+    place = lax.broadcasted_iota(jnp.int32, (LAG_ROWS, 1), 0)
+    alternate = jnp.where(place % 2 == 0, 1.0, -1.0)
+
+    def leave(half, d):
+        lines = pl.ds(half * 16, 16)
         return pltpu.make_async_copy(
-            o_ref.at[d % 2], out_hbm.at[pl.ds(d * CH, CH), :, :], out_sem.at[d % 2])
-
-    @pl.loop(0, ncol)
-    def _(d):
-        @pl.when(d >= 2)
-        def _():
-            leave(d - 2).wait()
-
-        for c in range(CH):
-            own = jnp.where(d == my_col, my_row * CH + c, -1)
-            for e in range(2):
-                drop = line + e * 16 == own
+            o_ref.at[pl.ds(d * CH, CH), lines, :], out_hbm.at[pl.ds(d * CH, CH), lines, :], out_sem.at[half, d])
+
+    for half in range(2):
+
+        @pl.loop(0, 4, unroll=4)
+        def _(n):
+            cols = pl.ds(pl.multiple_of(half * 1024 + n * 256, 256), 256)
+            for odd in range(2):
+                size = 256 if odd else LAG_ROWS
+                cos = jnp.dot(lag_ref[2 * odd, :size], x_ref[2 * odd, :, cols], preferred_element_type=F32)
+                sin = jnp.dot(lag_ref[2 * odd + 1, :size], x_ref[2 * odd + 1, :, cols], preferred_element_type=F32)
+                if not odd:
+                    cos += alternate * x_ref[1, 0:16, cols].astype(F32)[0:1]
+                later = (cos + sin)[:256]
+                sooner = cos - sin
+                turned = jnp.dot(turn_ref[odd], sooner[:256].astype(BF), preferred_element_type=F32)
+                for k in range(2):
+                    half_cols = slice(k * 128, k * 128 + 128)
+                    y_ref[k, pl.ds(odd, 256, stride=2), :] = turned[:, half_cols]
+                    y_ref[k, pl.ds(LAGS // 2 + odd, 256, stride=2), :] = later[:, half_cols]
+                    if not odd:
+                        y_ref[k, 0:1, :] = sooner[256:257, half_cols]
+            for k in range(2):
+                at = pl.ds((n * 2 + k) * 129, 128)
                 for t in range(LAGS // 128):
-                    v = f_ref[t, pl.ds(d * 8 + e * 4 + c, 16, stride=129), :]
+                    f_ref[t, at, :] = jnp.transpose(y_ref[k, t * 128 : t * 128 + 128, :])
+
+        @pl.loop(0, ncol)
+        def _(d):
+            for c in range(CH):
+                own = jnp.where(d == my_col, my_row * CH + c, -1)
+                drop = line + half * 16 == own
+                for t in range(LAGS // 128):
+                    v = jnp.concatenate(
+                        [f_ref[t, pl.ds(d * 8 + e * 4 + c, 8, stride=129), :] for e in range(2)], axis=0)
                     v = jnp.where(drop, 0.0, v * (1.0 / math.sqrt(SEGS * NF)))
-                    o_ref[d % 2, c, e * 16 : e * 16 + 16, t * 128 : t * 128 + 128] = v.astype(BF)
-        leave(d).start()
-
-    leave(ncol - 2).wait()
-    leave(ncol - 1).wait()
+                    o_ref[d * CH + c, half * 16 : half * 16 + 16, t * 128 : t * 128 + 128] = v.astype(BF)
+            leave(half, d).start()
+
+    for half in range(2):
+        for d in range(ncol):
+            leave(half, d).wait()
 
 
 def pairs_of(pos, a, b):
@@ -325,24 +345,25 @@
     return pl.pallas_call(
         pair_kernel,
         out_shape=jax.ShapeDtypeStruct((ncol * CH, nrow * CH, LAGS), BF),
-        in_specs=[pl.BlockSpec(memory_space=pltpu.SMEM)] + [anywhere] * (nrow + 2),
+        in_specs=[pl.BlockSpec(memory_space=pltpu.SMEM)] + [anywhere] * (nrow + 2)
+        + [pl.BlockSpec(memory_space=pltpu.VMEM)],
         out_specs=anywhere,
         scratch_shapes=[
             pltpu.VMEM((ncol, 1024, 128), BF),
             pltpu.VMEM((nrow, 1024, 128), BF),
-            pltpu.VMEM((4, LAGS // 2, HALF), BF),
+            pltpu.VMEM((4, LAG_ROWS, HALF), BF),
             pltpu.VMEM((4, HALF, 2048), BF),
             pltpu.VMEM((2, LAGS, 128), F32),
-            pltpu.VMEM((LAGS // 128, 16 * 129 + 8, 128), F32),
-            pltpu.VMEM((2, CH, nrow * CH, LAGS), BF),
+            pltpu.VMEM((LAGS // 128, 8 * 129 + 8, 128), F32),
+            pltpu.VMEM((ncol * CH, nrow * CH, LAGS), BF),
             pltpu.SemaphoreType.DMA((CHUNKS, nrow + 1)),
             pltpu.SemaphoreType.DMA,
-            pltpu.SemaphoreType.DMA((2,)),
+            pltpu.SemaphoreType.DMA((2, ncol)),
         ],
         compiler_params=pltpu.CompilerParams(vmem_limit_bytes=52 * 2**20),
         cost_estimate=pl.CostEstimate(flops=2**34, bytes_accessed=16 * 2**20, transcendentals=0),
         name="pairs",
-    )(pos, a, *b, lag_tables())
+    )(pos, a, *b, lag_tables(), turning_tables())
 
 
 def over_row(own, my_row):

time: 126 us -> 116 us (0.921)
  Pallas kernels: 46 us -> 35.7 us
    pallas_call x1, Pallas kernels: 34.8 us -> 24.5 us  [pairs_of(): pl.pallas_call(pair_kernel, out_shape=jax.ShapeDtypeStruct((ncol * CH, nr...]
where the time goes in v4:
time: 116 us; the launch traced here: 115 us
  Pallas kernels  35.7 us (31%)
  waiting for transfers between devices  30.6 us (26%)
  blocking collectives  24.7 us (21%)
  between operations  14.9 us (13%)
  starting transfers between devices  5.77 us (5%)
  local copies, waits for them, and re-layouts  2.19 us (2%)
    all_to_all x1, blocking collectives, local(): got = lax.all_to_all(sent, 'row', 0, 0).reshape(2 * nrow, WIN + 128)  24.7 us
    pallas_call x1, Pallas kernels, pairs_of(): pl.pallas_call(pair_kernel, out_shape=jax.ShapeDtypeStruct((ncol * CH, nr...  24.5 us
    ppermute x7, waiting for transfers between devices, move(): return lax.ppermute(block, 'row', pairs)  17.9 us
    all_gather x1, waiting for transfers between devices, local(): a = lax.all_gather(own, 'col', axis=0)  12.7 us
    pallas_call x1, Pallas kernels, spectra_of(): pl.pallas_call(spectra_kernel, out_shape=jax.ShapeDtypeStruct((1024, 128)...  11.2 us
    ppermute x7, starting transfers between devices, move(): return lax.ppermute(block, 'row', pairs)  5.77 us
  transfers between devices with their start and end apart: 8, of which 6 were waited for; matrix products, arithmetic and copies ran while one was open for 0% of the time, Pallas kernels for 0%

profile of v4, /device:TPU:1, one launch (start us, length us, event | category | flops | bytes accessed | tf_op | source)
XLA Modules:
  0.0 115.5 jit_solution(11260821042768931854)
XLA Ops:
  6.5 0.0 copy-start
  6.5 0.0 all-gather.3.cloned.1.call-start
  7.9 0.7 compare_select_fusion
  8.6 0.2 convert_reduce_fusion
  8.8 0.2 select_reduce_fusion
  9.0 0.0 copy-done
  9.0 0.5 convolution_convert_fusion
  9.5 0.1 broadcast_in_dim.14
  9.6 0.1 pad_maximum_fusion
  9.7 0.4 reshape.67
  10.1 24.7 %all_to_all.5 = bf16[8,2,32896]{2,1,0:T(2,128)(2,1)} all-to-all(bf16[8,2,32896]{2,1,0:T(2,128)(2,1)S(1)} %reshape.67), channel_id=1, replica_groups=mesh['row'=8,'col'=16] {'row'}, dimensions={0} | all-to-all | bytes 2105344 | tf_op jit(solution)/shard_map/all_to_all | solution.py:404
  34.8 0.0 copy-start.1
  34.8 0.0 copy-start.2
  34.8 0.0 copy-start.3
  34.8 0.0 copy-start.4
  34.8 1.6 %reshape.68.got_ref = bf16[16,32896]{1,0:T(8,128)(2,1)S(1)} reshape(bf16[8,2,32896]{2,1,0:T(2,128)(2,1)} %all_to_all.5) | data formatting | bytes 2105344 | tf_op jit(solution)/shard_map/reshape | solution.py:404
  36.4 0.0 copy-done.1
  36.4 0.0 copy-done.2
  36.4 0.0 copy-done.3
  36.4 0.0 copy-done.4
  36.4 11.2 %spectra.1.refs_0_ = bf16[1024,128]{1,0:T(8,128)(2,1)} custom-call(bf16[16,32896]{1,0:T(8,128)(2,1)S(1)} %reshape.68.got_ref, bf16[256,256]{1,0:T(8,128)(2,1)S(1)} %copy-done.3, bf16[5,512,128]{2,1,0:T(8,128)(2,1)S(1)} %copy-done.1, f32[2,1024]{1,0:T(2,128)S(1)} %copy-done.4, bf16[128,1024]{1,0:T(8,128)(2,1)S(1)} %copy-done.2, ...), custom_call_target="tpu_custom_call" | custom-call | flops 2147483648 | bytes 16777216 | tf_op jit(solution)/shard_map/spectra/pallas_call | solution.py:180
  47.6 0.0 all-gather.3.cloned.1.call-update
  47.7 0.6 collective-permute-start
  48.3 0.4 collective-permute-start.1
  48.7 6.6 %collective-permute-done.refs_1_ = bf16[1024,128]{1,0:T(8,128)(2,1)S(1)} collective-permute-done((bf16[1024,128]{1,0:T(8,128)(2,1)}, bf16[1024,128]{1,0:T(8,128)(2,1)S(1)}, u32[]{:S(2)}, u32[]{:S(2)}) %collective-permute-start) | collective-permute-done | bytes 262176 | tf_op jit(solution)/shard_map/ppermute | solution.py:372
  55.2 0.9 collective-permute-start.4
  56.1 0.7 collective-permute-start.2
  56.8 0.8 collective-permute-start.3
  57.6 0.0 collective-permute-done.1.refs_2_
  57.6 0.6 collective-permute-start.5
  58.2 2.6 %collective-permute-done.4.refs_5_ = bf16[1024,128]{1,0:T(8,128)(2,1)S(1)} collective-permute-done((bf16[1024,128]{1,0:T(8,128)(2,1)S(1)}, bf16[1024,128]{1,0:T(8,128)(2,1)S(1)}, u32[]{:S(2)}, u32[]{:S(2)}) %collective-permute-start.4) | collective-permute-done | bytes 262176 | tf_op jit(solution)/shard_map/ppermute | solution.py:372
  60.7 1.8 %collective-permute-start.6 = (bf16[1024,128]{1,0:T(8,128)(2,1)S(1)}, bf16[1024,128]{1,0:T(8,128)(2,1)S(1)}, u32[]{:S(2)}, u32[]{:S(2)}) collective-permute-start(bf16[1024,128]{1,0:T(8,128)(2,1)S(1)} %collective-permute-done.4.refs_5_), channel_id=1, source_target_pairs={{0,48},{16,0},{32,16},{48,32},{64,112},{80,64},{96,80},{112,96},{1... | collective-permute-start | bytes 786440 | tf_op jit(solution)/shard_map/ppermute | solution.py:372
  62.6 0.1 stack.43.pos_ref
  62.6 3.2 %collective-permute-done.2.refs_3_ = bf16[1024,128]{1,0:T(8,128)(2,1)S(1)} collective-permute-done((bf16[1024,128]{1,0:T(8,128)(2,1)}, bf16[1024,128]{1,0:T(8,128)(2,1)S(1)}, u32[]{:S(2)}, u32[]{:S(2)}) %collective-permute-start.2) | collective-permute-done | bytes 262176 | tf_op jit(solution)/shard_map/ppermute | solution.py:372
  65.8 2.3 %collective-permute-done.5.refs_6_ = bf16[1024,128]{1,0:T(8,128)(2,1)S(1)} collective-permute-done((bf16[1024,128]{1,0:T(8,128)(2,1)S(1)}, bf16[1024,128]{1,0:T(8,128)(2,1)S(1)}, u32[]{:S(2)}, u32[]{:S(2)}) %collective-permute-start.5) | collective-permute-done | bytes 262176 | tf_op jit(solution)/shard_map/ppermute | solution.py:372
  68.1 0.0 collective-permute-done.3.refs_4_
  68.1 3.3 %collective-permute-done.6.refs_7_ = bf16[1024,128]{1,0:T(8,128)(2,1)S(1)} collective-permute-done((bf16[1024,128]{1,0:T(8,128)(2,1)S(1)}, bf16[1024,128]{1,0:T(8,128)(2,1)S(1)}, u32[]{:S(2)}, u32[]{:S(2)}) %collective-permute-start.6) | collective-permute-done | bytes 262176 | tf_op jit(solution)/shard_map/ppermute | solution.py:372
  71.4 0.0 copy-start.5
  71.4 12.7 %all-gather.3.cloned.1.call-done = bf16[16384,128]{1,0:T(8,128)(2,1)} async-done(((bf16[1024,128]{1,0:T(8,128)(2,1)}), bf16[16384,128]{1,0:T(8,128)(2,1)}) %all-gather.3.cloned.1.call-update) | async-done | bytes 4194320 | tf_op jit(solution)/shard_map/all_gather | solution.py:406
  84.1 0.0 copy-done.5
  84.1 24.5 %pairs.1 = bf16[64,32,1024]{2,1,0:T(8,128)(2,1)} custom-call(s32[10]{0:T(128)S(1)} %stack.43.pos_ref, bf16[16,1024,128]{2,1,0:T(8,128)(2,1)} %bitcast.17, bf16[1024,128]{1,0:T(8,128)(2,1)} %spectra.1.refs_0_, bf16[1024,128]{1,0:T(8,128)(2,1)S(1)} %collective-permute-done.refs_1_, bf16[1024,128]{1,0:T(8,128)(2,1)S(1)} %collective-permute-done.1.refs_2_, ...), custom_call_target="tpu_custom_call" | custom-call | flops 17179869184 | bytes 16777216 | tf_op jit(solution)/shard_map/pairs/pallas_call | solution.py:345
  (2 shorter events, 0.0 us)
Async XLA Ops:
  6.5 2.5 %copy-start = (bf16[16,33280]{1,0:T(8,128)(2,1)S(1)}, bf16[16,33280]{1,0:T(8,128)(2,1)}, u32[]{:S(2)}) copy-start(bf16[16,33280]{1,0:T(8,128)(2,1)} %param.11) | copy-start | bytes 3194884
  6.5 77.6 %all-gather.3.cloned.1.call-start = ((), (), s32[]{:S(2)}) async-start(), calls=%async_computation.1 | async-start | bytes 4456448 | tf_op jit(solution)/shard_map/all_gather | solution.py:406
  34.8 1.6 %copy-start.1 = (bf16[5,512,128]{2,1,0:T(8,128)(2,1)S(1)}, bf16[5,512,128]{2,1,0:T(8,128)(2,1)}, u32[]{:S(2)}) copy-start(bf16[5,512,128]{2,1,0:T(8,128)(2,1)} %constant.134.clone.smooth_ref) | copy-start | bytes 1966084
  34.8 1.6 %copy-start.2 = (bf16[128,1024]{1,0:T(8,128)(2,1)S(1)}, bf16[128,1024]{1,0:T(8,128)(2,1)}, u32[]{:S(2)}) copy-start(bf16[128,1024]{1,0:T(8,128)(2,1)} %constant.136.clone.spread_ref) | copy-start | bytes 786436
  34.8 1.6 %copy-start.3 = (bf16[256,256]{1,0:T(8,128)(2,1)S(1)}, bf16[256,256]{1,0:T(8,128)(2,1)}, u32[]{:S(2)}) copy-start(bf16[256,256]{1,0:T(8,128)(2,1)} %constant.133.clone.part_ref) | copy-start | bytes 393220
  34.8 1.6 %copy-start.4 = (f32[2,1024]{1,0:T(2,128)S(1)}, f32[2,1024]{1,0:T(2,128)}, u32[]{:S(2)}) copy-start(f32[2,1024]{1,0:T(2,128)} %constant.135.clone.taper_ref) | copy-start | bytes 24580
  47.7 7.6 %collective-permute-start = (bf16[1024,128]{1,0:T(8,128)(2,1)}, bf16[1024,128]{1,0:T(8,128)(2,1)S(1)}, u32[]{:S(2)}, u32[]{:S(2)}) collective-permute-start(bf16[1024,128]{1,0:T(8,128)(2,1)} %spectra.1.refs_0_), channel_id=1, source_target_pairs={{0,64},{16,80},{32,96},{48,112},{64,0},{80,16},{96,32},{112,48},{1... | collective-permute-start | bytes 786440 | tf_op jit(solution)/shard_map/ppermute | solution.py:372
  48.3 9.3 %collective-permute-start.1 = (bf16[1024,128]{1,0:T(8,128)(2,1)}, bf16[1024,128]{1,0:T(8,128)(2,1)S(1)}, u32[]{:S(2)}, u32[]{:S(2)}) collective-permute-start(bf16[1024,128]{1,0:T(8,128)(2,1)} %spectra.1.refs_0_), channel_id=1, source_target_pairs={{0,16},{16,32},{32,48},{48,0},{64,80},{80,96},{96,112},{112,64},{1... | collective-permute-start | bytes 786440 | tf_op jit(solution)/shard_map/ppermute | solution.py:372
  55.2 5.5 %collective-permute-start.4 = (bf16[1024,128]{1,0:T(8,128)(2,1)S(1)}, bf16[1024,128]{1,0:T(8,128)(2,1)S(1)}, u32[]{:S(2)}, u32[]{:S(2)}) collective-permute-start(bf16[1024,128]{1,0:T(8,128)(2,1)S(1)} %collective-permute-done.refs_1_), channel_id=1, source_target_pairs={{0,48},{16,0},{32,16},{48,32},{64,112},{80,64},{96,80},{112,96},{1... | collective-permute-start | bytes 786440 | tf_op jit(solution)/shard_map/ppermute | solution.py:372
  56.1 9.7 %collective-permute-start.2 = (bf16[1024,128]{1,0:T(8,128)(2,1)}, bf16[1024,128]{1,0:T(8,128)(2,1)S(1)}, u32[]{:S(2)}, u32[]{:S(2)}) collective-permute-start(bf16[1024,128]{1,0:T(8,128)(2,1)} %spectra.1.refs_0_), channel_id=1, source_target_pairs={{0,48},{16,0},{32,16},{48,32},{64,112},{80,64},{96,80},{112,96},{1... | collective-permute-start | bytes 786440 | tf_op jit(solution)/shard_map/ppermute | solution.py:372
  56.8 11.3 %collective-permute-start.3 = (bf16[1024,128]{1,0:T(8,128)(2,1)S(1)}, bf16[1024,128]{1,0:T(8,128)(2,1)S(1)}, u32[]{:S(2)}, u32[]{:S(2)}) collective-permute-start(bf16[1024,128]{1,0:T(8,128)(2,1)S(1)} %collective-permute-done.refs_1_), channel_id=1, source_target_pairs={{0,16},{16,32},{32,48},{48,0},{64,80},{80,96},{96,112},{112,64},{1... | collective-permute-start | bytes 786440 | tf_op jit(solution)/shard_map/ppermute | solution.py:372
  57.6 10.5 %collective-permute-start.5 = (bf16[1024,128]{1,0:T(8,128)(2,1)S(1)}, bf16[1024,128]{1,0:T(8,128)(2,1)S(1)}, u32[]{:S(2)}, u32[]{:S(2)}) collective-permute-start(bf16[1024,128]{1,0:T(8,128)(2,1)S(1)} %collective-permute-done.1.refs_2_), channel_id=1, source_target_pairs={{0,16},{16,32},{32,48},{48,0},{64,80},{80,96},{96,112},{112,64},{1... | collective-permute-start | bytes 786440 | tf_op jit(solution)/shard_map/ppermute | solution.py:372
  60.7 10.7 %collective-permute-start.6 = (bf16[1024,128]{1,0:T(8,128)(2,1)S(1)}, bf16[1024,128]{1,0:T(8,128)(2,1)S(1)}, u32[]{:S(2)}, u32[]{:S(2)}) collective-permute-start(bf16[1024,128]{1,0:T(8,128)(2,1)S(1)} %collective-permute-done.4.refs_5_), channel_id=1, source_target_pairs={{0,48},{16,0},{32,16},{48,32},{64,112},{80,64},{96,80},{112,96},{1... | collective-permute-start | bytes 786440 | tf_op jit(solution)/shard_map/ppermute | solution.py:372
  71.4 12.7 %copy-start.5 = (bf16[1024,128]{1,0:T(8,128)(2,1)}, bf16[1024,128]{1,0:T(8,128)(2,1)S(1)}, u32[]{:S(2)}) copy-start(bf16[1024,128]{1,0:T(8,128)(2,1)S(1)} %collective-permute-done.6.refs_7_) | copy-start | bytes 786436
Sparse Core Ops, SparseCore 0:
  47.8 36.2 all-gather.2

commit v5 on v4

--- a/solution.py
+++ b/solution.py
@@ -19,12 +19,23 @@
 EDGE = 128
 WIN = SEGS * NT
 HALF = NF // 2
+QUARTER = NF // 4
 GRP = 16
 NGRP = HALF // GRP
 BF = jnp.bfloat16
 F32 = jnp.float32
 
 
+def band_places():
+    p = np.arange(QUARTER, dtype=np.int64)
+    return np.concatenate([p, np.where(p == 0, QUARTER, HALF - p)])
+
+
+def band_mirrors():
+    f = band_places()
+    return np.where(f == 0, HALF, NF - f)
+
+
 def trig(product, size):
     angle = (product % size).astype(np.float32) * np.float32(2.0 * math.pi / size)
     return np.cos(angle.astype(np.float64)), -np.sin(angle.astype(np.float64))
@@ -32,50 +43,47 @@
 
 @functools.cache
 def dft_table():
-    p = np.arange(HALF, dtype=np.int64)
+    p = np.arange(QUARTER, dtype=np.int64)
     parts = []
-    for odd in range(2):
-        n = np.arange(odd, NT, 2, dtype=np.int64)
+    for c in range(4):
+        n = np.arange(c, NT, 4, dtype=np.int64)
         cos, sin = trig(n[:, None] * p[None, :], NT)
-        mid_cos, mid_sin = trig(n * HALF, NT)
-        sin[:, 0] = np.rint(mid_sin if odd else mid_cos)
-        both = np.stack([cos.reshape(NT // 2, 8, 128), sin.reshape(NT // 2, 8, 128)], axis=2)
-        parts.append(both.transpose(1, 0, 2, 3).reshape(8, NT // 2, 256))
+        sin[:, 0] = np.where(np.arange(NT // 4) % 2 == 0, 1.0, -1.0) * (math.sqrt(0.5) if c % 2 else 1.0)
+        both = np.stack([cos.reshape(NT // 4, 4, 128), sin.reshape(NT // 4, 4, 128)], axis=2)
+        parts.append(both.transpose(1, 0, 2, 3).reshape(4, NT // 4, 256))
     return np.stack(parts, axis=1).astype(jnp.bfloat16)
 
 
 @functools.cache
 def parting_table():
-    lane = np.arange(256)
-    return (lane[:, None] == (lane % 128 * 2 + lane // 128)[None, :]).astype(jnp.bfloat16)
+    lane = np.arange(512)
+    return (lane[:, None] == (lane % 128 * 4 + lane // 128)[None, :]).astype(jnp.bfloat16)
 
 
 @functools.cache
 def smooth_tables():
-    p = np.arange(HALF)
-    order = np.concatenate([p, np.where(p == 0, HALF, NF - p)]).reshape(16, 128)
+    order = np.concatenate([band_places(), band_mirrors()]).reshape(16, 128)
     tables, use, count = [], [], 0
     for t in range(16):
         near = [np.abs(order[s][:, None] - order[t][None, :]) <= SMOOTH for s in range(16)]
         tiles = [s for s in range(16) if near[s].any()]
-        table = np.zeros((4, 128, 128), np.float32)
+        table = np.zeros((6, 128, 128), np.float32)
         for k, s in enumerate(tiles):
             table[k] = near[s]
         count += table.sum()
-        tiles += [t] * (4 - len(tiles))
+        tiles += [t] * (len(tiles) % 2)
         same = [k for k, other in enumerate(tables) if (other == table).all()]
         if not same:
             tables.append(table)
         use.append((tiles, same[0] if same else len(tables) - 1))
     f = np.arange(NF)
     assert count == (np.minimum(f + SMOOTH, NF - 1) - np.maximum(f - SMOOTH, 0) + 1).sum()
-    return np.stack(tables).reshape(len(tables), 512, 128).astype(jnp.bfloat16), tuple(use)
+    return np.stack(tables).reshape(len(tables), 768, 128).astype(jnp.bfloat16), tuple(use)
 
 
 @functools.cache
 def taper_rows():
-    p = np.arange(HALF)
-    f = np.stack([p, np.where(p == 0, HALF, NF - p)]).astype(np.float64)
+    f = np.stack([band_places(), band_mirrors()]).astype(np.float64)
     rising = np.minimum(np.minimum(f + 0.5, NF - f - 0.5) / EDGE, 1.0)
     return (np.sin(0.5 * math.pi * rising) ** 2).astype(np.float32)
 
@@ -94,7 +102,7 @@
 
 @functools.cache
 def lag_tables():
-    p = np.arange(HALF, dtype=np.int64)
+    p = band_places()
     out = np.zeros((4, LAG_ROWS, HALF), np.float32)
     for odd in range(2):
         m = np.arange(odd, LAGS // 2 + 1, 2, dtype=np.int64)
@@ -111,44 +119,58 @@
     return np.stack([(r[:, None] + r[None, :] == n) for n in (256, 255)]).astype(jnp.bfloat16)
 
 
-def spectra_kernel(got_ref, part_ref, smooth_ref, taper_ref, spread_ref, table_hbm, out_ref,
-                   table_ref, x_ref, half_ref, re_ref, im_ref, power_ref, sem):
+def spectra_kernel(got_ref, part_hbm, smooth_hbm, taper_hbm, spread_hbm, table_hbm, out_ref,
+                   part_ref, smooth_ref, taper_ref, spread_ref, table_ref,
+                   x_ref, class_ref, re_ref, im_ref, power_ref, sem, more_sem):
     def arrive(k):
         return pltpu.make_async_copy(table_hbm.at[k], table_ref.at[k], sem.at[k])
 
-    for k in range(8):
+    whole = [(part_hbm, part_ref), (smooth_hbm, smooth_ref), (taper_hbm, taper_ref), (spread_hbm, spread_ref)]
+    whole = [pltpu.make_async_copy(a, b, more_sem.at[n]) for n, (a, b) in enumerate(whole)]
+    whole[0].start()
+    for k in range(4):
         arrive(k).start()
+    for copy in whole[1:]:
+        copy.start()
     tags = jnp.transpose(got_ref[:, WIN : WIN + 128].astype(F32))[0:8]
     wanted = lax.broadcasted_iota(jnp.int32, (8, SLOTS), 0) % CH
     pick = (tags == wanted.astype(F32)).astype(F32).astype(BF)
     for s in range(SEGS):
         seg = got_ref[:, s * NT : (s + 1) * NT]
         x_ref[s * 8 : s * 8 + 8, :] = jnp.dot(pick, seg, preferred_element_type=F32)
-    for t in range(NT // 256):
-        x = x_ref[:, t * 256 : t * 256 + 256].astype(BF)
+    whole[0].wait()
+    for t in range(NT // 512):
+        x = x_ref[:, t * 512 : t * 512 + 512].astype(BF)
         parted = jnp.dot(x, part_ref[...], preferred_element_type=F32).astype(BF)
-        half_ref[0, :, t * 128 : t * 128 + 128] = parted[:, :128]
-        half_ref[1, :, t * 128 : t * 128 + 128] = parted[:, 128:]
+        for c in range(4):
+            class_ref[c, :, t * 128 : t * 128 + 128] = parted[:, c * 128 : c * 128 + 128]
 
     lane0 = lax.broadcasted_iota(jnp.int32, (64, 128), 1) == 0
 
-    @pl.loop(0, 8)
+    @pl.loop(0, 4)
     def _(k):
         arrive(k).wait()
-        even = jnp.dot(half_ref[0], table_ref[k, 0], preferred_element_type=F32)
-        odd = jnp.dot(half_ref[1], table_ref[k, 1], preferred_element_type=F32)
-        ec, es, oc, os = even[:, :128], even[:, 128:], odd[:, :128], odd[:, 128:]
-        middle = lane0 & (k == 0)
-        re = [ec + oc, jnp.where(middle, es, ec - oc)]
-        im = [jnp.where(middle, 0.0, es + os), jnp.where(middle, os, os - es)]
-        for h in range(2):
-            re_ref[h, k] = re[h]
-            im_ref[h, k] = im[h]
-            power = re[h] * re[h] + im[h] * im[h]
+        sums = [jnp.dot(class_ref[c], table_ref[k, c], preferred_element_type=F32) for c in range(4)]
+        c0, c1, c2, c3 = [v[:, :128] for v in sums]
+        s0, s1, s2, s3 = [v[:, 128:] for v in sums]
+        top = lane0 & (k == 0)
+        half, alone = c0 - c2, c3 - c1
+        places = [
+            (0, k, c0 + c1 + c2 + c3, jnp.where(top, 0.0, s0 + s1 + s2 + s3)),
+            (1, k, jnp.where(top, half, c0 + c2 - c1 - c3), jnp.where(top, alone, s1 + s3 - s0 - s2)),
+            (0, k + 4, jnp.where(top, s0 + s1 - s3, half - s1 + s3), jnp.where(top, -s2 - s1 - s3, alone - s0 + s2)),
+            (1, k + 4, jnp.where(top, s0 - s1 + s3, half + s1 - s3), jnp.where(top, s2 - s1 - s3, alone + s0 - s2)),
+        ]
+        for h, tile, re, im in places:
+            re_ref[h, tile] = re
+            im_ref[h, tile] = im
+            power = re * re + im * im
             hi = power.astype(BF)
-            power_ref[h, k, 0:64, :] = hi
-            power_ref[h, k, 64:128, :] = (power - hi.astype(F32)).astype(BF)
-
+            power_ref[h, tile, 0:64, :] = hi
+            power_ref[h, tile, 64:128, :] = (power - hi.astype(F32)).astype(BF)
+
+    for copy in whole[1:]:
+        copy.wait()
     use = smooth_tables()[1]
     is_re = (lax.broadcasted_iota(jnp.int32, (64, 128), 0) // CH) % 2 == 0
     lane_seg = lax.broadcasted_iota(jnp.int32, (8, 128), 1) // 16
@@ -157,7 +179,7 @@
         for h in range(2):
             tiles, number = use[h * 8 + t]
             near = jnp.concatenate([power_ref[k // 8, k % 8] for k in tiles], axis=1)
-            both = jnp.dot(near, smooth_ref[number], preferred_element_type=F32)
+            both = jnp.dot(near, smooth_ref[number, : near.shape[1]], preferred_element_type=F32)
             smooth = (both[:64] + both[64:]) * (1.0 / (2 * SMOOTH + 1))
             scale = taper_ref[h : h + 1, t * 128 : t * 128 + 128] * lax.rsqrt(smooth + 1e-06)
             spec = (jnp.where(is_re, re_ref[h, t], im_ref[h, t]) * scale).astype(BF)
@@ -180,19 +202,24 @@
     return pl.pallas_call(
         spectra_kernel,
         out_shape=jax.ShapeDtypeStruct((1024, 128), BF),
-        in_specs=[vmem] * 5 + [pl.BlockSpec(memory_space=pl.ANY)],
+        in_specs=[vmem] + [pl.BlockSpec(memory_space=pl.ANY)] * 5,
         out_specs=vmem,
         scratch_shapes=[
-            pltpu.VMEM((8, 2, NT // 2, 256), BF),
+            pltpu.VMEM((512, 512), BF),
+            pltpu.VMEM(smooth_tables()[0].shape, BF),
+            pltpu.VMEM((2, HALF), F32),
+            pltpu.VMEM((128, 1024), BF),
+            pltpu.VMEM((4, 4, NT // 4, 256), BF),
             pltpu.VMEM((64, NT), F32),
-            pltpu.VMEM((2, 64, NT // 2), BF),
+            pltpu.VMEM((4, 64, NT // 4), BF),
             pltpu.VMEM((2, 8, 64, 128), F32),
             pltpu.VMEM((2, 8, 64, 128), F32),
             pltpu.VMEM((2, 8, 128, 128), BF),
-            pltpu.SemaphoreType.DMA((8,)),
+            pltpu.SemaphoreType.DMA((4,)),
+            pltpu.SemaphoreType.DMA((4,)),
         ],
-        compiler_params=pltpu.CompilerParams(vmem_limit_bytes=40 * 2**20),
-        cost_estimate=pl.CostEstimate(flops=2**31, bytes_accessed=NT * NT, transcendentals=0),
+        compiler_params=pltpu.CompilerParams(vmem_limit_bytes=58 * 2**20),
+        cost_estimate=pl.CostEstimate(flops=2**30, bytes_accessed=NT * NT // 2, transcendentals=0),
         name="spectra",
     )(got, parting_table(), smooth_tables()[0], taper_rows(), spread_table(), dft_table())
 
@@ -202,17 +229,26 @@
 
 def pair_kernel(pos_ref, a_hbm, *refs):
     nrow, ncol = 8, 16
-    b_hbm = refs[:nrow]
+    b_hbm, c_hbm, refs = refs[:nrow], refs[nrow : 2 * nrow], refs[nrow:]
     lag_hbm, turn_ref, out_hbm, a_ref, b_ref, lag_ref, x_ref, y_ref, f_ref, o_ref, in_sem, lag_sem, out_sem = refs[nrow:]
     size = 1024 // CHUNKS
+    side = pos_ref[1] // 2 % 2
 
     def arrive(k):
         rows = pl.ds(k * size, size)
-        copies = [pltpu.make_async_copy(a_hbm.at[:, rows, :], a_ref.at[:, rows, :], in_sem.at[k, nrow])]
-        for r in range(nrow):
+        copies = []
+        for x in range(4):
+            copies.append(
+                pltpu.make_async_copy(
+                    a_hbm.at[pl.ds(x * 2, 2), rows, :], a_ref.at[pl.ds(x * 4 + side * 2, 2), rows, :],
+                    in_sem.at[k, 16 + x]))
+        for r in range(8):
             copies.append(
                 pltpu.make_async_copy(
                     b_hbm[r].at[rows, :], b_ref.at[pos_ref[2 + r], rows, :], in_sem.at[k, r]))
+            copies.append(
+                pltpu.make_async_copy(
+                    c_hbm[r].at[rows, :], a_ref.at[pos_ref[10 + r], rows, :], in_sem.at[k, 8 + r]))
         return copies
 
     for k in range(CHUNKS):
@@ -338,14 +374,14 @@
             leave(half, d).wait()
 
 
-def pairs_of(pos, a, b):
-    nrow, ncol = len(b), a.shape[0]
+def pairs_of(pos, a, b, c):
+    nrow, ncol = len(b), a.shape[0] + len(c)
     assert nrow == 8 and ncol == 16
     anywhere = pl.BlockSpec(memory_space=pl.ANY)
     return pl.pallas_call(
         pair_kernel,
         out_shape=jax.ShapeDtypeStruct((ncol * CH, nrow * CH, LAGS), BF),
-        in_specs=[pl.BlockSpec(memory_space=pltpu.SMEM)] + [anywhere] * (nrow + 2)
+        in_specs=[pl.BlockSpec(memory_space=pltpu.SMEM)] + [anywhere] * (2 * nrow + 2)
         + [pl.BlockSpec(memory_space=pltpu.VMEM)],
         out_specs=anywhere,
         scratch_shapes=[
@@ -356,14 +392,14 @@
             pltpu.VMEM((2, LAGS, 128), F32),
             pltpu.VMEM((LAGS // 128, 8 * 129 + 8, 128), F32),
             pltpu.VMEM((ncol * CH, nrow * CH, LAGS), BF),
-            pltpu.SemaphoreType.DMA((CHUNKS, nrow + 1)),
+            pltpu.SemaphoreType.DMA((CHUNKS, 20)),
             pltpu.SemaphoreType.DMA,
             pltpu.SemaphoreType.DMA((2, ncol)),
         ],
         compiler_params=pltpu.CompilerParams(vmem_limit_bytes=52 * 2**20),
         cost_estimate=pl.CostEstimate(flops=2**34, bytes_accessed=16 * 2**20, transcendentals=0),
         name="pairs",
-    )(pos, a, *b, lag_tables(), turning_tables())
+    )(pos, a, *b, *c, lag_tables(), turning_tables())
 
 
 def over_row(own, my_row):
@@ -383,6 +419,22 @@
         index(-1, 1), index(1, 1), index(2, 0), index(2, 1),
     ]
     return blocks, rows
+
+
+def over_col(own, my_col):
+    def move(block, step=0, across=0, core=0):
+        pairs = [
+            (x * 4 + y * 2 + c, (x + step) % 4 * 4 + (y ^ across) * 2 + (c ^ core))
+            for x in range(4) for y in range(2) for c in range(2)]
+        return lax.ppermute(block, "col", pairs)
+
+    x, y, core = my_col // 4, my_col // 2 % 2, my_col % 2
+    near = move(own, across=1)
+    left, right = move(near, 1), move(near, -1)
+    blocks = [near, left, right, move(left, 1)]
+    cols = [(x + step) % 4 * 4 + (y ^ 1) * 2 for step in (0, -1, 1, 2)]
+    blocks += [move(v, core=1) for v in blocks]
+    return blocks, [c + core for c in cols] + [c + (core ^ 1) for c in cols]
 
 
 def local(strain, file_channels, file_counts, window_start):
@@ -403,10 +455,12 @@
     sent = jnp.concatenate([bundle, tags], axis=1).reshape(nrow, 2, WIN + 128)
     got = lax.all_to_all(sent, "row", 0, 0).reshape(2 * nrow, WIN + 128)
     own = spectra_of(got)
-    a = lax.all_gather(own, "col", axis=0)
+    rings = [[x * 4 + y * 2 + core for x in range(4) for core in range(2)] for y in range(2)]
+    a = lax.all_gather(own, "col", axis=0, axis_index_groups=rings)
+    c, cols = over_col(own, my_col)
     b, rows = over_row(own, my_row)
-    pos = jnp.stack([my_row, my_col, *rows]).astype(jnp.int32)
-    return pairs_of(pos, a, b)
+    pos = jnp.stack([my_row, my_col, *rows, *cols]).astype(jnp.int32)
+    return pairs_of(pos, a, b, c)
 
 
 def solution(mesh):

time: 116 us -> 114 us (0.983)
  waiting for transfers between devices: 30.6 us -> 13 us
  starting transfers between devices: 5.77 us -> 21.5 us
    ppermute x7, waiting for transfers between devices: 17.9 us -> 1.11 us  [move(): return lax.ppermute(block, 'row', pairs)]
    ppermute x0 -> x8, starting transfers between devices: none -> 14.2 us  [move(): return lax.ppermute(block, 'col', pairs)]
    all_gather x1, waiting for transfers between devices: 12.7 us -> 0.01 us  [local(): a = lax.all_gather(own, 'col', axis=0, axis_index_groups=rings)]
    ppermute x0 -> x8, waiting for transfers between devices: none -> 11.9 us  [move(): return lax.ppermute(block, 'col', pairs)]
    ppermute x7, starting transfers between devices: 5.77 us -> 7.35 us  [move(): return lax.ppermute(block, 'row', pairs)]
    pallas_call x1, Pallas kernels: 24.5 us -> 25.7 us  [pairs_of(): pl.pallas_call(pair_kernel, out_shape=jax.ShapeDtypeStruct((ncol * CH, nr...]
    pallas_call x1, Pallas kernels: 11.2 us -> 10 us  [spectra_of(): pl.pallas_call(spectra_kernel, out_shape=jax.ShapeDtypeStruct((1024, 128)...]
  transfers between devices with their start and end apart: 8 -> 16, of which waited for: 6 -> 4; matrix products, arithmetic and copies ran while one was open for 0% -> 0% of each run, Pallas kernels for 0% -> 0%
where the time goes in v5:
time: 114 us
  Pallas kernels  35.8 us (31%)
  blocking collectives  24.6 us (22%)
  starting transfers between devices  21.5 us (19%)
  between operations  14.9 us (13%)
  waiting for transfers between devices  13 us (11%)
  local copies, waits for them, and re-layouts  2.78 us (2%)
    pallas_call x1, Pallas kernels, pairs_of(): pl.pallas_call(pair_kernel, out_shape=jax.ShapeDtypeStruct((ncol * CH, nr...  25.7 us
    all_to_all x1, blocking collectives, local(): got = lax.all_to_all(sent, 'row', 0, 0).reshape(2 * nrow, WIN + 128)  24.6 us
    ppermute x8, starting transfers between devices, move(): return lax.ppermute(block, 'col', pairs)  14.2 us
    ppermute x8, waiting for transfers between devices, move(): return lax.ppermute(block, 'col', pairs)  11.9 us
    pallas_call x1, Pallas kernels, spectra_of(): pl.pallas_call(spectra_kernel, out_shape=jax.ShapeDtypeStruct((1024, 128)...  10 us
    ppermute x7, starting transfers between devices, move(): return lax.ppermute(block, 'row', pairs)  7.35 us
  transfers between devices with their start and end apart: 16, of which 4 were waited for; matrix products, arithmetic and copies ran while one was open for 0% of the time, Pallas kernels for 0%

profile of v5, /device:TPU:1, one launch (start us, length us, event | category | flops | bytes accessed | tf_op | source)
XLA Modules:
  0.0 114.2 jit_solution(1708256692161414018)
XLA Ops:
  6.5 0.0 copy-start
  6.5 0.0 all-gather.3.cloned.1.call-start
  7.9 0.7 compare_select_fusion
  8.6 0.2 convert_reduce_fusion
  8.8 0.2 select_reduce_fusion
  9.0 0.0 copy-done
  9.0 0.5 convolution_convert_fusion
  9.5 0.1 broadcast_in_dim.14
  9.6 0.1 pad_maximum_fusion
  9.7 0.4 reshape.67
  10.1 24.6 %all_to_all.5 = bf16[8,2,32896]{2,1,0:T(2,128)(2,1)S(1)} all-to-all(bf16[8,2,32896]{2,1,0:T(2,128)(2,1)S(1)} %reshape.67), channel_id=1, replica_groups=mesh['row'=8,'col'=16] {'row'}, dimensions={0} | all-to-all | bytes 2105344 | tf_op jit(solution)/shard_map/all_to_all | solution.py:456
  34.7 1.2 %reshape.68.got_ref = bf16[16,32896]{1,0:T(8,128)(2,1)} reshape(bf16[8,2,32896]{2,1,0:T(2,128)(2,1)S(1)} %all_to_all.5) | data formatting | bytes 2105344 | tf_op jit(solution)/shard_map/reshape | solution.py:456
  35.9 10.0 %spectra.1.refs_0_ = bf16[1024,128]{1,0:T(8,128)(2,1)} custom-call(bf16[16,32896]{1,0:T(8,128)(2,1)} %reshape.68.got_ref, bf16[512,512]{1,0:T(8,128)(2,1)} %constant.171.clone.part_hbm, bf16[7,768,128]{2,1,0:T(8,128)(2,1)} %constant.172.clone.smooth_hbm, f32[2,1024]{1,0:T(2,128)} %constant.173.clone.taper_hbm, bf16[128,1024]{1,0:T(8,128)(2,1)} %constant.174.clone.spread_hbm, ...), custom_call_target="tpu_custom_call" | custom-call | flops 1073741824 | bytes 8388608 | tf_op jit(solution)/shard_map/spectra/pallas_call | solution.py:202
  46.0 0.0 all-gather.3.cloned.1.call-update
  46.0 0.6 collective-permute-start.7
  46.5 0.9 collective-permute-start.2
  47.4 0.6 collective-permute-start.1
  48.0 1.1 collective-permute-start
  49.1 2.8 %collective-permute-done.7.refs_8_ = bf16[1024,128]{1,0:T(8,128)(2,1)S(1)} collective-permute-done((bf16[1024,128]{1,0:T(8,128)(2,1)}, bf16[1024,128]{1,0:T(8,128)(2,1)S(1)}, u32[]{:S(2)}, u32[]{:S(2)}) %collective-permute-start.7) | collective-permute-done | bytes 262176 | tf_op jit(solution)/shard_map/ppermute | solution.py:429
  51.9 0.0 copy-start.2
  51.9 1.2 %collective-permute-start.8 = (bf16[1024,128]{1,0:T(8,128)(2,1)S(1)}, bf16[1024,128]{1,0:T(8,128)(2,1)S(1)}, u32[]{:S(2)}, u32[]{:S(2)}) collective-permute-start(bf16[1024,128]{1,0:T(8,128)(2,1)S(1)} %collective-permute-done.7.refs_8_), channel_id=1, source_target_pairs={{0,4},{1,5},{2,6},{3,7},{4,8},{5,9},{6,10},{7,11},{8,12},{9,13},{1... | collective-permute-start | bytes 786440 | tf_op jit(solution)/shard_map/ppermute | solution.py:429
  53.1 6.1 %collective-permute-start.11 = (bf16[1024,128]{1,0:T(8,128)(2,1)S(1)}, bf16[1024,128]{1,0:T(8,128)(2,1)S(1)}, u32[]{:S(2)}, u32[]{:S(2)}) collective-permute-start(bf16[1024,128]{1,0:T(8,128)(2,1)S(1)} %collective-permute-done.7.refs_8_), channel_id=1, source_target_pairs={{0,1},{1,0},{2,3},{3,2},{4,5},{5,4},{6,7},{7,6},{8,9},{9,8},{10,11... | collective-permute-start | bytes 786440 | tf_op jit(solution)/shard_map/ppermute | solution.py:429
  59.2 0.0 collective-permute-done.2.refs_3_
  59.2 1.5 %collective-permute-start.9 = (bf16[1024,128]{1,0:T(8,128)(2,1)S(1)}, bf16[1024,128]{1,0:T(8,128)(2,1)}, u32[]{:S(2)}, u32[]{:S(2)}) collective-permute-start(bf16[1024,128]{1,0:T(8,128)(2,1)S(1)} %collective-permute-done.7.refs_8_), channel_id=1, source_target_pairs={{0,12},{1,13},{2,14},{3,15},{4,0},{5,1},{6,2},{7,3},{8,4},{9,5},{1... | collective-permute-start | bytes 786440 | tf_op jit(solution)/shard_map/ppermute | solution.py:429
  60.6 0.0 collective-permute-done.1.refs_2_
  60.7 0.3 collective-permute-start.5
  60.9 0.0 collective-permute-done.refs_1_
  60.9 2.4 %collective-permute-start.4 = (bf16[1024,128]{1,0:T(8,128)(2,1)S(1)}, bf16[1024,128]{1,0:T(8,128)(2,1)S(1)}, u32[]{:S(2)}, u32[]{:S(2)}) collective-permute-start(bf16[1024,128]{1,0:T(8,128)(2,1)S(1)} %collective-permute-done.refs_1_), channel_id=1, source_target_pairs={{0,48},{16,0},{32,16},{48,32},{64,112},{80,64},{96,80},{112,96},{1... | collective-permute-start | bytes 786440 | tf_op jit(solution)/shard_map/ppermute | solution.py:408
  63.3 0.0 collective-permute-done.8.refs_9_
  63.3 0.0 copy-start.3
  63.3 0.0 collective-permute-start.10
  63.3 0.0 collective-permute-done.11.refs_12_
  63.4 0.0 copy-start.4
  63.4 0.1 collective-permute-start.3
  63.4 8.8 %collective-permute-done.9.refs_10_ = bf16[1024,128]{1,0:T(8,128)(2,1)} collective-permute-done((bf16[1024,128]{1,0:T(8,128)(2,1)S(1)}, bf16[1024,128]{1,0:T(8,128)(2,1)}, u32[]{:S(2)}, u32[]{:S(2)}) %collective-permute-start.9) | collective-permute-done | bytes 262176 | tf_op jit(solution)/shard_map/ppermute | solution.py:429
  72.2 0.5 collective-permute-start.12
  72.7 0.0 collective-permute-done.5.refs_6_
  72.7 0.1 collective-permute-start.13
  72.8 0.0 collective-permute-done.4.refs_5_
  72.8 2.1 %collective-permute-start.6 = (bf16[1024,128]{1,0:T(8,128)(2,1)S(1)}, bf16[1024,128]{1,0:T(8,128)(2,1)}, u32[]{:S(2)}, u32[]{:S(2)}) collective-permute-start(bf16[1024,128]{1,0:T(8,128)(2,1)S(1)} %collective-permute-done.4.refs_5_), channel_id=1, source_target_pairs={{0,48},{16,0},{32,16},{48,32},{64,112},{80,64},{96,80},{112,96},{1... | collective-permute-start | bytes 786440 | tf_op jit(solution)/shard_map/ppermute | solution.py:408
  74.9 0.0 collective-permute-done.10.refs_11_
  74.9 4.3 %collective-permute-start.14 = (bf16[1024,128]{1,0:T(8,128)(2,1)}, bf16[1024,128]{1,0:T(8,128)(2,1)}, u32[]{:S(2)}, u32[]{:S(2)}) collective-permute-start(bf16[1024,128]{1,0:T(8,128)(2,1)} %collective-permute-done.10.refs_11_), channel_id=1, source_target_pairs={{0,1},{1,0},{2,3},{3,2},{4,5},{5,4},{6,7},{7,6},{8,9},{9,8},{10,11... | collective-permute-start | bytes 786440 | tf_op jit(solution)/shard_map/ppermute | solution.py:429
  79.1 0.1 stack.75.pos_ref
  79.2 0.0 collective-permute-done.3.refs_4_
  79.2 0.0 collective-permute-done.13.refs_14_
  79.3 0.0 collective-permute-done.12.refs_13_
  79.3 1.1 collective-permute-done.6.refs_7_
  80.4 0.3 collective-permute-done.14.refs_15_
  80.6 0.0 all-gather.3.cloned.1.call-done
  80.6 0.0 copy-done.2
  80.6 0.0 copy-done.3
  80.7 0.0 copy-done.4
  80.7 0.0 copy-start.1
  80.7 0.9 copy-done.1
  81.6 25.7 %pairs.1 = bf16[64,32,1024]{2,1,0:T(8,128)(2,1)} custom-call(s32[18]{0:T(128)S(1)} %stack.75.pos_ref, bf16[8,1024,128]{2,1,0:T(8,128)(2,1)} %bitcast.25, bf16[1024,128]{1,0:T(8,128)(2,1)S(1)} %copy-done.1, bf16[1024,128]{1,0:T(8,128)(2,1)S(1)} %collective-permute-done.refs_1_, bf16[1024,128]{1,0:T(8,128)(2,1)S(1)} %collective-permute-done.1.refs_2_, ...), custom_call_target="tpu_custom_call" | custom-call | flops 17179869184 | bytes 16777216 | tf_op jit(solution)/shard_map/pairs/pallas_call | solution.py:381
  (2 shorter events, 0.0 us)
Async XLA Ops:
  6.5 2.5 %copy-start = (bf16[16,33280]{1,0:T(8,128)(2,1)S(1)}, bf16[16,33280]{1,0:T(8,128)(2,1)}, u32[]{:S(2)}) copy-start(bf16[16,33280]{1,0:T(8,128)(2,1)} %param.11) | copy-start | bytes 3194884
  6.5 74.1 %all-gather.3.cloned.1.call-start = ((), (), s32[]{:S(2)}) async-start(), calls=%async_computation.1 | async-start | bytes 2359296 | tf_op jit(solution)/shard_map/all_gather | solution.py:459
  46.0 5.9 %collective-permute-start.7 = (bf16[1024,128]{1,0:T(8,128)(2,1)}, bf16[1024,128]{1,0:T(8,128)(2,1)S(1)}, u32[]{:S(2)}, u32[]{:S(2)}) collective-permute-start(bf16[1024,128]{1,0:T(8,128)(2,1)} %spectra.1.refs_0_), channel_id=1, source_target_pairs={{0,2},{1,3},{2,0},{3,1},{4,6},{5,7},{6,4},{7,5},{8,10},{9,11},{10,... | collective-permute-start | bytes 786440 | tf_op jit(solution)/shard_map/ppermute | solution.py:429
  46.5 12.6 %collective-permute-start.2 = (bf16[1024,128]{1,0:T(8,128)(2,1)}, bf16[1024,128]{1,0:T(8,128)(2,1)S(1)}, u32[]{:S(2)}, u32[]{:S(2)}) collective-permute-start(bf16[1024,128]{1,0:T(8,128)(2,1)} %spectra.1.refs_0_), channel_id=1, source_target_pairs={{0,48},{16,0},{32,16},{48,32},{64,112},{80,64},{96,80},{112,96},{1... | collective-permute-start | bytes 786440 | tf_op jit(solution)/shard_map/ppermute | solution.py:408
  47.4 13.2 %collective-permute-start.1 = (bf16[1024,128]{1,0:T(8,128)(2,1)}, bf16[1024,128]{1,0:T(8,128)(2,1)S(1)}, u32[]{:S(2)}, u32[]{:S(2)}) collective-permute-start(bf16[1024,128]{1,0:T(8,128)(2,1)} %spectra.1.refs_0_), channel_id=1, source_target_pairs={{0,16},{16,32},{32,48},{48,0},{64,80},{80,96},{96,112},{112,64},{1... | collective-permute-start | bytes 786440 | tf_op jit(solution)/shard_map/ppermute | solution.py:408
  48.0 12.9 %collective-permute-start = (bf16[1024,128]{1,0:T(8,128)(2,1)}, bf16[1024,128]{1,0:T(8,128)(2,1)S(1)}, u32[]{:S(2)}, u32[]{:S(2)}) collective-permute-start(bf16[1024,128]{1,0:T(8,128)(2,1)} %spectra.1.refs_0_), channel_id=1, source_target_pairs={{0,64},{16,80},{32,96},{48,112},{64,0},{80,16},{96,32},{112,48},{1... | collective-permute-start | bytes 786440 | tf_op jit(solution)/shard_map/ppermute | solution.py:408
  51.9 28.8 %copy-start.2 = (bf16[1024,128]{1,0:T(8,128)(2,1)}, bf16[1024,128]{1,0:T(8,128)(2,1)S(1)}, u32[]{:S(2)}) copy-start(bf16[1024,128]{1,0:T(8,128)(2,1)S(1)} %collective-permute-done.7.refs_8_) | copy-start | bytes 786436
  51.9 11.4 %collective-permute-start.8 = (bf16[1024,128]{1,0:T(8,128)(2,1)S(1)}, bf16[1024,128]{1,0:T(8,128)(2,1)S(1)}, u32[]{:S(2)}, u32[]{:S(2)}) collective-permute-start(bf16[1024,128]{1,0:T(8,128)(2,1)S(1)} %collective-permute-done.7.refs_8_), channel_id=1, source_target_pairs={{0,4},{1,5},{2,6},{3,7},{4,8},{5,9},{6,10},{7,11},{8,12},{9,13},{1... | collective-permute-start | bytes 786440 | tf_op jit(solution)/shard_map/ppermute | solution.py:429
  53.1 10.3 %collective-permute-start.11 = (bf16[1024,128]{1,0:T(8,128)(2,1)S(1)}, bf16[1024,128]{1,0:T(8,128)(2,1)S(1)}, u32[]{:S(2)}, u32[]{:S(2)}) collective-permute-start(bf16[1024,128]{1,0:T(8,128)(2,1)S(1)} %collective-permute-done.7.refs_8_), channel_id=1, source_target_pairs={{0,1},{1,0},{2,3},{3,2},{4,5},{5,4},{6,7},{7,6},{8,9},{9,8},{10,11... | collective-permute-start | bytes 786440 | tf_op jit(solution)/shard_map/ppermute | solution.py:429
  59.2 13.0 %collective-permute-start.9 = (bf16[1024,128]{1,0:T(8,128)(2,1)S(1)}, bf16[1024,128]{1,0:T(8,128)(2,1)}, u32[]{:S(2)}, u32[]{:S(2)}) collective-permute-start(bf16[1024,128]{1,0:T(8,128)(2,1)S(1)} %collective-permute-done.7.refs_8_), channel_id=1, source_target_pairs={{0,12},{1,13},{2,14},{3,15},{4,0},{5,1},{6,2},{7,3},{8,4},{9,5},{1... | collective-permute-start | bytes 786440 | tf_op jit(solution)/shard_map/ppermute | solution.py:429
  60.7 12.1 %collective-permute-start.5 = (bf16[1024,128]{1,0:T(8,128)(2,1)S(1)}, bf16[1024,128]{1,0:T(8,128)(2,1)S(1)}, u32[]{:S(2)}, u32[]{:S(2)}) collective-permute-start(bf16[1024,128]{1,0:T(8,128)(2,1)S(1)} %collective-permute-done.1.refs_2_), channel_id=1, source_target_pairs={{0,16},{16,32},{32,48},{48,0},{64,80},{80,96},{96,112},{112,64},{1... | collective-permute-start | bytes 786440 | tf_op jit(solution)/shard_map/ppermute | solution.py:408
  60.9 11.9 %collective-permute-start.4 = (bf16[1024,128]{1,0:T(8,128)(2,1)S(1)}, bf16[1024,128]{1,0:T(8,128)(2,1)S(1)}, u32[]{:S(2)}, u32[]{:S(2)}) collective-permute-start(bf16[1024,128]{1,0:T(8,128)(2,1)S(1)} %collective-permute-done.refs_1_), channel_id=1, source_target_pairs={{0,48},{16,0},{32,16},{48,32},{64,112},{80,64},{96,80},{112,96},{1... | collective-permute-start | bytes 786440 | tf_op jit(solution)/shard_map/ppermute | solution.py:408
  63.3 17.3 %copy-start.3 = (bf16[1024,128]{1,0:T(8,128)(2,1)}, bf16[1024,128]{1,0:T(8,128)(2,1)S(1)}, u32[]{:S(2)}) copy-start(bf16[1024,128]{1,0:T(8,128)(2,1)S(1)} %collective-permute-done.8.refs_9_) | copy-start | bytes 786436
  63.3 11.5 %collective-permute-start.10 = (bf16[1024,128]{1,0:T(8,128)(2,1)S(1)}, bf16[1024,128]{1,0:T(8,128)(2,1)}, u32[]{:S(2)}, u32[]{:S(2)}) collective-permute-start(bf16[1024,128]{1,0:T(8,128)(2,1)S(1)} %collective-permute-done.8.refs_9_), channel_id=1, source_target_pairs={{0,4},{1,5},{2,6},{3,7},{4,8},{5,9},{6,10},{7,11},{8,12},{9,13},{1... | collective-permute-start | bytes 786440 | tf_op jit(solution)/shard_map/ppermute | solution.py:429
  63.4 17.3 %copy-start.4 = (bf16[1024,128]{1,0:T(8,128)(2,1)}, bf16[1024,128]{1,0:T(8,128)(2,1)S(1)}, u32[]{:S(2)}) copy-start(bf16[1024,128]{1,0:T(8,128)(2,1)S(1)} %collective-permute-done.11.refs_12_) | copy-start | bytes 786436
  63.4 15.9 %collective-permute-start.3 = (bf16[1024,128]{1,0:T(8,128)(2,1)S(1)}, bf16[1024,128]{1,0:T(8,128)(2,1)S(1)}, u32[]{:S(2)}, u32[]{:S(2)}) collective-permute-start(bf16[1024,128]{1,0:T(8,128)(2,1)S(1)} %collective-permute-done.refs_1_), channel_id=1, source_target_pairs={{0,16},{16,32},{32,48},{48,0},{64,80},{80,96},{96,112},{112,64},{1... | collective-permute-start | bytes 786440 | tf_op jit(solution)/shard_map/ppermute | solution.py:408
  72.2 7.0 %collective-permute-start.12 = (bf16[1024,128]{1,0:T(8,128)(2,1)S(1)}, bf16[1024,128]{1,0:T(8,128)(2,1)}, u32[]{:S(2)}, u32[]{:S(2)}) collective-permute-start(bf16[1024,128]{1,0:T(8,128)(2,1)S(1)} %collective-permute-done.8.refs_9_), channel_id=1, source_target_pairs={{0,1},{1,0},{2,3},{3,2},{4,5},{5,4},{6,7},{7,6},{8,9},{9,8},{10,11... | collective-permute-start | bytes 786440 | tf_op jit(solution)/shard_map/ppermute | solution.py:429
  72.7 6.5 %collective-permute-start.13 = (bf16[1024,128]{1,0:T(8,128)(2,1)}, bf16[1024,128]{1,0:T(8,128)(2,1)}, u32[]{:S(2)}, u32[]{:S(2)}) collective-permute-start(bf16[1024,128]{1,0:T(8,128)(2,1)} %collective-permute-done.9.refs_10_), channel_id=1, source_target_pairs={{0,1},{1,0},{2,3},{3,2},{4,5},{5,4},{6,7},{7,6},{8,9},{9,8},{10,11... | collective-permute-start | bytes 786440 | tf_op jit(solution)/shard_map/ppermute | solution.py:429
  72.8 7.6 %collective-permute-start.6 = (bf16[1024,128]{1,0:T(8,128)(2,1)S(1)}, bf16[1024,128]{1,0:T(8,128)(2,1)}, u32[]{:S(2)}, u32[]{:S(2)}) collective-permute-start(bf16[1024,128]{1,0:T(8,128)(2,1)S(1)} %collective-permute-done.4.refs_5_), channel_id=1, source_target_pairs={{0,48},{16,0},{32,16},{48,32},{64,112},{80,64},{96,80},{112,96},{1... | collective-permute-start | bytes 786440 | tf_op jit(solution)/shard_map/ppermute | solution.py:408
  74.9 5.8 %collective-permute-start.14 = (bf16[1024,128]{1,0:T(8,128)(2,1)}, bf16[1024,128]{1,0:T(8,128)(2,1)}, u32[]{:S(2)}, u32[]{:S(2)}) collective-permute-start(bf16[1024,128]{1,0:T(8,128)(2,1)} %collective-permute-done.10.refs_11_), channel_id=1, source_target_pairs={{0,1},{1,0},{2,3},{3,2},{4,5},{5,4},{6,7},{7,6},{8,9},{9,8},{10,11... | collective-permute-start | bytes 786440 | tf_op jit(solution)/shard_map/ppermute | solution.py:429
  80.7 1.0 copy-start.1
Sparse Core Ops, SparseCore 0:
  46.1 27.5 all-gather.2

commit v6 on v5

--- a/solution.py
+++ b/solution.py
@@ -396,7 +396,7 @@
             pltpu.SemaphoreType.DMA,
             pltpu.SemaphoreType.DMA((2, ncol)),
         ],
-        compiler_params=pltpu.CompilerParams(vmem_limit_bytes=52 * 2**20),
+        compiler_params=pltpu.CompilerParams(vmem_limit_bytes=60 * 2**20),
         cost_estimate=pl.CostEstimate(flops=2**34, bytes_accessed=16 * 2**20, transcendentals=0),
         name="pairs",
     )(pos, a, *b, *c, lag_tables(), turning_tables())

time: 114 us -> 112 us (0.982)
  Pallas kernels: 35.8 us -> 34.2 us
    pallas_call x1, Pallas kernels: 25.7 us -> 24.2 us  [pairs_of(): pl.pallas_call(pair_kernel, out_shape=jax.ShapeDtypeStruct((ncol * CH, nr...]
  transfers between devices with their start and end apart: 16 -> 16, of which waited for: 4 -> 4; matrix products, arithmetic and copies ran while one was open for 0% -> 1% of each run, Pallas kernels for 0% -> 0%
where the time goes in v6:
time: 112 us
  Pallas kernels  34.2 us (31%)
  blocking collectives  24.6 us (22%)
  starting transfers between devices  21.7 us (19%)
  between operations  14.9 us (13%)
  waiting for transfers between devices  12.3 us (11%)
  local copies, waits for them, and re-layouts  2.4 us (2%)
  other arithmetic  1.13 us (1%)
    all_to_all x1, blocking collectives, local(): got = lax.all_to_all(sent, 'row', 0, 0).reshape(2 * nrow, WIN + 128)  24.6 us
    pallas_call x1, Pallas kernels, pairs_of(): pl.pallas_call(pair_kernel, out_shape=jax.ShapeDtypeStruct((ncol * CH, nr...  24.2 us
    ppermute x8, starting transfers between devices, move(): return lax.ppermute(block, 'col', pairs)  14.4 us
    ppermute x8, waiting for transfers between devices, move(): return lax.ppermute(block, 'col', pairs)  11.7 us
    pallas_call x1, Pallas kernels, spectra_of(): pl.pallas_call(spectra_kernel, out_shape=jax.ShapeDtypeStruct((1024, 128)...  10 us
    ppermute x7, starting transfers between devices, move(): return lax.ppermute(block, 'row', pairs)  7.33 us
  transfers between devices with their start and end apart: 16, of which 4 were waited for; matrix products, arithmetic and copies ran while one was open for 1% of the time, Pallas kernels for 0%

profile of v6, /device:TPU:1, one launch (start us, length us, event | category | flops | bytes accessed | tf_op | source)
XLA Modules:
  0.0 111.8 jit_solution(11828885377857043454)
XLA Ops:
  6.5 0.0 copy-start
  6.5 0.0 all-gather.3.cloned.1.call-start
  7.9 0.7 compare_select_fusion
  8.6 0.2 convert_reduce_fusion
  8.8 0.2 select_reduce_fusion
  9.0 0.0 copy-done
  9.0 0.5 convolution_convert_fusion
  9.5 0.1 broadcast_in_dim.14
  9.6 0.1 pad_maximum_fusion
  9.7 0.4 reshape.67
  10.1 24.6 %all_to_all.5 = bf16[8,2,32896]{2,1,0:T(2,128)(2,1)S(1)} all-to-all(bf16[8,2,32896]{2,1,0:T(2,128)(2,1)S(1)} %reshape.67), channel_id=1, replica_groups=mesh['row'=8,'col'=16] {'row'}, dimensions={0} | all-to-all | bytes 2105344 | tf_op jit(solution)/shard_map/all_to_all | solution.py:456
  34.7 1.2 %reshape.68.got_ref = bf16[16,32896]{1,0:T(8,128)(2,1)} reshape(bf16[8,2,32896]{2,1,0:T(2,128)(2,1)S(1)} %all_to_all.5) | data formatting | bytes 2105344 | tf_op jit(solution)/shard_map/reshape | solution.py:456
  35.9 10.0 %spectra.1.refs_0_ = bf16[1024,128]{1,0:T(8,128)(2,1)} custom-call(bf16[16,32896]{1,0:T(8,128)(2,1)} %reshape.68.got_ref, bf16[512,512]{1,0:T(8,128)(2,1)} %constant.171.clone.part_hbm, bf16[7,768,128]{2,1,0:T(8,128)(2,1)} %constant.172.clone.smooth_hbm, f32[2,1024]{1,0:T(2,128)} %constant.173.clone.taper_hbm, bf16[128,1024]{1,0:T(8,128)(2,1)} %constant.174.clone.spread_hbm, ...), custom_call_target="tpu_custom_call" | custom-call | flops 1073741824 | bytes 8388608 | tf_op jit(solution)/shard_map/spectra/pallas_call | solution.py:202
  46.0 0.0 all-gather.3.cloned.1.call-update
  46.0 0.6 collective-permute-start.7
  46.6 0.9 collective-permute-start.2
  47.4 0.6 collective-permute-start.1
  48.0 1.1 collective-permute-start
  49.1 2.8 %collective-permute-done.7.refs_8_ = bf16[1024,128]{1,0:T(8,128)(2,1)S(1)} collective-permute-done((bf16[1024,128]{1,0:T(8,128)(2,1)}, bf16[1024,128]{1,0:T(8,128)(2,1)S(1)}, u32[]{:S(2)}, u32[]{:S(2)}) %collective-permute-start.7) | collective-permute-done | bytes 262176 | tf_op jit(solution)/shard_map/ppermute | solution.py:429
  51.9 0.0 copy-start.1
  51.9 1.2 %collective-permute-start.8 = (bf16[1024,128]{1,0:T(8,128)(2,1)S(1)}, bf16[1024,128]{1,0:T(8,128)(2,1)S(1)}, u32[]{:S(2)}, u32[]{:S(2)}) collective-permute-start(bf16[1024,128]{1,0:T(8,128)(2,1)S(1)} %collective-permute-done.7.refs_8_), channel_id=1, source_target_pairs={{0,4},{1,5},{2,6},{3,7},{4,8},{5,9},{6,10},{7,11},{8,12},{9,13},{1... | collective-permute-start | bytes 786440 | tf_op jit(solution)/shard_map/ppermute | solution.py:429
  53.1 6.1 %collective-permute-start.11 = (bf16[1024,128]{1,0:T(8,128)(2,1)S(1)}, bf16[1024,128]{1,0:T(8,128)(2,1)S(1)}, u32[]{:S(2)}, u32[]{:S(2)}) collective-permute-start(bf16[1024,128]{1,0:T(8,128)(2,1)S(1)} %collective-permute-done.7.refs_8_), channel_id=1, source_target_pairs={{0,1},{1,0},{2,3},{3,2},{4,5},{5,4},{6,7},{7,6},{8,9},{9,8},{10,11... | collective-permute-start | bytes 786440 | tf_op jit(solution)/shard_map/ppermute | solution.py:429
  59.2 0.0 collective-permute-done.2.refs_3_
  59.2 0.0 copy-start.2
  59.2 1.5 %collective-permute-start.9 = (bf16[1024,128]{1,0:T(8,128)(2,1)S(1)}, bf16[1024,128]{1,0:T(8,128)(2,1)S(1)}, u32[]{:S(2)}, u32[]{:S(2)}) collective-permute-start(bf16[1024,128]{1,0:T(8,128)(2,1)S(1)} %collective-permute-done.7.refs_8_), channel_id=1, source_target_pairs={{0,12},{1,13},{2,14},{3,15},{4,0},{5,1},{6,2},{7,3},{8,4},{9,5},{1... | collective-permute-start | bytes 786440 | tf_op jit(solution)/shard_map/ppermute | solution.py:429
  60.7 0.0 collective-permute-done.1.refs_2_
  60.7 0.0 copy-start.3
  60.7 0.3 collective-permute-start.5
  61.0 0.0 collective-permute-done.refs_1_
  61.0 0.0 copy-start.4
  61.0 2.4 %collective-permute-start.4 = (bf16[1024,128]{1,0:T(8,128)(2,1)S(1)}, bf16[1024,128]{1,0:T(8,128)(2,1)S(1)}, u32[]{:S(2)}, u32[]{:S(2)}) collective-permute-start(bf16[1024,128]{1,0:T(8,128)(2,1)S(1)} %collective-permute-done.refs_1_), channel_id=1, source_target_pairs={{0,48},{16,0},{32,16},{48,32},{64,112},{80,64},{96,80},{112,96},{1... | collective-permute-start | bytes 786440 | tf_op jit(solution)/shard_map/ppermute | solution.py:408
  63.3 0.0 collective-permute-done.8.refs_9_
  63.3 0.0 copy-start.5
  63.3 0.0 collective-permute-start.10
  63.4 0.0 collective-permute-done.11.refs_12_
  63.4 0.0 copy-start.6
  63.4 0.1 collective-permute-start.3
  63.5 8.6 %collective-permute-done.9.refs_10_ = bf16[1024,128]{1,0:T(8,128)(2,1)S(1)} collective-permute-done((bf16[1024,128]{1,0:T(8,128)(2,1)S(1)}, bf16[1024,128]{1,0:T(8,128)(2,1)S(1)}, u32[]{:S(2)}, u32[]{:S(2)}) %collective-permute-start.9) | collective-permute-done | bytes 262176 | tf_op jit(solution)/shard_map/ppermute | solution.py:429
  72.1 0.0 copy-start.7
  72.1 0.6 collective-permute-start.12
  72.7 0.0 collective-permute-done.5.refs_6_
  72.7 0.0 copy-start.8
  72.7 0.1 collective-permute-start.13
  72.8 0.0 collective-permute-done.4.refs_5_
  72.8 0.0 copy-start.9
  72.8 2.0 %collective-permute-start.6 = (bf16[1024,128]{1,0:T(8,128)(2,1)S(1)}, bf16[1024,128]{1,0:T(8,128)(2,1)}, u32[]{:S(2)}, u32[]{:S(2)}) collective-permute-start(bf16[1024,128]{1,0:T(8,128)(2,1)S(1)} %collective-permute-done.4.refs_5_), channel_id=1, source_target_pairs={{0,48},{16,0},{32,16},{48,32},{64,112},{80,64},{96,80},{112,96},{1... | collective-permute-start | bytes 786440 | tf_op jit(solution)/shard_map/ppermute | solution.py:408
  74.9 0.0 collective-permute-done.10.refs_11_
  74.9 4.3 %collective-permute-start.14 = (bf16[1024,128]{1,0:T(8,128)(2,1)}, bf16[1024,128]{1,0:T(8,128)(2,1)}, u32[]{:S(2)}, u32[]{:S(2)}) collective-permute-start(bf16[1024,128]{1,0:T(8,128)(2,1)} %collective-permute-done.10.refs_11_), channel_id=1, source_target_pairs={{0,1},{1,0},{2,3},{3,2},{4,5},{5,4},{6,7},{7,6},{8,9},{9,8},{10,11... | collective-permute-start | bytes 786440 | tf_op jit(solution)/shard_map/ppermute | solution.py:429
  79.2 0.6 stack.75.pos_ref
  79.8 0.0 collective-permute-done.3.refs_4_
  79.8 0.0 collective-permute-done.13.refs_14_
  79.8 0.0 collective-permute-done.12.refs_13_
  79.8 0.6 collective-permute-done.6.refs_7_
  80.4 0.3 collective-permute-done.14.refs_15_
  80.7 0.0 copy-done.1
  80.7 0.0 copy-done.2
  80.7 0.0 copy-done.3
  80.7 0.0 copy-done.4
  80.7 0.0 copy-done.5
  80.7 0.0 copy-done.6
  80.7 0.0 copy-done.7
  80.7 0.0 copy-done.8
  80.7 0.0 copy-done.9
  80.7 24.2 %pairs.1 = bf16[64,32,1024]{2,1,0:T(8,128)(2,1)} custom-call(s32[18]{0:T(128)} %stack.75.pos_ref, bf16[8,1024,128]{2,1,0:T(8,128)(2,1)} %bitcast.25, bf16[1024,128]{1,0:T(8,128)(2,1)} %spectra.1.refs_0_, bf16[1024,128]{1,0:T(8,128)(2,1)} %copy-done.4, bf16[1024,128]{1,0:T(8,128)(2,1)} %copy-done.3, bf16[1024,128]{1,0:T(8,128)(2,1)} %copy-done.2, ...), custom_call_target="tpu_custom_call" | custom-call | flops 17179869184 | bytes 16777216 | tf_op jit(solution)/shard_map/pairs/pallas_call | solution.py:381
  (3 shorter events, 0.0 us)
Async XLA Ops:
  6.5 2.5 %copy-start = (bf16[16,33280]{1,0:T(8,128)(2,1)S(1)}, bf16[16,33280]{1,0:T(8,128)(2,1)}, u32[]{:S(2)}) copy-start(bf16[16,33280]{1,0:T(8,128)(2,1)} %param.11) | copy-start | bytes 3194884
  6.5 74.1 %all-gather.3.cloned.1.call-start = ((), (), s32[]{:S(2)}) async-start(), calls=%async_computation.1 | async-start | bytes 2359296 | tf_op jit(solution)/shard_map/all_gather | solution.py:459
  46.0 5.9 %collective-permute-start.7 = (bf16[1024,128]{1,0:T(8,128)(2,1)}, bf16[1024,128]{1,0:T(8,128)(2,1)S(1)}, u32[]{:S(2)}, u32[]{:S(2)}) collective-permute-start(bf16[1024,128]{1,0:T(8,128)(2,1)} %spectra.1.refs_0_), channel_id=1, source_target_pairs={{0,2},{1,3},{2,0},{3,1},{4,6},{5,7},{6,4},{7,5},{8,10},{9,11},{10,... | collective-permute-start | bytes 786440 | tf_op jit(solution)/shard_map/ppermute | solution.py:429
  46.6 12.6 %collective-permute-start.2 = (bf16[1024,128]{1,0:T(8,128)(2,1)}, bf16[1024,128]{1,0:T(8,128)(2,1)S(1)}, u32[]{:S(2)}, u32[]{:S(2)}) collective-permute-start(bf16[1024,128]{1,0:T(8,128)(2,1)} %spectra.1.refs_0_), channel_id=1, source_target_pairs={{0,48},{16,0},{32,16},{48,32},{64,112},{80,64},{96,80},{112,96},{1... | collective-permute-start | bytes 786440 | tf_op jit(solution)/shard_map/ppermute | solution.py:408
  47.4 13.2 %collective-permute-start.1 = (bf16[1024,128]{1,0:T(8,128)(2,1)}, bf16[1024,128]{1,0:T(8,128)(2,1)S(1)}, u32[]{:S(2)}, u32[]{:S(2)}) collective-permute-start(bf16[1024,128]{1,0:T(8,128)(2,1)} %spectra.1.refs_0_), channel_id=1, source_target_pairs={{0,16},{16,32},{32,48},{48,0},{64,80},{80,96},{96,112},{112,64},{1... | collective-permute-start | bytes 786440 | tf_op jit(solution)/shard_map/ppermute | solution.py:408
  48.0 12.9 %collective-permute-start = (bf16[1024,128]{1,0:T(8,128)(2,1)}, bf16[1024,128]{1,0:T(8,128)(2,1)S(1)}, u32[]{:S(2)}, u32[]{:S(2)}) collective-permute-start(bf16[1024,128]{1,0:T(8,128)(2,1)} %spectra.1.refs_0_), channel_id=1, source_target_pairs={{0,64},{16,80},{32,96},{48,112},{64,0},{80,16},{96,32},{112,48},{1... | collective-permute-start | bytes 786440 | tf_op jit(solution)/shard_map/ppermute | solution.py:408
  51.9 28.8 %copy-start.1 = (bf16[1024,128]{1,0:T(8,128)(2,1)}, bf16[1024,128]{1,0:T(8,128)(2,1)S(1)}, u32[]{:S(2)}) copy-start(bf16[1024,128]{1,0:T(8,128)(2,1)S(1)} %collective-permute-done.7.refs_8_) | copy-start | bytes 786436
  51.9 11.4 %collective-permute-start.8 = (bf16[1024,128]{1,0:T(8,128)(2,1)S(1)}, bf16[1024,128]{1,0:T(8,128)(2,1)S(1)}, u32[]{:S(2)}, u32[]{:S(2)}) collective-permute-start(bf16[1024,128]{1,0:T(8,128)(2,1)S(1)} %collective-permute-done.7.refs_8_), channel_id=1, source_target_pairs={{0,4},{1,5},{2,6},{3,7},{4,8},{5,9},{6,10},{7,11},{8,12},{9,13},{1... | collective-permute-start | bytes 786440 | tf_op jit(solution)/shard_map/ppermute | solution.py:429
  53.1 10.2 %collective-permute-start.11 = (bf16[1024,128]{1,0:T(8,128)(2,1)S(1)}, bf16[1024,128]{1,0:T(8,128)(2,1)S(1)}, u32[]{:S(2)}, u32[]{:S(2)}) collective-permute-start(bf16[1024,128]{1,0:T(8,128)(2,1)S(1)} %collective-permute-done.7.refs_8_), channel_id=1, source_target_pairs={{0,1},{1,0},{2,3},{3,2},{4,5},{5,4},{6,7},{7,6},{8,9},{9,8},{10,11... | collective-permute-start | bytes 786440 | tf_op jit(solution)/shard_map/ppermute | solution.py:429
  59.2 21.5 %copy-start.2 = (bf16[1024,128]{1,0:T(8,128)(2,1)}, bf16[1024,128]{1,0:T(8,128)(2,1)S(1)}, u32[]{:S(2)}) copy-start(bf16[1024,128]{1,0:T(8,128)(2,1)S(1)} %collective-permute-done.2.refs_3_) | copy-start | bytes 786436
  59.2 12.9 %collective-permute-start.9 = (bf16[1024,128]{1,0:T(8,128)(2,1)S(1)}, bf16[1024,128]{1,0:T(8,128)(2,1)S(1)}, u32[]{:S(2)}, u32[]{:S(2)}) collective-permute-start(bf16[1024,128]{1,0:T(8,128)(2,1)S(1)} %collective-permute-done.7.refs_8_), channel_id=1, source_target_pairs={{0,12},{1,13},{2,14},{3,15},{4,0},{5,1},{6,2},{7,3},{8,4},{9,5},{1... | collective-permute-start | bytes 786440 | tf_op jit(solution)/shard_map/ppermute | solution.py:429
  60.7 20.0 %copy-start.3 = (bf16[1024,128]{1,0:T(8,128)(2,1)}, bf16[1024,128]{1,0:T(8,128)(2,1)S(1)}, u32[]{:S(2)}) copy-start(bf16[1024,128]{1,0:T(8,128)(2,1)S(1)} %collective-permute-done.1.refs_2_) | copy-start | bytes 786436
  60.7 12.1 %collective-permute-start.5 = (bf16[1024,128]{1,0:T(8,128)(2,1)S(1)}, bf16[1024,128]{1,0:T(8,128)(2,1)S(1)}, u32[]{:S(2)}, u32[]{:S(2)}) collective-permute-start(bf16[1024,128]{1,0:T(8,128)(2,1)S(1)} %collective-permute-done.1.refs_2_), channel_id=1, source_target_pairs={{0,16},{16,32},{32,48},{48,0},{64,80},{80,96},{96,112},{112,64},{1... | collective-permute-start | bytes 786440 | tf_op jit(solution)/shard_map/ppermute | solution.py:408
  61.0 19.7 %copy-start.4 = (bf16[1024,128]{1,0:T(8,128)(2,1)}, bf16[1024,128]{1,0:T(8,128)(2,1)S(1)}, u32[]{:S(2)}) copy-start(bf16[1024,128]{1,0:T(8,128)(2,1)S(1)} %collective-permute-done.refs_1_) | copy-start | bytes 786436
  61.0 11.9 %collective-permute-start.4 = (bf16[1024,128]{1,0:T(8,128)(2,1)S(1)}, bf16[1024,128]{1,0:T(8,128)(2,1)S(1)}, u32[]{:S(2)}, u32[]{:S(2)}) collective-permute-start(bf16[1024,128]{1,0:T(8,128)(2,1)S(1)} %collective-permute-done.refs_1_), channel_id=1, source_target_pairs={{0,48},{16,0},{32,16},{48,32},{64,112},{80,64},{96,80},{112,96},{1... | collective-permute-start | bytes 786440 | tf_op jit(solution)/shard_map/ppermute | solution.py:408
  63.3 17.3 %copy-start.5 = (bf16[1024,128]{1,0:T(8,128)(2,1)}, bf16[1024,128]{1,0:T(8,128)(2,1)S(1)}, u32[]{:S(2)}) copy-start(bf16[1024,128]{1,0:T(8,128)(2,1)S(1)} %collective-permute-done.8.refs_9_) | copy-start | bytes 786436
  63.3 11.5 %collective-permute-start.10 = (bf16[1024,128]{1,0:T(8,128)(2,1)S(1)}, bf16[1024,128]{1,0:T(8,128)(2,1)}, u32[]{:S(2)}, u32[]{:S(2)}) collective-permute-start(bf16[1024,128]{1,0:T(8,128)(2,1)S(1)} %collective-permute-done.8.refs_9_), channel_id=1, source_target_pairs={{0,4},{1,5},{2,6},{3,7},{4,8},{5,9},{6,10},{7,11},{8,12},{9,13},{1... | collective-permute-start | bytes 786440 | tf_op jit(solution)/shard_map/ppermute | solution.py:429
  63.4 17.3 %copy-start.6 = (bf16[1024,128]{1,0:T(8,128)(2,1)}, bf16[1024,128]{1,0:T(8,128)(2,1)S(1)}, u32[]{:S(2)}) copy-start(bf16[1024,128]{1,0:T(8,128)(2,1)S(1)} %collective-permute-done.11.refs_12_) | copy-start | bytes 786436
  63.4 16.4 %collective-permute-start.3 = (bf16[1024,128]{1,0:T(8,128)(2,1)S(1)}, bf16[1024,128]{1,0:T(8,128)(2,1)}, u32[]{:S(2)}, u32[]{:S(2)}) collective-permute-start(bf16[1024,128]{1,0:T(8,128)(2,1)S(1)} %collective-permute-done.refs_1_), channel_id=1, source_target_pairs={{0,16},{16,32},{32,48},{48,0},{64,80},{80,96},{96,112},{112,64},{1... | collective-permute-start | bytes 786440 | tf_op jit(solution)/shard_map/ppermute | solution.py:408
  72.1 8.6 %copy-start.7 = (bf16[1024,128]{1,0:T(8,128)(2,1)}, bf16[1024,128]{1,0:T(8,128)(2,1)S(1)}, u32[]{:S(2)}) copy-start(bf16[1024,128]{1,0:T(8,128)(2,1)S(1)} %collective-permute-done.9.refs_10_) | copy-start | bytes 786436
  72.1 7.7 %collective-permute-start.12 = (bf16[1024,128]{1,0:T(8,128)(2,1)S(1)}, bf16[1024,128]{1,0:T(8,128)(2,1)}, u32[]{:S(2)}, u32[]{:S(2)}) collective-permute-start(bf16[1024,128]{1,0:T(8,128)(2,1)S(1)} %collective-permute-done.8.refs_9_), channel_id=1, source_target_pairs={{0,1},{1,0},{2,3},{3,2},{4,5},{5,4},{6,7},{7,6},{8,9},{9,8},{10,11... | collective-permute-start | bytes 786440 | tf_op jit(solution)/shard_map/ppermute | solution.py:429
  72.7 8.0 %copy-start.8 = (bf16[1024,128]{1,0:T(8,128)(2,1)}, bf16[1024,128]{1,0:T(8,128)(2,1)S(1)}, u32[]{:S(2)}) copy-start(bf16[1024,128]{1,0:T(8,128)(2,1)S(1)} %collective-permute-done.5.refs_6_) | copy-start | bytes 786436
  72.7 7.1 %collective-permute-start.13 = (bf16[1024,128]{1,0:T(8,128)(2,1)S(1)}, bf16[1024,128]{1,0:T(8,128)(2,1)}, u32[]{:S(2)}, u32[]{:S(2)}) collective-permute-start(bf16[1024,128]{1,0:T(8,128)(2,1)S(1)} %collective-permute-done.9.refs_10_), channel_id=1, source_target_pairs={{0,1},{1,0},{2,3},{3,2},{4,5},{5,4},{6,7},{7,6},{8,9},{9,8},{10,11... | collective-permute-start | bytes 786440 | tf_op jit(solution)/shard_map/ppermute | solution.py:429
  72.8 7.9 %copy-start.9 = (bf16[1024,128]{1,0:T(8,128)(2,1)}, bf16[1024,128]{1,0:T(8,128)(2,1)S(1)}, u32[]{:S(2)}) copy-start(bf16[1024,128]{1,0:T(8,128)(2,1)S(1)} %collective-permute-done.4.refs_5_) | copy-start | bytes 786436
  72.8 7.6 %collective-permute-start.6 = (bf16[1024,128]{1,0:T(8,128)(2,1)S(1)}, bf16[1024,128]{1,0:T(8,128)(2,1)}, u32[]{:S(2)}, u32[]{:S(2)}) collective-permute-start(bf16[1024,128]{1,0:T(8,128)(2,1)S(1)} %collective-permute-done.4.refs_5_), channel_id=1, source_target_pairs={{0,48},{16,0},{32,16},{48,32},{64,112},{80,64},{96,80},{112,96},{1... | collective-permute-start | bytes 786440 | tf_op jit(solution)/shard_map/ppermute | solution.py:408
  74.9 5.8 %collective-permute-start.14 = (bf16[1024,128]{1,0:T(8,128)(2,1)}, bf16[1024,128]{1,0:T(8,128)(2,1)}, u32[]{:S(2)}, u32[]{:S(2)}) collective-permute-start(bf16[1024,128]{1,0:T(8,128)(2,1)} %collective-permute-done.10.refs_11_), channel_id=1, source_target_pairs={{0,1},{1,0},{2,3},{3,2},{4,5},{5,4},{6,7},{7,6},{8,9},{9,8},{10,11... | collective-permute-start | bytes 786440 | tf_op jit(solution)/shard_map/ppermute | solution.py:429
Sparse Core Ops, SparseCore 0:
  46.1 27.4 all-gather.2

commit v7 on v6

--- a/solution.py
+++ b/solution.py
@@ -229,26 +229,17 @@
 
 def pair_kernel(pos_ref, a_hbm, *refs):
     nrow, ncol = 8, 16
-    b_hbm, c_hbm, refs = refs[:nrow], refs[nrow : 2 * nrow], refs[nrow:]
+    b_hbm = refs[:nrow]
     lag_hbm, turn_ref, out_hbm, a_ref, b_ref, lag_ref, x_ref, y_ref, f_ref, o_ref, in_sem, lag_sem, out_sem = refs[nrow:]
     size = 1024 // CHUNKS
-    side = pos_ref[1] // 2 % 2
 
     def arrive(k):
         rows = pl.ds(k * size, size)
-        copies = []
-        for x in range(4):
-            copies.append(
-                pltpu.make_async_copy(
-                    a_hbm.at[pl.ds(x * 2, 2), rows, :], a_ref.at[pl.ds(x * 4 + side * 2, 2), rows, :],
-                    in_sem.at[k, 16 + x]))
-        for r in range(8):
+        copies = [pltpu.make_async_copy(a_hbm.at[:, rows, :], a_ref.at[:, rows, :], in_sem.at[k, nrow])]
+        for r in range(nrow):
             copies.append(
                 pltpu.make_async_copy(
                     b_hbm[r].at[rows, :], b_ref.at[pos_ref[2 + r], rows, :], in_sem.at[k, r]))
-            copies.append(
-                pltpu.make_async_copy(
-                    c_hbm[r].at[rows, :], a_ref.at[pos_ref[10 + r], rows, :], in_sem.at[k, 8 + r]))
         return copies
 
     for k in range(CHUNKS):
@@ -374,14 +365,14 @@
             leave(half, d).wait()
 
 
-def pairs_of(pos, a, b, c):
-    nrow, ncol = len(b), a.shape[0] + len(c)
+def pairs_of(pos, a, b):
+    nrow, ncol = len(b), a.shape[0]
     assert nrow == 8 and ncol == 16
     anywhere = pl.BlockSpec(memory_space=pl.ANY)
     return pl.pallas_call(
         pair_kernel,
         out_shape=jax.ShapeDtypeStruct((ncol * CH, nrow * CH, LAGS), BF),
-        in_specs=[pl.BlockSpec(memory_space=pltpu.SMEM)] + [anywhere] * (2 * nrow + 2)
+        in_specs=[pl.BlockSpec(memory_space=pltpu.SMEM)] + [anywhere] * (nrow + 2)
         + [pl.BlockSpec(memory_space=pltpu.VMEM)],
         out_specs=anywhere,
         scratch_shapes=[
@@ -392,14 +383,14 @@
             pltpu.VMEM((2, LAGS, 128), F32),
             pltpu.VMEM((LAGS // 128, 8 * 129 + 8, 128), F32),
             pltpu.VMEM((ncol * CH, nrow * CH, LAGS), BF),
-            pltpu.SemaphoreType.DMA((CHUNKS, 20)),
+            pltpu.SemaphoreType.DMA((CHUNKS, nrow + 1)),
             pltpu.SemaphoreType.DMA,
             pltpu.SemaphoreType.DMA((2, ncol)),
         ],
         compiler_params=pltpu.CompilerParams(vmem_limit_bytes=60 * 2**20),
         cost_estimate=pl.CostEstimate(flops=2**34, bytes_accessed=16 * 2**20, transcendentals=0),
         name="pairs",
-    )(pos, a, *b, *c, lag_tables(), turning_tables())
+    )(pos, a, *b, lag_tables(), turning_tables())
 
 
 def over_row(own, my_row):
@@ -419,22 +410,6 @@
         index(-1, 1), index(1, 1), index(2, 0), index(2, 1),
     ]
     return blocks, rows
-
-
-def over_col(own, my_col):
-    def move(block, step=0, across=0, core=0):
-        pairs = [
-            (x * 4 + y * 2 + c, (x + step) % 4 * 4 + (y ^ across) * 2 + (c ^ core))
-            for x in range(4) for y in range(2) for c in range(2)]
-        return lax.ppermute(block, "col", pairs)
-
-    x, y, core = my_col // 4, my_col // 2 % 2, my_col % 2
-    near = move(own, across=1)
-    left, right = move(near, 1), move(near, -1)
-    blocks = [near, left, right, move(left, 1)]
-    cols = [(x + step) % 4 * 4 + (y ^ 1) * 2 for step in (0, -1, 1, 2)]
-    blocks += [move(v, core=1) for v in blocks]
-    return blocks, [c + core for c in cols] + [c + (core ^ 1) for c in cols]
 
 
 def local(strain, file_channels, file_counts, window_start):
@@ -455,12 +430,10 @@
     sent = jnp.concatenate([bundle, tags], axis=1).reshape(nrow, 2, WIN + 128)
     got = lax.all_to_all(sent, "row", 0, 0).reshape(2 * nrow, WIN + 128)
     own = spectra_of(got)
-    rings = [[x * 4 + y * 2 + core for x in range(4) for core in range(2)] for y in range(2)]
-    a = lax.all_gather(own, "col", axis=0, axis_index_groups=rings)
-    c, cols = over_col(own, my_col)
+    a = lax.all_gather(own, "col", axis=0)
     b, rows = over_row(own, my_row)
-    pos = jnp.stack([my_row, my_col, *rows, *cols]).astype(jnp.int32)
-    return pairs_of(pos, a, b, c)
+    pos = jnp.stack([my_row, my_col, *rows]).astype(jnp.int32)
+    return pairs_of(pos, a, b)
 
 
 def solution(mesh):

time: 112 us -> 113 us (level)
  waiting for transfers between devices: 12.3 us -> 30.2 us
  starting transfers between devices: 21.7 us -> 5.7 us
    ppermute x7, waiting for transfers between devices: 0.61 us -> 17.2 us  [move(): return lax.ppermute(block, 'row', pairs)]
    ppermute x8 -> x0, starting transfers between devices: 14.4 us -> none  [move(): return lax.ppermute(block, 'col', pairs)]
    all_gather x1, waiting for transfers between devices: 0.01 us -> 13 us  [local(): a = lax.all_gather(own, 'col', axis=0)]
    ppermute x8 -> x0, waiting for transfers between devices: 11.7 us -> none  [move(): return lax.ppermute(block, 'col', pairs)]
    ppermute x7, starting transfers between devices: 7.33 us -> 5.7 us  [move(): return lax.ppermute(block, 'row', pairs)]
  transfers between devices with their start and end apart: 16 -> 8, of which waited for: 4 -> 6; matrix products, arithmetic and copies ran while one was open for 1% -> 1% of each run, Pallas kernels for 0% -> 0%
where the time goes in v7:
time: 113 us
  Pallas kernels  33.7 us (30%)
  waiting for transfers between devices  30.2 us (27%)
  blocking collectives  24.6 us (22%)
  between operations  14.9 us (13%)
  starting transfers between devices  5.7 us (5%)
  local copies, waits for them, and re-layouts  2.36 us (2%)
    all_to_all x1, blocking collectives, local(): got = lax.all_to_all(sent, 'row', 0, 0).reshape(2 * nrow, WIN + 128)  24.6 us
    pallas_call x1, Pallas kernels, pairs_of(): pl.pallas_call(pair_kernel, out_shape=jax.ShapeDtypeStruct((ncol * CH, nr...  23.6 us
    ppermute x7, waiting for transfers between devices, move(): return lax.ppermute(block, 'row', pairs)  17.2 us
    all_gather x1, waiting for transfers between devices, local(): a = lax.all_gather(own, 'col', axis=0)  13 us
    pallas_call x1, Pallas kernels, spectra_of(): pl.pallas_call(spectra_kernel, out_shape=jax.ShapeDtypeStruct((1024, 128)...  10.1 us
    ppermute x7, starting transfers between devices, move(): return lax.ppermute(block, 'row', pairs)  5.7 us
  transfers between devices with their start and end apart: 8, of which 6 were waited for; matrix products, arithmetic and copies ran while one was open for 1% of the time, Pallas kernels for 0%

profile of v7, /device:TPU:1, one launch (start us, length us, event | category | flops | bytes accessed | tf_op | source)
XLA Modules:
  0.0 113.0 jit_solution(15241544115678516949)
XLA Ops:
  6.5 0.0 copy-start
  6.5 0.0 all-gather.3.cloned.1.call-start
  7.9 0.7 compare_select_fusion
  8.6 0.2 convert_reduce_fusion
  8.8 0.2 select_reduce_fusion
  9.0 0.0 copy-done
  9.0 0.5 convolution_convert_fusion
  9.5 0.1 broadcast_in_dim.14
  9.6 0.1 pad_maximum_fusion
  9.7 0.4 reshape.67
  10.1 24.6 %all_to_all.5 = bf16[8,2,32896]{2,1,0:T(2,128)(2,1)S(1)} all-to-all(bf16[8,2,32896]{2,1,0:T(2,128)(2,1)S(1)} %reshape.67), channel_id=1, replica_groups=mesh['row'=8,'col'=16] {'row'}, dimensions={0} | all-to-all | bytes 2105344 | tf_op jit(solution)/shard_map/all_to_all | solution.py:431
  34.7 1.2 %reshape.68.got_ref = bf16[16,32896]{1,0:T(8,128)(2,1)} reshape(bf16[8,2,32896]{2,1,0:T(2,128)(2,1)S(1)} %all_to_all.5) | data formatting | bytes 2105344 | tf_op jit(solution)/shard_map/reshape | solution.py:431
  35.9 10.1 %spectra.1.refs_0_ = bf16[1024,128]{1,0:T(8,128)(2,1)} custom-call(bf16[16,32896]{1,0:T(8,128)(2,1)} %reshape.68.got_ref, bf16[512,512]{1,0:T(8,128)(2,1)} %constant.133.clone.part_hbm, bf16[7,768,128]{2,1,0:T(8,128)(2,1)} %constant.134.clone.smooth_hbm, f32[2,1024]{1,0:T(2,128)} %constant.135.clone.taper_hbm, bf16[128,1024]{1,0:T(8,128)(2,1)} %constant.136.clone.spread_hbm, ...), custom_call_target="tpu_custom_call" | custom-call | flops 1073741824 | bytes 8388608 | tf_op jit(solution)/shard_map/spectra/pallas_call | solution.py:202
  46.0 0.0 all-gather.3.cloned.1.call-update
  46.0 0.6 collective-permute-start
  46.6 0.4 collective-permute-start.1
  47.1 6.3 %collective-permute-done.refs_1_ = bf16[1024,128]{1,0:T(8,128)(2,1)S(1)} collective-permute-done((bf16[1024,128]{1,0:T(8,128)(2,1)}, bf16[1024,128]{1,0:T(8,128)(2,1)S(1)}, u32[]{:S(2)}, u32[]{:S(2)}) %collective-permute-start) | collective-permute-done | bytes 262176 | tf_op jit(solution)/shard_map/ppermute | solution.py:399
  53.4 0.0 copy-start.1
  53.4 0.9 collective-permute-start.4
  54.3 0.9 collective-permute-start.2
  55.2 0.6 collective-permute-start.3
  55.8 0.0 collective-permute-done.1.refs_2_
  55.8 0.0 copy-start.2
  55.8 0.6 collective-permute-start.5
  56.4 2.7 %collective-permute-done.4.refs_5_ = bf16[1024,128]{1,0:T(8,128)(2,1)S(1)} collective-permute-done((bf16[1024,128]{1,0:T(8,128)(2,1)S(1)}, bf16[1024,128]{1,0:T(8,128)(2,1)S(1)}, u32[]{:S(2)}, u32[]{:S(2)}) %collective-permute-start.4) | collective-permute-done | bytes 262176 | tf_op jit(solution)/shard_map/ppermute | solution.py:399
  59.0 0.0 copy-start.3
  59.0 1.7 %collective-permute-start.6 = (bf16[1024,128]{1,0:T(8,128)(2,1)S(1)}, bf16[1024,128]{1,0:T(8,128)(2,1)S(1)}, u32[]{:S(2)}, u32[]{:S(2)}) collective-permute-start(bf16[1024,128]{1,0:T(8,128)(2,1)S(1)} %collective-permute-done.4.refs_5_), channel_id=1, source_target_pairs={{0,48},{16,0},{32,16},{48,32},{64,112},{80,64},{96,80},{112,96},{1... | collective-permute-start | bytes 786440 | tf_op jit(solution)/shard_map/ppermute | solution.py:399
  60.7 0.6 stack.43.pos_ref
  61.3 2.4 %collective-permute-done.2.refs_3_ = bf16[1024,128]{1,0:T(8,128)(2,1)S(1)} collective-permute-done((bf16[1024,128]{1,0:T(8,128)(2,1)}, bf16[1024,128]{1,0:T(8,128)(2,1)S(1)}, u32[]{:S(2)}, u32[]{:S(2)}) %collective-permute-start.2) | collective-permute-done | bytes 262176 | tf_op jit(solution)/shard_map/ppermute | solution.py:399
  63.7 0.0 copy-start.4
  63.7 2.7 %collective-permute-done.5.refs_6_ = bf16[1024,128]{1,0:T(8,128)(2,1)S(1)} collective-permute-done((bf16[1024,128]{1,0:T(8,128)(2,1)S(1)}, bf16[1024,128]{1,0:T(8,128)(2,1)S(1)}, u32[]{:S(2)}, u32[]{:S(2)}) %collective-permute-start.5) | collective-permute-done | bytes 262176 | tf_op jit(solution)/shard_map/ppermute | solution.py:399
  66.4 0.0 copy-start.6
  66.4 0.0 collective-permute-done.3.refs_4_
  66.4 0.0 copy-start.5
  66.4 3.0 %collective-permute-done.6.refs_7_ = bf16[1024,128]{1,0:T(8,128)(2,1)S(1)} collective-permute-done((bf16[1024,128]{1,0:T(8,128)(2,1)S(1)}, bf16[1024,128]{1,0:T(8,128)(2,1)S(1)}, u32[]{:S(2)}, u32[]{:S(2)}) %collective-permute-start.6) | collective-permute-done | bytes 262176 | tf_op jit(solution)/shard_map/ppermute | solution.py:399
  69.5 0.0 copy-start.7
  69.5 13.0 %all-gather.3.cloned.1.call-done = bf16[16384,128]{1,0:T(8,128)(2,1)} async-done(((bf16[1024,128]{1,0:T(8,128)(2,1)}), bf16[16384,128]{1,0:T(8,128)(2,1)}) %all-gather.3.cloned.1.call-update) | async-done | bytes 4194320 | tf_op jit(solution)/shard_map/all_gather | solution.py:433
  82.5 0.0 copy-done.1
  82.5 0.0 copy-done.2
  82.5 0.0 copy-done.3
  82.5 0.0 copy-done.4
  82.5 0.0 copy-done.6
  82.5 0.0 copy-done.5
  82.5 0.0 copy-done.7
  82.5 23.6 %pairs.1 = bf16[64,32,1024]{2,1,0:T(8,128)(2,1)} custom-call(s32[10]{0:T(128)} %stack.43.pos_ref, bf16[16,1024,128]{2,1,0:T(8,128)(2,1)} %bitcast.17, bf16[1024,128]{1,0:T(8,128)(2,1)} %spectra.1.refs_0_, bf16[1024,128]{1,0:T(8,128)(2,1)} %copy-done.1, bf16[1024,128]{1,0:T(8,128)(2,1)} %copy-done.2, bf16[1024,128]{1,0:T(8,128)(2,1)} %copy-done.4, ...), custom_call_target="tpu_custom_call" | custom-call | flops 17179869184 | bytes 16777216 | tf_op jit(solution)/shard_map/pairs/pallas_call | solution.py:372
  (2 shorter events, 0.0 us)
Async XLA Ops:
  6.5 2.5 %copy-start = (bf16[16,33280]{1,0:T(8,128)(2,1)S(1)}, bf16[16,33280]{1,0:T(8,128)(2,1)}, u32[]{:S(2)}) copy-start(bf16[16,33280]{1,0:T(8,128)(2,1)} %param.11) | copy-start | bytes 3194884
  6.5 75.9 %all-gather.3.cloned.1.call-start = ((), (), s32[]{:S(2)}) async-start(), calls=%async_computation.1 | async-start | bytes 4456448 | tf_op jit(solution)/shard_map/all_gather | solution.py:433
  46.0 7.4 %collective-permute-start = (bf16[1024,128]{1,0:T(8,128)(2,1)}, bf16[1024,128]{1,0:T(8,128)(2,1)S(1)}, u32[]{:S(2)}, u32[]{:S(2)}) collective-permute-start(bf16[1024,128]{1,0:T(8,128)(2,1)} %spectra.1.refs_0_), channel_id=1, source_target_pairs={{0,64},{16,80},{32,96},{48,112},{64,0},{80,16},{96,32},{112,48},{1... | collective-permute-start | bytes 786440 | tf_op jit(solution)/shard_map/ppermute | solution.py:399
  46.6 9.1 %collective-permute-start.1 = (bf16[1024,128]{1,0:T(8,128)(2,1)}, bf16[1024,128]{1,0:T(8,128)(2,1)S(1)}, u32[]{:S(2)}, u32[]{:S(2)}) collective-permute-start(bf16[1024,128]{1,0:T(8,128)(2,1)} %spectra.1.refs_0_), channel_id=1, source_target_pairs={{0,16},{16,32},{32,48},{48,0},{64,80},{80,96},{96,112},{112,64},{1... | collective-permute-start | bytes 786440 | tf_op jit(solution)/shard_map/ppermute | solution.py:399
  53.4 29.0 %copy-start.1 = (bf16[1024,128]{1,0:T(8,128)(2,1)}, bf16[1024,128]{1,0:T(8,128)(2,1)S(1)}, u32[]{:S(2)}) copy-start(bf16[1024,128]{1,0:T(8,128)(2,1)S(1)} %collective-permute-done.refs_1_) | copy-start | bytes 786436
  53.4 5.6 %collective-permute-start.4 = (bf16[1024,128]{1,0:T(8,128)(2,1)S(1)}, bf16[1024,128]{1,0:T(8,128)(2,1)S(1)}, u32[]{:S(2)}, u32[]{:S(2)}) collective-permute-start(bf16[1024,128]{1,0:T(8,128)(2,1)S(1)} %collective-permute-done.refs_1_), channel_id=1, source_target_pairs={{0,48},{16,0},{32,16},{48,32},{64,112},{80,64},{96,80},{112,96},{1... | collective-permute-start | bytes 786440 | tf_op jit(solution)/shard_map/ppermute | solution.py:399
  54.3 9.4 %collective-permute-start.2 = (bf16[1024,128]{1,0:T(8,128)(2,1)}, bf16[1024,128]{1,0:T(8,128)(2,1)S(1)}, u32[]{:S(2)}, u32[]{:S(2)}) collective-permute-start(bf16[1024,128]{1,0:T(8,128)(2,1)} %spectra.1.refs_0_), channel_id=1, source_target_pairs={{0,48},{16,0},{32,16},{48,32},{64,112},{80,64},{96,80},{112,96},{1... | collective-permute-start | bytes 786440 | tf_op jit(solution)/shard_map/ppermute | solution.py:399
  55.2 11.3 %collective-permute-start.3 = (bf16[1024,128]{1,0:T(8,128)(2,1)S(1)}, bf16[1024,128]{1,0:T(8,128)(2,1)S(1)}, u32[]{:S(2)}, u32[]{:S(2)}) collective-permute-start(bf16[1024,128]{1,0:T(8,128)(2,1)S(1)} %collective-permute-done.refs_1_), channel_id=1, source_target_pairs={{0,16},{16,32},{32,48},{48,0},{64,80},{80,96},{96,112},{112,64},{1... | collective-permute-start | bytes 786440 | tf_op jit(solution)/shard_map/ppermute | solution.py:399
  55.8 26.7 %copy-start.2 = (bf16[1024,128]{1,0:T(8,128)(2,1)}, bf16[1024,128]{1,0:T(8,128)(2,1)S(1)}, u32[]{:S(2)}) copy-start(bf16[1024,128]{1,0:T(8,128)(2,1)S(1)} %collective-permute-done.1.refs_2_) | copy-start | bytes 786436
  55.8 10.7 %collective-permute-start.5 = (bf16[1024,128]{1,0:T(8,128)(2,1)S(1)}, bf16[1024,128]{1,0:T(8,128)(2,1)S(1)}, u32[]{:S(2)}, u32[]{:S(2)}) collective-permute-start(bf16[1024,128]{1,0:T(8,128)(2,1)S(1)} %collective-permute-done.1.refs_2_), channel_id=1, source_target_pairs={{0,16},{16,32},{32,48},{48,0},{64,80},{80,96},{96,112},{112,64},{1... | collective-permute-start | bytes 786440 | tf_op jit(solution)/shard_map/ppermute | solution.py:399
  59.0 23.4 %copy-start.3 = (bf16[1024,128]{1,0:T(8,128)(2,1)}, bf16[1024,128]{1,0:T(8,128)(2,1)S(1)}, u32[]{:S(2)}) copy-start(bf16[1024,128]{1,0:T(8,128)(2,1)S(1)} %collective-permute-done.4.refs_5_) | copy-start | bytes 786436
  59.0 10.4 %collective-permute-start.6 = (bf16[1024,128]{1,0:T(8,128)(2,1)S(1)}, bf16[1024,128]{1,0:T(8,128)(2,1)S(1)}, u32[]{:S(2)}, u32[]{:S(2)}) collective-permute-start(bf16[1024,128]{1,0:T(8,128)(2,1)S(1)} %collective-permute-done.4.refs_5_), channel_id=1, source_target_pairs={{0,48},{16,0},{32,16},{48,32},{64,112},{80,64},{96,80},{112,96},{1... | collective-permute-start | bytes 786440 | tf_op jit(solution)/shard_map/ppermute | solution.py:399
  63.7 18.7 %copy-start.4 = (bf16[1024,128]{1,0:T(8,128)(2,1)}, bf16[1024,128]{1,0:T(8,128)(2,1)S(1)}, u32[]{:S(2)}) copy-start(bf16[1024,128]{1,0:T(8,128)(2,1)S(1)} %collective-permute-done.2.refs_3_) | copy-start | bytes 786436
  66.4 16.1 %copy-start.6 = (bf16[1024,128]{1,0:T(8,128)(2,1)}, bf16[1024,128]{1,0:T(8,128)(2,1)S(1)}, u32[]{:S(2)}) copy-start(bf16[1024,128]{1,0:T(8,128)(2,1)S(1)} %collective-permute-done.5.refs_6_) | copy-start | bytes 786436
  66.4 16.1 %copy-start.5 = (bf16[1024,128]{1,0:T(8,128)(2,1)}, bf16[1024,128]{1,0:T(8,128)(2,1)S(1)}, u32[]{:S(2)}) copy-start(bf16[1024,128]{1,0:T(8,128)(2,1)S(1)} %collective-permute-done.3.refs_4_) | copy-start | bytes 786436
  69.5 13.0 %copy-start.7 = (bf16[1024,128]{1,0:T(8,128)(2,1)}, bf16[1024,128]{1,0:T(8,128)(2,1)S(1)}, u32[]{:S(2)}) copy-start(bf16[1024,128]{1,0:T(8,128)(2,1)S(1)} %collective-permute-done.6.refs_7_) | copy-start | bytes 786436
Sparse Core Ops, SparseCore 0:
  46.1 36.2 all-gather.2
